TPU v7x, 128 devices: a whole 4x4x4 slice. The times are simulated.
128 devices in a mesh: py: 8 (over z, core), px: 16 (over x, y).
Axes of the slice: x: 4, y: 4, z: 4, core: 2. Of those that a mesh axis runs over, the one named last changes fastest.
Arguments:
- features: bfloat16 [512, 2048, 256], P('py', 'px'), may hold values from -6 to 6
- coarse: bfloat16 [1024, 100, 128], P(('py', 'px')), may hold values from -6 to 6
- send_ids: int32 [128, 128, 2], P(('py', 'px')), may hold values from 0 to 7, as said below
- send_counts: int32 [128, 128], P(('py', 'px')), may hold values from 0 to 2, as said below
- entry_slot: int32 [128, 256], P(('py', 'px')), may hold values from 0 to 255, as said below
- entry_weight_pattern: int32 [128, 256], P(('py', 'px')), may hold values from 0 to 7
- interpolation_weights: bfloat16 [8, 128, 128], replicated, may hold values from -0.25 to 0.25
- lift_weight: bfloat16 [100, 256], replicated, may hold values from -0.625 to 0.625
- conv_a: bfloat16 [3, 3, 256, 256], replicated, may hold values from -0.125 to 0.125
- conv_b: bfloat16 [3, 3, 256, 512], replicated, may hold values from -0.125 to 0.125
- up_weight: bfloat16 [512, 256], replicated, may hold values from -0.25 to 0.25
Outputs:
- output: bfloat16 [512, 2048, 256], P('py', 'px')
Inputs may be any that keep to these rules, and one draw needn't show every extreme that they name: send_ids[s, p, k] is the local index, on owner s, of the k-th block that s sends to patch p; the first send_counts[s, p] of them are distinct. send_counts[s, p] blocks go from owner s to patch p; send_counts[p, p] = 2. entry_slot[p, e] = s * 2 + k names the k-th block sent by owner s to patch p, with k < send_counts[s, p]; every block sent to patch p is named by some entry of p.
All inputs are finite; a program needn't handle non-finite values.
Results may differ from a plain program's by a relative error of at most 0.013.
Values may be sent and summed in bfloat16 or wider, within the bound.
No kernel may reach another device: no remote copies, remote signals or barrier semaphores. Data moves between devices by JAX's collectives and lax.ppermute only.
A program may use at most 256 MiB of HBM per device.

v0:
```python
import jax
import jax.numpy as jnp
from jax import lax
from jax.experimental import pallas as pl
from jax.experimental.pallas import tpu as pltpu
from jax.sharding import PartitionSpec as P

F32 = jnp.float32
BF16 = jnp.bfloat16
MIB = 1024 * 1024

SUBTILE_ENTRIES = 4
SUBTILE_ROWS = 8
SUBTILE_COLUMNS = 16
PY = 8
PX = 16
DEVICES = PY * PX
OWNED = 8
CELLS = 128
CHANNELS = 100
PART = 7
SLOT = 8
PATTERNS = 8
SUBTILES = 64
ENTRIES = SUBTILES * SUBTILE_ENTRIES
ROWS = 64
COLUMNS = 128
FINE = 256
WIDE = 512
TILES = DEVICES * OWNED
ZERO_TILE = PATTERNS * TILES


def silu(v):
    return 0.5 * v * (1.0 + jnp.tanh(0.5 * v))


def dot(a, b):
    return jnp.dot(a, b, preferred_element_type=F32)


def pack_kernel(coarse_ref, tables_ref, out_ref, parts_ref):
    @pl.when(pl.program_id(0) == 0)
    def _():
        row = lax.broadcasted_iota(jnp.int32, (PX * SLOT, CHANNELS), 0)
        channel = lax.broadcasted_iota(jnp.int32, (PX * SLOT, CHANNELS), 1)
        place = row % SLOT
        chosen = (channel == (row // SLOT) * PART + place) & (place < PART)
        pick = jnp.where(chosen, 1.0, 0.0).astype(BF16)
        for block in range(OWNED):
            parts_ref[:, block] = dot(pick, coarse_ref[block]).reshape(PX, SLOT, CELLS)

    place = lax.broadcasted_iota(jnp.int32, (PX, OWNED, SLOT, CELLS), 2)
    tables = jnp.broadcast_to(tables_ref[0][None, :, None, :], place.shape)
    merged = jnp.where(place == PART, tables, parts_ref[...])
    out_ref[0] = merged.reshape(PX, OWNED * SLOT, CELLS).astype(BF16)


def pack(coarse, tables):
    return pl.pallas_call(
        pack_kernel,
        grid=(PY,),
        in_specs=[
            pl.BlockSpec((OWNED, CHANNELS, CELLS), lambda i: (0, 0, 0)),
            pl.BlockSpec((1, OWNED, CELLS), lambda i: (i, 0, 0)),
        ],
        out_specs=pl.BlockSpec((1, PX, OWNED * SLOT, CELLS), lambda i: (i, 0, 0, 0)),
        out_shape=jax.ShapeDtypeStruct((PY, PX, OWNED * SLOT, CELLS), BF16),
        scratch_shapes=[pltpu.VMEM((PX, OWNED, SLOT, CELLS), F32)],
        compiler_params=pltpu.CompilerParams(vmem_limit_bytes=24 * MIB),
    )(coarse, tables)


def blend_kernel(index_ref, blocks_ref, weights_ref, out_ref, table_ref):
    chunk = 1024

    def multiply(step, carry):
        rows = pl.ds(pl.multiple_of(step * chunk, chunk), chunk)
        tiles = pl.ds(pl.multiple_of(step * (chunk // SLOT), chunk // SLOT), chunk // SLOT)
        part = blocks_ref[rows, :]
        for pair in range(PATTERNS // 2):
            both = jnp.concatenate([weights_ref[2 * pair], weights_ref[2 * pair + 1]], axis=1)
            product = dot(part, both)
            for half in range(2):
                table_ref[2 * pair + half, tiles] = product[:, half * CELLS : (half + 1) * CELLS].reshape(
                    chunk // SLOT, SLOT, CELLS
                )
        return carry

    lax.fori_loop(0, TILES * SLOT // chunk, multiply, 0)
    table_ref[PATTERNS, 0] = jnp.zeros((SLOT, CELLS), F32)

    def total(base):
        tile = [table_ref[index_ref[base + i] // TILES, index_ref[base + i] % TILES] for i in range(SUBTILE_ENTRIES)]
        return (tile[0] + tile[1]) + (tile[2] + tile[3])

    group = 8

    def gather(step, carry):
        base = step * (group * SUBTILE_ENTRIES)
        sums = [total(base + k * SUBTILE_ENTRIES) for k in range(group)]
        rows = pl.ds(pl.multiple_of(step * group * SLOT, group * SLOT), group * SLOT)
        out_ref[rows, :] = jnp.concatenate(sums, axis=0).astype(BF16)
        return carry

    lax.fori_loop(0, PX * SUBTILES // group, gather, 0)


def blend(index, blocks, weights):
    return pl.pallas_call(
        blend_kernel,
        in_specs=[
            pl.BlockSpec(memory_space=pltpu.SMEM),
            pl.BlockSpec(memory_space=pltpu.VMEM),
            pl.BlockSpec(memory_space=pltpu.VMEM),
        ],
        out_specs=pl.BlockSpec(memory_space=pltpu.VMEM),
        out_shape=jax.ShapeDtypeStruct((PX * SUBTILES * SLOT, CELLS), BF16),
        scratch_shapes=[pltpu.VMEM((PATTERNS + 1, TILES, SLOT, CELLS), F32)],
        compiler_params=pltpu.CompilerParams(vmem_limit_bytes=56 * MIB),
    )(index, blocks, weights)


def entry_index(received):
    rows = received.reshape(DEVICES, OWNED, SLOT, CELLS)[:, :, PART, :]
    sent = rows[:, 4, : 3 * PX].astype(jnp.int32)
    owner = lax.broadcasted_iota(jnp.int32, (PX, DEVICES), 1)
    counts = sent[:, 2 * PX : 3 * PX].T
    where = [
        jnp.where(k < counts, owner * OWNED + sent[:, k * PX : (k + 1) * PX].T, -1) for k in range(2)
    ]
    mine = lax.dynamic_slice_in_dim(rows, lax.axis_index("py") * PX, PX, axis=0).astype(jnp.int32)
    slot = mine[:, 0:2].reshape(PX, ENTRIES)
    pattern = mine[:, 2:4].reshape(PX, ENTRIES)
    owner_at = lax.broadcasted_iota(jnp.int32, (PX, ENTRIES, DEVICES), 2)
    found = jnp.where(slot[:, :, None] % 2 == 0, where[0][:, None, :], where[1][:, None, :])
    block = jnp.sum(jnp.where(slot[:, :, None] // 2 == owner_at, found, 0), axis=2)
    return jnp.where(block >= 0, pattern * TILES + block, ZERO_TILE).reshape(PX * ENTRIES)


def shifted(rows, left, right):
    wide = rows.astype(F32)
    column = lax.broadcasted_iota(jnp.int32, wide.shape, 0)
    last = wide.shape[0] - 1
    before = jnp.where(column == 0, jnp.broadcast_to(left, wide.shape), pltpu.roll(wide, 1, 0))
    after = jnp.where(column == last, jnp.broadcast_to(right, wide.shape), pltpu.roll(wide, last, 0))
    return before.astype(BF16), rows, after.astype(BF16)


def fill(taps_ref, row, cells, left_ref, right_ref):
    depth = cells.shape[-1]
    parts = shifted(cells, left_ref[row], right_ref[row])
    for k in range(3):
        taps_ref[row, :, k * depth : (k + 1) * depth] = parts[k]


def fill_all(taps_ref, cells_ref, top_ref, bottom_ref, left_ref, right_ref):
    count = cells_ref.shape[0]
    fill(taps_ref, 0, top_ref[0], left_ref, right_ref)

    def one(row, carry):
        fill(taps_ref, row + 1, cells_ref[row], left_ref, right_ref)
        return carry

    lax.fori_loop(0, count, one, 0)
    fill(taps_ref, count + 1, bottom_ref[0], left_ref, right_ref)


def taps_dot(taps_ref, weights_ref, first_row, count):
    columns, depth = taps_ref.shape[1], taps_ref.shape[2]
    total = None
    for row_off in range(3):
        rows = taps_ref[pl.ds(first_row + row_off, count)].reshape(count * columns, depth)
        product = dot(rows, weights_ref[row_off])
        total = product if total is None else total + product
    return total


STRIP = 8


def conv_kernel(cells_ref, top_ref, bottom_ref, left_ref, right_ref, weights_ref, out_ref, taps_ref):
    step = pl.program_id(0)

    @pl.when(step == 0)
    def _():
        fill_all(taps_ref, cells_ref, top_ref, bottom_ref, left_ref, right_ref)

    out_ref[...] = taps_dot(taps_ref, weights_ref, step * STRIP, STRIP).reshape(STRIP, COLUMNS, FINE)


def whole(*shape):
    return pl.BlockSpec(shape, lambda i: (0,) * len(shape))


def conv_fine(cells, halo, weights):
    return pl.pallas_call(
        conv_kernel,
        grid=(ROWS // STRIP,),
        in_specs=[
            whole(ROWS, COLUMNS, FINE),
            whole(1, COLUMNS, FINE),
            whole(1, COLUMNS, FINE),
            whole(ROWS + 2, 1, FINE),
            whole(ROWS + 2, 1, FINE),
            whole(3, 3 * FINE, FINE),
        ],
        out_specs=pl.BlockSpec((STRIP, COLUMNS, FINE), lambda i: (i, 0, 0)),
        out_shape=jax.ShapeDtypeStruct((ROWS, COLUMNS, FINE), F32),
        scratch_shapes=[pltpu.VMEM((ROWS + 2, COLUMNS, 3 * FINE), BF16)],
        compiler_params=pltpu.CompilerParams(vmem_limit_bytes=48 * MIB),
    )(cells, *halo, weights)


def first_kernel(blended_ref, lift_ref, conv_ref, cells_ref, first_ref, pooled_ref):
    cell = lax.broadcasted_iota(jnp.int32, (32, CELLS), 1)
    target = lax.broadcasted_iota(jnp.int32, (32, CELLS), 0)
    row = cell // SUBTILE_COLUMNS
    column = cell % SUBTILE_COLUMNS
    pool = jnp.where((row // 2) * 8 + column // 2 == target, 0.25, 0.0).astype(BF16)
    for pair in range(COLUMNS // SUBTILE_COLUMNS // 2):
        both = blended_ref[:, pair * 2 * SLOT : (pair + 1) * 2 * SLOT, :].astype(F32)
        for half in range(2):
            tile = 2 * pair + half
            columns = slice(tile * SUBTILE_COLUMNS, (tile + 1) * SUBTILE_COLUMNS)
            part = both[:, half * SLOT : (half + 1) * SLOT, :].reshape(PX * SLOT, CELLS).astype(BF16)
            guidance = lax.dot_general(
                part, lift_ref[...], (((0,), (0,)), ((), ())), preferred_element_type=F32
            ).astype(BF16)
            summed = conv_ref[:, columns, :].reshape(CELLS, FINE) + guidance.astype(F32)
            kept = cells_ref[:, columns, :].reshape(CELLS, FINE).astype(F32)
            first = (kept + silu(summed)).astype(BF16)
            first_ref[:, columns, :] = first.reshape(SUBTILE_ROWS, SUBTILE_COLUMNS, FINE)
            pooled_ref[:, tile * 8 : (tile + 1) * 8, :] = dot(pool, first).reshape(4, 8, FINE).astype(BF16)


def first_level(blended, lift, conv, cells):
    strip = pl.BlockSpec((STRIP, COLUMNS, FINE), lambda i: (i, 0, 0))
    return pl.pallas_call(
        first_kernel,
        grid=(ROWS // STRIP,),
        in_specs=[
            pl.BlockSpec((PX, 8 * SLOT, CELLS), lambda i: (0, i, 0)),
            whole(PX * SLOT, FINE),
            strip,
            strip,
        ],
        out_specs=[strip, pl.BlockSpec((STRIP // 2, COLUMNS // 2, FINE), lambda i: (i, 0, 0))],
        out_shape=[
            jax.ShapeDtypeStruct((ROWS, COLUMNS, FINE), BF16),
            jax.ShapeDtypeStruct((ROWS // 2, COLUMNS // 2, FINE), BF16),
        ],
        compiler_params=pltpu.CompilerParams(vmem_limit_bytes=32 * MIB),
    )(blended, lift, conv, cells)


SECOND = 8


def second_kernel(
    pooled_ref, top_ref, bottom_ref, left_ref, right_ref, weights_ref, up_ref, first_ref, out_ref, taps_ref, spread_ref
):
    step = pl.program_id(0)

    @pl.when(step == 0)
    def _():
        fill_all(taps_ref, pooled_ref, top_ref, bottom_ref, left_ref, right_ref)

    second = silu(taps_dot(taps_ref, weights_ref, step * SECOND, SECOND)).astype(BF16)
    projected = dot(second, up_ref[...])
    half = COLUMNS // 2
    for lane in range(FINE // 128):
        part = projected[:, lane * 128 : (lane + 1) * 128]
        for side in range(2):
            spread_ref[lane, pl.ds(side, SECOND * half, stride=2), :] = part
    for lane in range(FINE // 128):
        lanes = slice(lane * 128, (lane + 1) * 128)
        for row in range(SECOND):
            added = spread_ref[lane, row * COLUMNS : (row + 1) * COLUMNS, :]
            for side in range(2):
                first = first_ref[2 * row + side, :, lanes].astype(F32)
                out_ref[2 * row + side, :, lanes] = (first + added).astype(BF16)


def second_level(pooled, halo, weights, up, first):
    strip = pl.BlockSpec((2 * SECOND, COLUMNS, FINE), lambda i: (i, 0, 0))
    return pl.pallas_call(
        second_kernel,
        grid=(ROWS // 2 // SECOND,),
        in_specs=[
            whole(ROWS // 2, COLUMNS // 2, FINE),
            whole(1, COLUMNS // 2, FINE),
            whole(1, COLUMNS // 2, FINE),
            whole(ROWS // 2 + 2, 1, FINE),
            whole(ROWS // 2 + 2, 1, FINE),
            whole(3, 3 * FINE, WIDE),
            whole(WIDE, FINE),
            strip,
        ],
        out_specs=strip,
        out_shape=jax.ShapeDtypeStruct((ROWS, COLUMNS, FINE), BF16),
        scratch_shapes=[
            pltpu.VMEM((ROWS // 2 + 2, COLUMNS // 2, 3 * FINE), BF16),
            pltpu.VMEM((FINE // 128, SECOND * COLUMNS, 128), F32),
        ],
        compiler_params=pltpu.CompilerParams(vmem_limit_bytes=48 * MIB),
    )(pooled, *halo, weights, up, first)


def halo_of(cells):
    down = [(i, i + 1) for i in range(PY - 1)]
    up = [(i + 1, i) for i in range(PY - 1)]
    top = lax.ppermute(cells[-1:], "py", down)
    bottom = lax.ppermute(cells[:1], "py", up)

    def column(at):
        return jnp.concatenate([top[:, at], cells[:, at], bottom[:, at]], axis=0)

    left = lax.ppermute(column(-1), "px", [(i, i + 1) for i in range(PX - 1)])
    right = lax.ppermute(column(0), "px", [(i + 1, i) for i in range(PX - 1)])
    return top, bottom, left[:, None].astype(F32), right[:, None].astype(F32)


def local(
    features,
    coarse,
    send_ids,
    send_counts,
    entry_slot,
    entry_weight_pattern,
    interpolation_weights,
    lift_weight,
    conv_a,
    conv_b,
    up_weight,
):
    ids = send_ids[0].reshape(PY, PX, 2)
    sent = jnp.concatenate([ids[:, :, 0], ids[:, :, 1], send_counts[0].reshape(PY, PX)], axis=1)
    sent = jnp.pad(sent, ((0, 0), (0, CELLS - 3 * PX)))[:, None]
    named = jnp.concatenate([entry_slot[0].reshape(2, CELLS), entry_weight_pattern[0].reshape(2, CELLS)], axis=0)
    named = jnp.broadcast_to(named[None], (PY, 4, CELLS))
    tables = jnp.concatenate([named, sent, jnp.zeros((PY, 3, CELLS), jnp.int32)], axis=1).astype(F32)
    outgoing = pack(coarse, tables).reshape(DEVICES, OWNED * SLOT, CELLS)
    received = lax.all_to_all(outgoing, ("py", "px"), split_axis=0, concat_axis=0, tiled=True)
    index = entry_index(received)
    parts = blend(index, received.reshape(TILES * SLOT, CELLS), interpolation_weights)
    blended = lax.all_to_all(
        parts.reshape(PX, SUBTILES * SLOT, CELLS), "px", split_axis=0, concat_axis=0, tiled=True
    )
    conv = conv_fine(features, halo_of(features), conv_a.reshape(3, 3 * FINE, FINE))
    lift = jnp.pad(lift_weight, ((0, PX * PART - CHANNELS), (0, 0))).reshape(PX, PART, FINE)
    lift = jnp.pad(lift, ((0, 0), (0, SLOT - PART), (0, 0))).reshape(PX * SLOT, FINE)
    first, pooled = first_level(blended, lift, conv, features)
    return second_level(pooled, halo_of(pooled), conv_b.reshape(3, 3 * FINE, WIDE), up_weight, first)


def solution(mesh):
    placed = (
        P("py", "px", None),
        P(("py", "px"), None, None),
        P(("py", "px"), None, None),
        P(("py", "px"), None),
        P(("py", "px"), None),
        P(("py", "px"), None),
        P(),
        P(),
        P(),
        P(),
        P(),
    )
    return jax.shard_map(
        local, mesh=mesh, in_specs=placed, out_specs=P("py", "px", None), check_vma=False
    )
```

profile of v0, /device:TPU:29, one launch (start us, length us, event | category | flops | bytes accessed | tf_op | source)
XLA Modules:
  0.0 183.6 jit_solution(8961650347149674692)
XLA Ops:
  0.0 0.1 pad.29.clone
  0.1 0.5 broadcast.113
  0.6 1.3 reduce.3
  1.9 0.1 reshape_squeeze.15
  2.0 0.8 reshape_squeeze.14
  2.8 0.1 pad_add_fusion
  2.8 1.0 copy.33.coarse_ref
  3.8 0.7 pad_add_fusion.1
  4.5 0.1 add_convert_fusion.tables_ref
  4.6 3.2 %shard_map.109 = bf16[8,16,64,128]{3,2,1,0:T(8,128)(2,1)} custom-call(bf16[8,100,128]{2,1,0:T(8,128)(2,1)S(1)} %copy.33.coarse_ref, f32[8,8,128]{2,1,0:T(8,128)S(1)} %add_convert_fusion.tables_ref), custom_call_target="tpu_custom_call" | custom-call | tf_op jit(solution)/shard_map/pallas_call | solution.py:60
  7.9 10.6 %all-to-all-start = ((bf16[128,64,128]{2,1,0:T(8,128)(2,1)}), bf16[128,64,128]{2,1,0:T(8,128)(2,1)S(1)}, u32[]{:S(2)}, u32[]{:S(2)}) async-start(bf16[128,64,128]{2,1,0:T(8,128)(2,1)} %bitcast.5), calls=%async_computation | async-start | bytes 4194304 | tf_op jit(solution)/shard_map/all_to_all | solution.py:344
  18.4 25.9 %all-to-all-done = bf16[128,64,128]{2,1,0:T(8,128)(2,1)S(1)} async-done(((bf16[128,64,128]{2,1,0:T(8,128)(2,1)}), bf16[128,64,128]{2,1,0:T(8,128)(2,1)S(1)}, u32[]{:S(2)}, u32[]{:S(2)}) %all-to-all-start) | async-done | bytes 2097184 | tf_op jit(solution)/shard_map/all_to_all | solution.py:344
  44.4 0.6 slice.102
  45.0 0.1 dynamic-slice_convert_fusion
  45.2 0.1 slice_convert_fusion
  45.3 0.1 fusion.3
  45.4 0.1 copy.34
  45.5 0.1 copy.35
  45.5 2.1 %select_reduce_fusion = s32[16,256]{1,0:T(8,128)S(1)} fusion(s32[16,128]{1,0:T(8,128)S(1)} %copy.35, s32[16,128]{1,0:T(8,128)S(1)} %copy.34, s32[16,256]{1,0:T(8,128)S(1)} %add_select_fusion.1, pred[16,256]{1,0:T(8,128)(4,1)S(1)} %fusion.4), kind=kLoop, calls=%fused_computation | loop fusion | flops 2093056 | bytes 53248 | tf_op jit(solution)/shard_map/reduce_sum | solution.py:137
  47.6 0.6 add_select_fusion.2.index_ref
  48.2 36.4 %shard_map.110 = bf16[8192,128]{1,0:T(8,128)(2,1)} custom-call(s32[4096]{0:T(1024)} %add_select_fusion.2.index_ref, bf16[8192,128]{1,0:T(8,128)(2,1)} %bitcast.85, bf16[8,128,128]{2,1,0:T(8,128)(2,1)} %weights_ref.1), custom_call_target="tpu_custom_call" | custom-call | tf_op jit(solution)/shard_map/pallas_call | solution.py:110
  84.7 7.5 %all-to-all-start.1 = ((bf16[16,512,128]{2,1,0:T(8,128)(2,1)}), bf16[16,512,128]{2,1,0:T(8,128)(2,1)S(1)}, u32[]{:S(2)}, u32[]{:S(2)}) async-start(bf16[16,512,128]{2,1,0:T(8,128)(2,1)} %bitcast.86), calls=%async_computation.1 | async-start | bytes 4194304 | tf_op jit(solution)/shard_map/all_to_all | solution.py:347
  92.2 1.5 fusion.9
  93.7 3.5 %collective-permute-start.1 = (bf16[1,128,256]{2,1,0:T(8,128)(2,1)}, bf16[1,128,256]{2,1,0:T(8,128)(2,1)S(1)}, u32[]{:S(2)}, u32[]{:S(2)}) collective-permute-start(bf16[1,128,256]{2,1,0:T(8,128)(2,1)} %get-tuple-element.11), channel_id=1, source_target_pairs={{16,0},{32,16},{48,32},{64,48},{80,64},{96,80},{112,96},{17,1},{33... | collective-permute-start | bytes 196616 | tf_op jit(solution)/shard_map/ppermute | solution.py:314
  97.2 2.0 %collective-permute-start = (bf16[1,128,256]{2,1,0:T(8,128)(2,1)}, bf16[1,128,256]{2,1,0:T(8,128)(2,1)S(1)}, u32[]{:S(2)}, u32[]{:S(2)}) collective-permute-start(bf16[1,128,256]{2,1,0:T(8,128)(2,1)} %get-tuple-element.12), channel_id=1, source_target_pairs={{0,16},{16,32},{32,48},{48,64},{64,80},{80,96},{96,112},{1,17},{17... | collective-permute-start | bytes 196616 | tf_op jit(solution)/shard_map/ppermute | solution.py:313
  99.3 1.8 fusion.8
  101.0 0.6 pad.13
  101.7 0.8 reshape.139
  102.5 0.8 copy.68
  103.4 2.8 %collective-permute-start.2 = (bf16[66,256]{1,0:T(8,128)(2,1)S(1)}, bf16[66,256]{1,0:T(8,128)(2,1)S(1)}, u32[]{:S(2)}, u32[]{:S(2)}) collective-permute-start(bf16[66,256]{1,0:T(8,128)(2,1)S(1)} %pad_maximum_fusion), channel_id=1, source_target_pairs={{0,1},{1,2},{2,3},{3,4},{4,5},{5,6},{6,7},{7,8},{8,9},{9,10},{10,1... | collective-permute-start | bytes 101384 | tf_op jit(solution)/shard_map/ppermute | solution.py:319
  106.3 2.5 %collective-permute-start.3 = (bf16[66,256]{1,0:T(8,128)(2,1)S(1)}, bf16[66,256]{1,0:T(8,128)(2,1)S(1)}, u32[]{:S(2)}, u32[]{:S(2)}) collective-permute-start(bf16[66,256]{1,0:T(8,128)(2,1)S(1)} %pad_maximum_fusion.1), channel_id=1, source_target_pairs={{1,0},{2,1},{3,2},{4,3},{5,4},{6,5},{7,6},{8,7},{9,8},{10,9},{11,1... | collective-permute-start | bytes 101384 | tf_op jit(solution)/shard_map/ppermute | solution.py:320
  108.8 5.6 %collective-permute-done.2 = bf16[66,256]{1,0:T(8,128)(2,1)S(1)} collective-permute-done((bf16[66,256]{1,0:T(8,128)(2,1)S(1)}, bf16[66,256]{1,0:T(8,128)(2,1)S(1)}, u32[]{:S(2)}, u32[]{:S(2)}) %collective-permute-start.2) | collective-permute-done | bytes 33824 | tf_op jit(solution)/shard_map/ppermute | solution.py:319
  114.4 1.9 %collective-permute-done.3 = bf16[66,256]{1,0:T(8,128)(2,1)S(1)} collective-permute-done((bf16[66,256]{1,0:T(8,128)(2,1)S(1)}, bf16[66,256]{1,0:T(8,128)(2,1)S(1)}, u32[]{:S(2)}, u32[]{:S(2)}) %collective-permute-start.3) | collective-permute-done | bytes 33824 | tf_op jit(solution)/shard_map/ppermute | solution.py:320
  116.3 0.0 copy-start.1
  116.4 2.2 %copy-done.1 = bf16[64,128,256]{2,1,0:T(8,128)(2,1)S(1)} copy-done((bf16[64,128,256]{2,1,0:T(8,128)(2,1)S(1)}, bf16[64,128,256]{2,1,0:T(8,128)(2,1)}, u32[]{:S(2)}) %copy-start.1) | copy-done | bytes 4194328
  118.5 14.3 %shard_map.111.conv_ref = f32[64,128,256]{2,1,0:T(8,128)} custom-call(bf16[64,128,256]{2,1,0:T(8,128)(2,1)S(1)} %copy-done.1, bf16[1,128,256]{2,1,0:T(8,128)(2,1)S(1)} %collective-permute-done.top_ref, bf16[1,128,256]{2,1,0:T(8,128)(2,1)S(1)} %collective-permute-done.1.bottom_ref, f32[66,1,256]{2,1,0:T(1,128)S(1)} %reshape.145.left_ref, ...), custom_call_target="tpu_custom_call" | custom-call | tf_op jit(solution)/shard_map/pallas_call | solution.py:197
  132.8 3.4 %copy-done = f32[64,128,256]{2,1,0:T(8,128)S(1)} copy-done((f32[64,128,256]{2,1,0:T(8,128)S(1)}, f32[64,128,256]{2,1,0:T(8,128)}, u32[]{:S(2)}) %copy-start) | copy-done | bytes 8388632
  136.2 2.2 %copy-done.2 = bf16[64,128,256]{2,1,0:T(8,128)(2,1)S(1)} copy-done((bf16[64,128,256]{2,1,0:T(8,128)(2,1)S(1)}, bf16[64,128,256]{2,1,0:T(8,128)(2,1)}, u32[]{:S(2)}) %copy-start.2) | copy-done | bytes 4194328
  138.4 13.1 %shard_map.112 = (bf16[64,128,256]{2,1,0:T(8,128)(2,1)S(1)}, bf16[32,64,256]{2,1,0:T(8,128)(2,1)S(1)}) custom-call(bf16[16,512,128]{2,1,0:T(8,128)(2,1)S(1)} %all-to-all-done.1.blended_ref, bf16[128,256]{1,0:T(8,128)(2,1)S(1)} %pad_bitcast_fusion.lift_ref, f32[64,128,256]{2,1,0:T(8,128)S(1)} %copy-done, bf16[64,128,256]{2,1,0:T(8,128)(2,1)S(1)} %copy-done.2), custom_call_target="tpu_custom_call" | custom-call | tf_op jit(solution)/shard_map/pallas_call | solution.py:239
  151.5 2.0 %copy-done.3 = bf16[64,128,256]{2,1,0:T(8,128)(2,1)} copy-done((bf16[64,128,256]{2,1,0:T(8,128)(2,1)}, bf16[64,128,256]{2,1,0:T(8,128)(2,1)S(1)}, u32[]{:S(2)}) %copy-start.3) | copy-done | bytes 4194328
  153.4 0.6 copy.38
  154.0 6.3 %collective-permute-start.5 = (bf16[1,64,256]{2,1,0:T(8,128)(2,1)S(1)}, bf16[1,64,256]{2,1,0:T(8,128)(2,1)S(1)}, u32[]{:S(2)}, u32[]{:S(2)}) collective-permute-start(bf16[1,64,256]{2,1,0:T(8,128)(2,1)S(1)} %get-tuple-element.15), channel_id=1, source_target_pairs={{16,0},{32,16},{48,32},{64,48},{80,64},{96,80},{112,96},{17,1},{33... | collective-permute-start | bytes 98312 | tf_op jit(solution)/shard_map/ppermute | solution.py:314
  160.4 1.9 %collective-permute-start.4 = (bf16[1,64,256]{2,1,0:T(8,128)(2,1)S(1)}, bf16[1,64,256]{2,1,0:T(8,128)(2,1)S(1)}, u32[]{:S(2)}, u32[]{:S(2)}) collective-permute-start(bf16[1,64,256]{2,1,0:T(8,128)(2,1)S(1)} %get-tuple-element.16), channel_id=1, source_target_pairs={{0,16},{16,32},{32,48},{48,64},{64,80},{80,96},{96,112},{1,17},{17... | collective-permute-start | bytes 98312 | tf_op jit(solution)/shard_map/ppermute | solution.py:313
  162.3 1.1 collective-permute-done.4.top_ref
  163.5 3.6 %collective-permute-start.6 = (bf16[34,256]{1,0:T(8,128)(2,1)S(1)}, bf16[34,256]{1,0:T(8,128)(2,1)S(1)}, u32[]{:S(2)}, u32[]{:S(2)}) collective-permute-start(bf16[34,256]{1,0:T(8,128)(2,1)S(1)} %pad_maximum_fusion.2), channel_id=1, source_target_pairs={{0,1},{1,2},{2,3},{3,4},{4,5},{5,6},{6,7},{7,8},{8,9},{9,10},{10,1... | collective-permute-start | bytes 52232 | tf_op jit(solution)/shard_map/ppermute | solution.py:319
  167.1 1.9 %collective-permute-start.7 = (bf16[34,256]{1,0:T(8,128)(2,1)S(1)}, bf16[34,256]{1,0:T(8,128)(2,1)S(1)}, u32[]{:S(2)}, u32[]{:S(2)}) collective-permute-start(bf16[34,256]{1,0:T(8,128)(2,1)S(1)} %pad_maximum_fusion.3), channel_id=1, source_target_pairs={{1,0},{2,1},{3,2},{4,3},{5,4},{6,5},{7,6},{8,7},{9,8},{10,9},{11,1... | collective-permute-start | bytes 52232 | tf_op jit(solution)/shard_map/ppermute | solution.py:320
  169.1 4.7 %collective-permute-done.7 = bf16[34,256]{1,0:T(8,128)(2,1)S(1)} collective-permute-done((bf16[34,256]{1,0:T(8,128)(2,1)S(1)}, bf16[34,256]{1,0:T(8,128)(2,1)S(1)}, u32[]{:S(2)}, u32[]{:S(2)}) %collective-permute-start.7) | collective-permute-done | bytes 17440 | tf_op jit(solution)/shard_map/ppermute | solution.py:320
  173.8 9.8 %shard_map.113 = bf16[64,128,256]{2,1,0:T(8,128)(2,1)} custom-call(bf16[32,64,256]{2,1,0:T(8,128)(2,1)S(1)} %get-tuple-element.7.pooled_ref, bf16[1,64,256]{2,1,0:T(8,128)(2,1)S(1)} %collective-permute-done.4.top_ref, bf16[1,64,256]{2,1,0:T(8,128)(2,1)S(1)} %collective-permute-done.5.bottom_ref, f32[34,1,256]{2,1,0:T(1,128)S(1)} %reshape.147.left_ref, ...), custom_call_target="tpu_custom_call" | custom-call | tf_op jit(solution)/shard_map/pallas_call | solution.py:287
  (44 shorter events, 0.4 us)
Async XLA Ops:
  7.9 36.5 %all-to-all-start = ((bf16[128,64,128]{2,1,0:T(8,128)(2,1)}), bf16[128,64,128]{2,1,0:T(8,128)(2,1)S(1)}, u32[]{:S(2)}, u32[]{:S(2)}) async-start(bf16[128,64,128]{2,1,0:T(8,128)(2,1)} %bitcast.5), calls=%async_computation | async-start | bytes 4194304 | tf_op jit(solution)/shard_map/all_to_all | solution.py:344
  44.4 3.9 %copy-start.7 = (bf16[128,64,128]{2,1,0:T(8,128)(2,1)}, bf16[128,64,128]{2,1,0:T(8,128)(2,1)S(1)}, u32[]{:S(2)}) copy-start(bf16[128,64,128]{2,1,0:T(8,128)(2,1)S(1)} %all-to-all-done) | copy-start | bytes 6291460
  84.7 16.3 %copy-start.8 = (bf16[100,256]{1,0:T(8,128)(2,1)S(1)}, bf16[100,256]{1,0:T(8,128)(2,1)}, u32[]{:S(2)}) copy-start(bf16[100,256]{1,0:T(8,128)(2,1)} %param.18) | copy-start | bytes 153604
  84.7 31.7 %copy-start.5 = (bf16[3,3,256,256]{3,2,1,0:T(8,128)(2,1)S(1)}, bf16[3,3,256,256]{3,2,1,0:T(8,128)(2,1)}, u32[]{:S(2)}) copy-start(bf16[3,3,256,256]{3,2,1,0:T(8,128)(2,1)} %param.19) | copy-start | bytes 3538948
  84.7 48.1 %all-to-all-start.1 = ((bf16[16,512,128]{2,1,0:T(8,128)(2,1)}), bf16[16,512,128]{2,1,0:T(8,128)(2,1)S(1)}, u32[]{:S(2)}, u32[]{:S(2)}) async-start(bf16[16,512,128]{2,1,0:T(8,128)(2,1)} %bitcast.86), calls=%async_computation.1 | async-start | bytes 4194304 | tf_op jit(solution)/shard_map/all_to_all | solution.py:347
  93.7 9.7 %collective-permute-start.1 = (bf16[1,128,256]{2,1,0:T(8,128)(2,1)}, bf16[1,128,256]{2,1,0:T(8,128)(2,1)S(1)}, u32[]{:S(2)}, u32[]{:S(2)}) collective-permute-start(bf16[1,128,256]{2,1,0:T(8,128)(2,1)} %get-tuple-element.11), channel_id=1, source_target_pairs={{16,0},{32,16},{48,32},{64,48},{80,64},{96,80},{112,96},{17,1},{33... | collective-permute-start | bytes 196616 | tf_op jit(solution)/shard_map/ppermute | solution.py:314
  97.2 6.2 %collective-permute-start = (bf16[1,128,256]{2,1,0:T(8,128)(2,1)}, bf16[1,128,256]{2,1,0:T(8,128)(2,1)S(1)}, u32[]{:S(2)}, u32[]{:S(2)}) collective-permute-start(bf16[1,128,256]{2,1,0:T(8,128)(2,1)} %get-tuple-element.12), channel_id=1, source_target_pairs={{0,16},{16,32},{32,48},{48,64},{64,80},{80,96},{96,112},{1,17},{17... | collective-permute-start | bytes 196616 | tf_op jit(solution)/shard_map/ppermute | solution.py:313
  103.4 10.9 %collective-permute-start.2 = (bf16[66,256]{1,0:T(8,128)(2,1)S(1)}, bf16[66,256]{1,0:T(8,128)(2,1)S(1)}, u32[]{:S(2)}, u32[]{:S(2)}) collective-permute-start(bf16[66,256]{1,0:T(8,128)(2,1)S(1)} %pad_maximum_fusion), channel_id=1, source_target_pairs={{0,1},{1,2},{2,3},{3,4},{4,5},{5,6},{6,7},{7,8},{8,9},{9,10},{10,1... | collective-permute-start | bytes 101384 | tf_op jit(solution)/shard_map/ppermute | solution.py:319
  106.3 10.0 %collective-permute-start.3 = (bf16[66,256]{1,0:T(8,128)(2,1)S(1)}, bf16[66,256]{1,0:T(8,128)(2,1)S(1)}, u32[]{:S(2)}, u32[]{:S(2)}) collective-permute-start(bf16[66,256]{1,0:T(8,128)(2,1)S(1)} %pad_maximum_fusion.1), channel_id=1, source_target_pairs={{1,0},{2,1},{3,2},{4,3},{5,4},{6,5},{7,6},{8,7},{9,8},{10,9},{11,1... | collective-permute-start | bytes 101384 | tf_op jit(solution)/shard_map/ppermute | solution.py:320
  116.3 2.2 %copy-start.1 = (bf16[64,128,256]{2,1,0:T(8,128)(2,1)S(1)}, bf16[64,128,256]{2,1,0:T(8,128)(2,1)}, u32[]{:S(2)}) copy-start(bf16[64,128,256]{2,1,0:T(8,128)(2,1)} %cells_ref.3) | copy-start | bytes 12582916
  132.8 3.4 %copy-start = (f32[64,128,256]{2,1,0:T(8,128)S(1)}, f32[64,128,256]{2,1,0:T(8,128)}, u32[]{:S(2)}) copy-start(f32[64,128,256]{2,1,0:T(8,128)} %shard_map.111.conv_ref) | copy-start | bytes 25165828
  136.2 2.2 %copy-start.2 = (bf16[64,128,256]{2,1,0:T(8,128)(2,1)S(1)}, bf16[64,128,256]{2,1,0:T(8,128)(2,1)}, u32[]{:S(2)}) copy-start(bf16[64,128,256]{2,1,0:T(8,128)(2,1)} %cells_ref.3) | copy-start | bytes 12582916
  138.4 35.4 %copy-start.6 = (bf16[512,256]{1,0:T(8,128)(2,1)S(1)}, bf16[512,256]{1,0:T(8,128)(2,1)}, u32[]{:S(2)}) copy-start(bf16[512,256]{1,0:T(8,128)(2,1)} %up_ref.1) | copy-start | bytes 786436
  151.4 2.0 %copy-start.3 = (bf16[64,128,256]{2,1,0:T(8,128)(2,1)}, bf16[64,128,256]{2,1,0:T(8,128)(2,1)S(1)}, u32[]{:S(2)}) copy-start(bf16[64,128,256]{2,1,0:T(8,128)(2,1)S(1)} %get-tuple-element.8.first_ref) | copy-start | bytes 12582916
  153.4 20.4 %copy-start.4 = (bf16[3,3,256,512]{3,2,1,0:T(8,128)(2,1)S(1)}, bf16[3,3,256,512]{3,2,1,0:T(8,128)(2,1)}, u32[]{:S(2)}) copy-start(bf16[3,3,256,512]{3,2,1,0:T(8,128)(2,1)} %param.20) | copy-start | bytes 7077892
  154.0 8.3 %collective-permute-start.5 = (bf16[1,64,256]{2,1,0:T(8,128)(2,1)S(1)}, bf16[1,64,256]{2,1,0:T(8,128)(2,1)S(1)}, u32[]{:S(2)}, u32[]{:S(2)}) collective-permute-start(bf16[1,64,256]{2,1,0:T(8,128)(2,1)S(1)} %get-tuple-element.15), channel_id=1, source_target_pairs={{16,0},{32,16},{48,32},{64,48},{80,64},{96,80},{112,96},{17,1},{33... | collective-permute-start | bytes 98312 | tf_op jit(solution)/shard_map/ppermute | solution.py:314
  160.4 3.1 %collective-permute-start.4 = (bf16[1,64,256]{2,1,0:T(8,128)(2,1)S(1)}, bf16[1,64,256]{2,1,0:T(8,128)(2,1)S(1)}, u32[]{:S(2)}, u32[]{:S(2)}) collective-permute-start(bf16[1,64,256]{2,1,0:T(8,128)(2,1)S(1)} %get-tuple-element.16), channel_id=1, source_target_pairs={{0,16},{16,32},{32,48},{48,64},{64,80},{80,96},{96,112},{1,17},{17... | collective-permute-start | bytes 98312 | tf_op jit(solution)/shard_map/ppermute | solution.py:313
  163.5 5.6 %collective-permute-start.6 = (bf16[34,256]{1,0:T(8,128)(2,1)S(1)}, bf16[34,256]{1,0:T(8,128)(2,1)S(1)}, u32[]{:S(2)}, u32[]{:S(2)}) collective-permute-start(bf16[34,256]{1,0:T(8,128)(2,1)S(1)} %pad_maximum_fusion.2), channel_id=1, source_target_pairs={{0,1},{1,2},{2,3},{3,4},{4,5},{5,6},{6,7},{7,8},{8,9},{9,10},{10,1... | collective-permute-start | bytes 52232 | tf_op jit(solution)/shard_map/ppermute | solution.py:319
  167.1 6.6 %collective-permute-start.7 = (bf16[34,256]{1,0:T(8,128)(2,1)S(1)}, bf16[34,256]{1,0:T(8,128)(2,1)S(1)}, u32[]{:S(2)}, u32[]{:S(2)}) collective-permute-start(bf16[34,256]{1,0:T(8,128)(2,1)S(1)} %pad_maximum_fusion.3), channel_id=1, source_target_pairs={{1,0},{2,1},{3,2},{4,3},{5,4},{6,5},{7,6},{8,7},{9,8},{10,9},{11,1... | collective-permute-start | bytes 52232 | tf_op jit(solution)/shard_map/ppermute | solution.py:320
where the time goes:
time: 186 us; the launch traced here: 184 us
  Pallas kernels  76.8 us (41%)
  starting transfers between devices  42.7 us (23%)
  waiting for transfers between devices  39.2 us (21%)
  local copies, waits for them, and re-layouts  19.2 us (10%)
  other arithmetic  5.31 us (3%)
    pallas_call x1, Pallas kernels, blend(): pl.pallas_call(blend_kernel, in_specs=[pl.BlockSpec(memory_space=pltpu.SM...  36.4 us
    all_to_all x1, waiting for transfers between devices, local(): lax.all_to_all(outgoing, ('py', 'px'), split_axis=0, concat_axis=0, tiled...  25.9 us
    pallas_call x1, Pallas kernels, conv_fine(): pl.pallas_call(conv_kernel, grid=(ROWS // STRIP,), in_specs=[whole(ROWS,...  14.3 us
    pallas_call x1, Pallas kernels, first_level(): pl.pallas_call(first_kernel, grid=(ROWS // STRIP,), in_specs=[pl.BlockSpe...  13.1 us
    unnamed x24, local copies, waits for them, and re-layouts  12.1 us
    all_to_all x1, starting transfers between devices, local(): lax.all_to_all(outgoing, ('py', 'px'), split_axis=0, concat_axis=0, tiled...  10.6 us
    ppermute x2, starting transfers between devices, halo_of(): bottom = lax.ppermute(cells[:1], 'py', up)  9.84 us
    pallas_call x1, Pallas kernels, second_level(): pl.pallas_call(second_kernel, grid=(ROWS // 2 // SECOND,), in_specs=[whol...  9.78 us
  transfers between devices with their start and end apart: 10, of which 5 were waited for; matrix products, arithmetic and copies ran while one was open for 3% of the time, Pallas kernels for 8%

commit v1 on v0

--- a/solution.py
+++ b/solution.py
@@ -3,6 +3,7 @@
 from jax import lax
 from jax.experimental import pallas as pl
 from jax.experimental.pallas import tpu as pltpu
+from jax.sharding import Mesh
 from jax.sharding import PartitionSpec as P
 
 F32 = jnp.float32
@@ -12,8 +13,11 @@
 SUBTILE_ENTRIES = 4
 SUBTILE_ROWS = 8
 SUBTILE_COLUMNS = 16
-PY = 8
+Z = 4
+CORES = 2
+PY = Z * CORES
 PX = 16
+NEAR = PY // CORES * PX
 DEVICES = PY * PX
 OWNED = 8
 CELLS = 128
@@ -59,82 +63,96 @@
 def pack(coarse, tables):
     return pl.pallas_call(
         pack_kernel,
-        grid=(PY,),
+        grid=(Z,),
         in_specs=[
             pl.BlockSpec((OWNED, CHANNELS, CELLS), lambda i: (0, 0, 0)),
             pl.BlockSpec((1, OWNED, CELLS), lambda i: (i, 0, 0)),
         ],
         out_specs=pl.BlockSpec((1, PX, OWNED * SLOT, CELLS), lambda i: (i, 0, 0, 0)),
-        out_shape=jax.ShapeDtypeStruct((PY, PX, OWNED * SLOT, CELLS), BF16),
+        out_shape=jax.ShapeDtypeStruct((Z, PX, OWNED * SLOT, CELLS), BF16),
         scratch_shapes=[pltpu.VMEM((PX, OWNED, SLOT, CELLS), F32)],
         compiler_params=pltpu.CompilerParams(vmem_limit_bytes=24 * MIB),
     )(coarse, tables)
 
 
-def blend_kernel(index_ref, blocks_ref, weights_ref, out_ref, table_ref):
+def blend_kernel(index_ref, own_ref, other_ref, weights_ref, out_ref, table_ref):
     chunk = 1024
 
-    def multiply(step, carry):
+    def multiply(blocks_ref, first, step):
         rows = pl.ds(pl.multiple_of(step * chunk, chunk), chunk)
-        tiles = pl.ds(pl.multiple_of(step * (chunk // SLOT), chunk // SLOT), chunk // SLOT)
         part = blocks_ref[rows, :]
         for pair in range(PATTERNS // 2):
             both = jnp.concatenate([weights_ref[2 * pair], weights_ref[2 * pair + 1]], axis=1)
             product = dot(part, both)
             for half in range(2):
-                table_ref[2 * pair + half, tiles] = product[:, half * CELLS : (half + 1) * CELLS].reshape(
-                    chunk // SLOT, SLOT, CELLS
-                )
-        return carry
-
-    lax.fori_loop(0, TILES * SLOT // chunk, multiply, 0)
-    table_ref[PATTERNS, 0] = jnp.zeros((SLOT, CELLS), F32)
+                tiles = pl.ds((2 * pair + half) * TILES + first + step * (chunk // SLOT), chunk // SLOT)
+                lanes = slice(half * CELLS, (half + 1) * CELLS)
+                table_ref[tiles] = product[:, lanes].reshape(chunk // SLOT, SLOT, CELLS)
+
+    for first, blocks_ref in ((0, own_ref), (TILES // 2, other_ref)):
+
+        def one(step, carry):
+            multiply(blocks_ref, first, step)
+            return carry
+
+        lax.fori_loop(0, TILES // 2 * SLOT // chunk, one, 0)
+    table_ref[ZERO_TILE] = jnp.zeros((SLOT, CELLS), F32)
 
     def total(base):
-        tile = [table_ref[index_ref[base + i] // TILES, index_ref[base + i] % TILES] for i in range(SUBTILE_ENTRIES)]
+        tile = [table_ref[index_ref[base + i]] for i in range(SUBTILE_ENTRIES)]
         return (tile[0] + tile[1]) + (tile[2] + tile[3])
 
-    group = 8
+    group = 32
 
     def gather(step, carry):
         base = step * (group * SUBTILE_ENTRIES)
         sums = [total(base + k * SUBTILE_ENTRIES) for k in range(group)]
-        rows = pl.ds(pl.multiple_of(step * group * SLOT, group * SLOT), group * SLOT)
-        out_ref[rows, :] = jnp.concatenate(sums, axis=0).astype(BF16)
+        for k in range(0, group, 2):
+            rows = pl.ds(pl.multiple_of((step * group + k) * SLOT, 2 * SLOT), 2 * SLOT)
+            out_ref[rows, :] = jnp.concatenate(sums[k : k + 2], axis=0).astype(BF16)
         return carry
 
     lax.fori_loop(0, PX * SUBTILES // group, gather, 0)
 
 
-def blend(index, blocks, weights):
+def blend(index, own, other, weights):
     return pl.pallas_call(
         blend_kernel,
         in_specs=[
             pl.BlockSpec(memory_space=pltpu.SMEM),
             pl.BlockSpec(memory_space=pltpu.VMEM),
             pl.BlockSpec(memory_space=pltpu.VMEM),
+            pl.BlockSpec(memory_space=pltpu.VMEM),
         ],
         out_specs=pl.BlockSpec(memory_space=pltpu.VMEM),
         out_shape=jax.ShapeDtypeStruct((PX * SUBTILES * SLOT, CELLS), BF16),
-        scratch_shapes=[pltpu.VMEM((PATTERNS + 1, TILES, SLOT, CELLS), F32)],
-        compiler_params=pltpu.CompilerParams(vmem_limit_bytes=56 * MIB),
-    )(index, blocks, weights)
-
-
-def entry_index(received):
-    rows = received.reshape(DEVICES, OWNED, SLOT, CELLS)[:, :, PART, :]
-    sent = rows[:, 4, : 3 * PX].astype(jnp.int32)
-    owner = lax.broadcasted_iota(jnp.int32, (PX, DEVICES), 1)
+        scratch_shapes=[pltpu.VMEM((ZERO_TILE + 1, SLOT, CELLS), F32)],
+        compiler_params=pltpu.CompilerParams(vmem_limit_bytes=42 * MIB),
+    )(index, own, other, weights)
+
+
+def entry_index(own, other):
+    core = lax.axis_index("core")
+
+    def tables(part):
+        return part.reshape(NEAR, OWNED, SLOT, CELLS)[:, :, PART, :]
+
+    rows = jnp.concatenate([tables(own), tables(other)], axis=0)
+    mine = lax.dynamic_slice_in_dim(rows[:NEAR], lax.axis_index("z") * PX, PX, axis=0).astype(jnp.int32)
+    slot = mine[:, 0:2].reshape(PX, ENTRIES)
+    pattern = mine[:, 2:4].reshape(PX, ENTRIES)
+    sent = lax.dynamic_slice_in_dim(rows[:, 4], core * 3 * PX, 3 * PX, axis=1).astype(jnp.int32)
+    sender = lax.broadcasted_iota(jnp.int32, (PX, DEVICES), 1)
     counts = sent[:, 2 * PX : 3 * PX].T
     where = [
-        jnp.where(k < counts, owner * OWNED + sent[:, k * PX : (k + 1) * PX].T, -1) for k in range(2)
+        jnp.where(k < counts, sender * OWNED + sent[:, k * PX : (k + 1) * PX].T, -1) for k in range(2)
     ]
-    mine = lax.dynamic_slice_in_dim(rows, lax.axis_index("py") * PX, PX, axis=0).astype(jnp.int32)
-    slot = mine[:, 0:2].reshape(PX, ENTRIES)
-    pattern = mine[:, 2:4].reshape(PX, ENTRIES)
-    owner_at = lax.broadcasted_iota(jnp.int32, (PX, ENTRIES, DEVICES), 2)
+    owner = slot // 2
+    near = owner // (CORES * PX) * PX + owner % PX
+    place = near + jnp.where(owner // PX % CORES == core, 0, NEAR)
+    sender_at = lax.broadcasted_iota(jnp.int32, (PX, ENTRIES, DEVICES), 2)
     found = jnp.where(slot[:, :, None] % 2 == 0, where[0][:, None, :], where[1][:, None, :])
-    block = jnp.sum(jnp.where(slot[:, :, None] // 2 == owner_at, found, 0), axis=2)
+    block = jnp.sum(jnp.where(place[:, :, None] == sender_at, found, 0), axis=2)
     return jnp.where(block >= 0, pattern * TILES + block, ZERO_TILE).reshape(PX * ENTRIES)
 
 
@@ -307,11 +325,14 @@
     )(pooled, *halo, weights, up, first)
 
 
+ROWS_AXES = ("z", "core")
+
+
 def halo_of(cells):
     down = [(i, i + 1) for i in range(PY - 1)]
     up = [(i + 1, i) for i in range(PY - 1)]
-    top = lax.ppermute(cells[-1:], "py", down)
-    bottom = lax.ppermute(cells[:1], "py", up)
+    top = lax.ppermute(cells[-1:], ROWS_AXES, down)
+    bottom = lax.ppermute(cells[:1], ROWS_AXES, up)
 
     def column(at):
         return jnp.concatenate([top[:, at], cells[:, at], bottom[:, at]], axis=0)
@@ -334,20 +355,24 @@
     conv_b,
     up_weight,
 ):
-    ids = send_ids[0].reshape(PY, PX, 2)
-    sent = jnp.concatenate([ids[:, :, 0], ids[:, :, 1], send_counts[0].reshape(PY, PX)], axis=1)
-    sent = jnp.pad(sent, ((0, 0), (0, CELLS - 3 * PX)))[:, None]
+    edges = halo_of(features)
+    ids = send_ids[0].reshape(Z, CORES, PX, 2).transpose(0, 1, 3, 2).reshape(Z, CORES, 2 * PX)
+    sent = jnp.concatenate([ids, send_counts[0].reshape(Z, CORES, PX)], axis=2).reshape(Z, 1, CORES * 3 * PX)
+    sent = jnp.pad(sent, ((0, 0), (0, 0), (0, CELLS - CORES * 3 * PX)))
     named = jnp.concatenate([entry_slot[0].reshape(2, CELLS), entry_weight_pattern[0].reshape(2, CELLS)], axis=0)
-    named = jnp.broadcast_to(named[None], (PY, 4, CELLS))
-    tables = jnp.concatenate([named, sent, jnp.zeros((PY, 3, CELLS), jnp.int32)], axis=1).astype(F32)
-    outgoing = pack(coarse, tables).reshape(DEVICES, OWNED * SLOT, CELLS)
-    received = lax.all_to_all(outgoing, ("py", "px"), split_axis=0, concat_axis=0, tiled=True)
-    index = entry_index(received)
-    parts = blend(index, received.reshape(TILES * SLOT, CELLS), interpolation_weights)
+    named = jnp.broadcast_to(named[None], (Z, 4, CELLS))
+    tables = jnp.concatenate([named, sent, jnp.zeros((Z, 3, CELLS), jnp.int32)], axis=1).astype(F32)
+    outgoing = pack(coarse, tables).reshape(NEAR, OWNED * SLOT, CELLS)
+    own = lax.all_to_all(outgoing, ("z", "px"), split_axis=0, concat_axis=0, tiled=True)
+    other = lax.ppermute(own, "core", [(0, 1), (1, 0)])
+    index = entry_index(own, other)
+    index, edges = lax.optimization_barrier((index, edges))
+    half = (NEAR * OWNED * SLOT, CELLS)
+    parts = blend(index, own.reshape(half), other.reshape(half), interpolation_weights)
     blended = lax.all_to_all(
         parts.reshape(PX, SUBTILES * SLOT, CELLS), "px", split_axis=0, concat_axis=0, tiled=True
     )
-    conv = conv_fine(features, halo_of(features), conv_a.reshape(3, 3 * FINE, FINE))
+    conv = conv_fine(features, edges, conv_a.reshape(3, 3 * FINE, FINE))
     lift = jnp.pad(lift_weight, ((0, PX * PART - CHANNELS), (0, 0))).reshape(PX, PART, FINE)
     lift = jnp.pad(lift, ((0, 0), (0, SLOT - PART), (0, 0))).reshape(PX * SLOT, FINE)
     first, pooled = first_level(blended, lift, conv, features)
@@ -355,13 +380,15 @@
 
 
 def solution(mesh):
+    split = Mesh(mesh.devices.reshape(Z, CORES, PX), ("z", "core", "px"))
+    every = ("z", "core", "px")
     placed = (
-        P("py", "px", None),
-        P(("py", "px"), None, None),
-        P(("py", "px"), None, None),
-        P(("py", "px"), None),
-        P(("py", "px"), None),
-        P(("py", "px"), None),
+        P(ROWS_AXES, "px", None),
+        P(every, None, None),
+        P(every, None, None),
+        P(every, None),
+        P(every, None),
+        P(every, None),
         P(),
         P(),
         P(),
@@ -369,5 +396,5 @@
         P(),
     )
     return jax.shard_map(
-        local, mesh=mesh, in_specs=placed, out_specs=P("py", "px", None), check_vma=False
+        local, mesh=split, in_specs=placed, out_specs=P(ROWS_AXES, "px", None), check_vma=False
     )

time: 186 us -> 144 us (0.77)
  Pallas kernels: 76.8 us -> 50.3 us
  waiting for transfers between devices: 39.2 us -> 20.4 us
  starting transfers between devices: 42.7 us -> 44.9 us
    pallas_call x1, Pallas kernels: 36.4 us -> 11.4 us  [blend(): pl.pallas_call(blend_kernel, in_specs=[pl.BlockSpec(memory_space=pltpu.SM...]
    all_to_all x1, waiting for transfers between devices: 25.9 us -> 1.08 us  [local(): lax.all_to_all(outgoing, ('z', 'px'), split_axis=0, concat_axis=0, tiled=...]
    ppermute x2, waiting for transfers between devices: 5.58 us -> 0.01 us  [halo_of(): left = lax.ppermute(column(-1), 'px', [(i, i + 1) for i in range(PX - 1)])]
    ppermute x4 -> x5, waiting for transfers between devices: 1.14 us -> 5.52 us  [the longest x2 4.18 us: halo_of(): top = lax.ppermute(cells[-1:], ROWS_AXES, down)]
    all_to_all x1, waiting for transfers between devices: 0.01 us -> 4.29 us  [local(): lax.all_to_all(parts.reshape(PX, SUBTILES * SLOT, CELLS), 'px', split_axi...]
    ppermute x2, waiting for transfers between devices: 6.57 us -> 9.48 us  [halo_of(): right = lax.ppermute(column(0), 'px', [(i + 1, i) for i in range(PX - 1)])]
    ppermute x2, starting transfers between devices: 6.44 us -> 8.49 us  [halo_of(): left = lax.ppermute(column(-1), 'px', [(i, i + 1) for i in range(PX - 1)])]
    unnamed x24 -> x28, local copies, waits for them, and re-layouts: 12.1 us -> 14 us
  transfers between devices with their start and end apart: 10 -> 11, of which waited for: 5 -> 7; matrix products, arithmetic and copies ran while one was open for 3% -> 4% of each run, Pallas kernels for 8% -> 10%
where the time goes in v1:
time: 144 us; the launch traced here: 142 us
  Pallas kernels  50.3 us (35%)
  starting transfers between devices  44.9 us (31%)
  local copies, waits for them, and re-layouts  20.9 us (15%)
  waiting for transfers between devices  20.4 us (14%)
  other arithmetic  4.78 us (3%)
    pallas_call x1, Pallas kernels, conv_fine(): pl.pallas_call(conv_kernel, grid=(ROWS // STRIP,), in_specs=[whole(ROWS,...  14.3 us
    unnamed x28, local copies, waits for them, and re-layouts  14 us
    pallas_call x1, Pallas kernels, first_level(): pl.pallas_call(first_kernel, grid=(ROWS // STRIP,), in_specs=[pl.BlockSpe...  13.1 us
    pallas_call x1, Pallas kernels, blend(): pl.pallas_call(blend_kernel, in_specs=[pl.BlockSpec(memory_space=pltpu.SM...  11.4 us
    all_to_all x1, starting transfers between devices, local(): lax.all_to_all(outgoing, ('z', 'px'), split_axis=0, concat_axis=0, tiled=...  10.6 us
    pallas_call x1, Pallas kernels, second_level(): pl.pallas_call(second_kernel, grid=(ROWS // 2 // SECOND,), in_specs=[whol...  9.78 us
    ppermute x2, waiting for transfers between devices, halo_of(): right = lax.ppermute(column(0), 'px', [(i + 1, i) for i in range(PX - 1)])  9.48 us
    ppermute x2, starting transfers between devices, halo_of(): bottom = lax.ppermute(cells[:1], ROWS_AXES, up)  8.56 us
  transfers between devices with their start and end apart: 11, of which 7 were waited for; matrix products, arithmetic and copies ran while one was open for 4% of the time, Pallas kernels for 10%

profile of v1, /device:TPU:29, one launch (start us, length us, event | category | flops | bytes accessed | tf_op | source)
XLA Modules:
  0.0 141.7 jit_solution(5371503913771309435)
XLA Ops:
  0.1 0.5 broadcast.221
  0.6 1.3 reduce.3
  1.9 0.1 reshape_squeeze.15
  2.0 0.8 reshape_squeeze.14
  3.0 1.0 copy.46.coarse_ref
  4.0 0.7 pad_add_fusion.2
  4.8 1.8 %shard_map.109 = bf16[4,16,64,128]{3,2,1,0:T(8,128)(2,1)} custom-call(bf16[8,100,128]{2,1,0:T(8,128)(2,1)S(1)} %copy.46.coarse_ref, f32[4,8,128]{2,1,0:T(8,128)S(1)} %fusion.14.tables_ref), custom_call_target="tpu_custom_call" | custom-call | tf_op jit(solution)/shard_map/pallas_call | solution.py:64
  6.6 10.6 %all-to-all-start = ((bf16[64,64,128]{2,1,0:T(8,128)(2,1)}), bf16[64,64,128]{2,1,0:T(8,128)(2,1)S(1)}, u32[]{:S(2)}, u32[]{:S(2)}) async-start(bf16[64,64,128]{2,1,0:T(8,128)(2,1)} %bitcast.3), calls=%async_computation | async-start | bytes 2097152 | tf_op jit(solution)/shard_map/all_to_all | solution.py:366
  17.1 0.9 fusion.20
  18.1 3.1 %collective-permute-start.2 = (bf16[1,128,256]{2,1,0:T(8,128)(2,1)S(1)}, bf16[1,128,256]{2,1,0:T(8,128)(2,1)S(1)}, u32[]{:S(2)}, u32[]{:S(2)}) collective-permute-start(bf16[1,128,256]{2,1,0:T(8,128)(2,1)S(1)} %get-tuple-element.21), channel_id=1, source_target_pairs={{16,0},{32,16},{48,32},{64,48},{80,64},{96,80},{112,96},{17,1},{33... | collective-permute-start | bytes 196616 | tf_op jit(solution)/shard_map/ppermute | solution.py:335
  21.2 3.0 %collective-permute-start.1 = (bf16[1,128,256]{2,1,0:T(8,128)(2,1)S(1)}, bf16[1,128,256]{2,1,0:T(8,128)(2,1)S(1)}, u32[]{:S(2)}, u32[]{:S(2)}) collective-permute-start(bf16[1,128,256]{2,1,0:T(8,128)(2,1)S(1)} %get-tuple-element.22), channel_id=1, source_target_pairs={{0,16},{16,32},{32,48},{48,64},{64,80},{80,96},{96,112},{1,17},{17... | collective-permute-start | bytes 196616 | tf_op jit(solution)/shard_map/ppermute | solution.py:334
  24.3 1.1 fusion.19
  25.5 1.3 collective-permute-done.2.bottom_ref
  26.8 3.0 %collective-permute-done.1.top_ref = bf16[1,128,256]{2,1,0:T(8,128)(2,1)S(1)} collective-permute-done((bf16[1,128,256]{2,1,0:T(8,128)(2,1)S(1)}, bf16[1,128,256]{2,1,0:T(8,128)(2,1)S(1)}, u32[]{:S(2)}, u32[]{:S(2)}) %collective-permute-start.1) | collective-permute-done | bytes 65568 | tf_op jit(solution)/shard_map/ppermute | solution.py:334
  29.9 0.6 copy-done.9
  30.5 1.1 all-to-all-done
  31.6 2.0 %collective-permute-start = (bf16[64,64,128]{2,1,0:T(8,128)(2,1)S(1)}, bf16[64,64,128]{2,1,0:T(8,128)(2,1)S(1)}, u32[]{:S(2)}, u32[]{:S(2)}) collective-permute-start(bf16[64,64,128]{2,1,0:T(8,128)(2,1)S(1)} %all-to-all-done), channel_id=1, source_target_pairs={{0,16},{16,0},{1,17},{17,1},{2,18},{18,2},{3,19},{19,3},{4,20},{20... | collective-permute-start | bytes 3145736 | tf_op jit(solution)/shard_map/ppermute | solution.py:367
  33.6 4.1 %collective-permute-start.3 = (bf16[66,256]{1,0:T(8,128)(2,1)S(1)}, bf16[66,256]{1,0:T(8,128)(2,1)S(1)}, u32[]{:S(2)}, u32[]{:S(2)}) collective-permute-start(bf16[66,256]{1,0:T(8,128)(2,1)S(1)} %pad_maximum_fusion), channel_id=1, source_target_pairs={{0,1},{1,2},{2,3},{3,4},{4,5},{5,6},{6,7},{7,8},{8,9},{9,10},{10,1... | collective-permute-start | bytes 101384 | tf_op jit(solution)/shard_map/ppermute | solution.py:340
  37.7 1.9 %collective-permute-start.4 = (bf16[66,256]{1,0:T(8,128)(2,1)S(1)}, bf16[66,256]{1,0:T(8,128)(2,1)S(1)}, u32[]{:S(2)}, u32[]{:S(2)}) collective-permute-start(bf16[66,256]{1,0:T(8,128)(2,1)S(1)} %pad_maximum_fusion.1), channel_id=1, source_target_pairs={{1,0},{2,1},{3,2},{4,3},{5,4},{6,5},{7,6},{8,7},{9,8},{10,9},{11,1... | collective-permute-start | bytes 101384 | tf_op jit(solution)/shard_map/ppermute | solution.py:341
  39.7 4.8 %collective-permute-done.4 = bf16[66,256]{1,0:T(8,128)(2,1)S(1)} collective-permute-done((bf16[66,256]{1,0:T(8,128)(2,1)S(1)}, bf16[66,256]{1,0:T(8,128)(2,1)S(1)}, u32[]{:S(2)}, u32[]{:S(2)}) %collective-permute-start.4) | collective-permute-done | bytes 33824 | tf_op jit(solution)/shard_map/ppermute | solution.py:341
  44.6 0.3 slice.96
  44.9 0.1 dynamic-slice_convert_fusion
  45.1 0.3 slice.98
  45.4 0.2 fusion.4
  45.6 0.1 fusion.3
  45.8 2.1 %select_reduce_fusion = s32[16,256]{1,0:T(8,128)S(1)} fusion(s32[16,128]{1,0:T(8,128)S(1)} %copy.48, s32[16,128]{1,0:T(8,128)S(1)} %copy.47, s32[16,256]{1,0:T(8,128)S(1)} %fusion.8, pred[16,256]{1,0:T(8,128)(4,1)S(1)} %fusion.11), kind=kLoop, calls=%fused_computation | loop fusion | flops 2093056 | bytes 53248 | tf_op jit(solution)/shard_map/reduce_sum | solution.py:155
  47.9 11.4 %shard_map.110 = bf16[8192,128]{1,0:T(8,128)(2,1)S(1)} custom-call(s32[4096]{0:T(1024)S(1)} %add_select_fusion.6.index_ref, bf16[4096,128]{1,0:T(8,128)(2,1)S(1)} %bitcast.85, bf16[4096,128]{1,0:T(8,128)(2,1)S(1)} %bitcast.88, bf16[8,128,128]{2,1,0:T(8,128)(2,1)S(1)} %copy-done.7), custom_call_target="tpu_custom_call" | custom-call | tf_op jit(solution)/shard_map/pallas_call | solution.py:119
  59.3 1.3 copy-done.3
  60.6 6.5 %all-to-all-start.1 = ((bf16[16,512,128]{2,1,0:T(8,128)(2,1)}), bf16[16,512,128]{2,1,0:T(8,128)(2,1)S(1)}, u32[]{:S(2)}, u32[]{:S(2)}) async-start(bf16[16,512,128]{2,1,0:T(8,128)(2,1)} %bitcast.83), calls=%async_computation.1 | async-start | bytes 4194304 | tf_op jit(solution)/shard_map/all_to_all | solution.py:372
  67.1 0.8 pad.13
  67.9 0.7 reshape.181
  68.6 0.9 pad_bitcast_fusion.lift_ref
  69.5 2.2 %copy-done.1 = bf16[64,128,256]{2,1,0:T(8,128)(2,1)S(1)} copy-done((bf16[64,128,256]{2,1,0:T(8,128)(2,1)S(1)}, bf16[64,128,256]{2,1,0:T(8,128)(2,1)}, u32[]{:S(2)}) %copy-start.1) | copy-done | bytes 4194328
  71.7 0.8 copy-done.10
  72.5 14.3 %shard_map.111.conv_ref = f32[64,128,256]{2,1,0:T(8,128)} custom-call(bf16[64,128,256]{2,1,0:T(8,128)(2,1)S(1)} %copy-done.1, bf16[1,128,256]{2,1,0:T(8,128)(2,1)S(1)} %copy-done.10, bf16[1,128,256]{2,1,0:T(8,128)(2,1)S(1)} %collective-permute-done.2.bottom_ref, f32[66,1,256]{2,1,0:T(1,128)S(1)} %reshape.187.left_ref, f32[66,1,256]{2,1,0:T(1,128)S(1)} %reshape.188.right_ref, ...), custom_call_target="tpu_custom_call" | custom-call | tf_op jit(solution)/shard_map/pallas_call | solution.py:215
  86.8 4.3 %all-to-all-done.1.blended_ref = bf16[16,512,128]{2,1,0:T(8,128)(2,1)S(1)} async-done(((bf16[16,512,128]{2,1,0:T(8,128)(2,1)}), bf16[16,512,128]{2,1,0:T(8,128)(2,1)S(1)}, u32[]{:S(2)}, u32[]{:S(2)}) %all-to-all-start.1) | async-done | bytes 2097184 | tf_op jit(solution)/shard_map/all_to_all | solution.py:372
  91.1 3.4 %copy-done = f32[64,128,256]{2,1,0:T(8,128)S(1)} copy-done((f32[64,128,256]{2,1,0:T(8,128)S(1)}, f32[64,128,256]{2,1,0:T(8,128)}, u32[]{:S(2)}) %copy-start) | copy-done | bytes 8388632
  94.4 2.2 %copy-done.2 = bf16[64,128,256]{2,1,0:T(8,128)(2,1)S(1)} copy-done((bf16[64,128,256]{2,1,0:T(8,128)(2,1)S(1)}, bf16[64,128,256]{2,1,0:T(8,128)(2,1)}, u32[]{:S(2)}) %copy-start.2) | copy-done | bytes 4194328
  96.6 13.1 %shard_map.112 = (bf16[64,128,256]{2,1,0:T(8,128)(2,1)S(1)}, bf16[32,64,256]{2,1,0:T(8,128)(2,1)S(1)}) custom-call(bf16[16,512,128]{2,1,0:T(8,128)(2,1)S(1)} %all-to-all-done.1.blended_ref, bf16[128,256]{1,0:T(8,128)(2,1)S(1)} %pad_bitcast_fusion.lift_ref, f32[64,128,256]{2,1,0:T(8,128)S(1)} %copy-done, bf16[64,128,256]{2,1,0:T(8,128)(2,1)S(1)} %copy-done.2), custom_call_target="tpu_custom_call" | custom-call | tf_op jit(solution)/shard_map/pallas_call | solution.py:257
  109.8 2.0 %copy-done.4 = bf16[64,128,256]{2,1,0:T(8,128)(2,1)} copy-done((bf16[64,128,256]{2,1,0:T(8,128)(2,1)}, bf16[64,128,256]{2,1,0:T(8,128)(2,1)S(1)}, u32[]{:S(2)}) %copy-start.4) | copy-done | bytes 4194328
  111.7 0.6 copy.51
  112.3 5.4 %collective-permute-start.6 = (bf16[1,64,256]{2,1,0:T(8,128)(2,1)S(1)}, bf16[1,64,256]{2,1,0:T(8,128)(2,1)S(1)}, u32[]{:S(2)}, u32[]{:S(2)}) collective-permute-start(bf16[1,64,256]{2,1,0:T(8,128)(2,1)S(1)} %get-tuple-element.25), channel_id=1, source_target_pairs={{16,0},{32,16},{48,32},{64,48},{80,64},{96,80},{112,96},{17,1},{33... | collective-permute-start | bytes 98312 | tf_op jit(solution)/shard_map/ppermute | solution.py:335
  117.7 1.9 %collective-permute-start.5 = (bf16[1,64,256]{2,1,0:T(8,128)(2,1)S(1)}, bf16[1,64,256]{2,1,0:T(8,128)(2,1)S(1)}, u32[]{:S(2)}, u32[]{:S(2)}) collective-permute-start(bf16[1,64,256]{2,1,0:T(8,128)(2,1)S(1)} %get-tuple-element.26), channel_id=1, source_target_pairs={{0,16},{16,32},{32,48},{48,64},{64,80},{80,96},{96,112},{1,17},{17... | collective-permute-start | bytes 98312 | tf_op jit(solution)/shard_map/ppermute | solution.py:334
  119.7 1.1 collective-permute-done.5.top_ref
  120.9 4.4 %collective-permute-start.7 = (bf16[34,256]{1,0:T(8,128)(2,1)S(1)}, bf16[34,256]{1,0:T(8,128)(2,1)S(1)}, u32[]{:S(2)}, u32[]{:S(2)}) collective-permute-start(bf16[34,256]{1,0:T(8,128)(2,1)S(1)} %pad_maximum_fusion.2), channel_id=1, source_target_pairs={{0,1},{1,2},{2,3},{3,4},{4,5},{5,6},{6,7},{7,8},{8,9},{9,10},{10,1... | collective-permute-start | bytes 52232 | tf_op jit(solution)/shard_map/ppermute | solution.py:340
  125.3 1.9 %collective-permute-start.8 = (bf16[34,256]{1,0:T(8,128)(2,1)S(1)}, bf16[34,256]{1,0:T(8,128)(2,1)S(1)}, u32[]{:S(2)}, u32[]{:S(2)}) collective-permute-start(bf16[34,256]{1,0:T(8,128)(2,1)S(1)} %pad_maximum_fusion.3), channel_id=1, source_target_pairs={{1,0},{2,1},{3,2},{4,3},{5,4},{6,5},{7,6},{8,7},{9,8},{10,9},{11,1... | collective-permute-start | bytes 52232 | tf_op jit(solution)/shard_map/ppermute | solution.py:341
  127.2 4.7 %collective-permute-done.8 = bf16[34,256]{1,0:T(8,128)(2,1)S(1)} collective-permute-done((bf16[34,256]{1,0:T(8,128)(2,1)S(1)}, bf16[34,256]{1,0:T(8,128)(2,1)S(1)}, u32[]{:S(2)}, u32[]{:S(2)}) %collective-permute-start.8) | collective-permute-done | bytes 17440 | tf_op jit(solution)/shard_map/ppermute | solution.py:341
  132.0 9.8 %shard_map.113 = bf16[64,128,256]{2,1,0:T(8,128)(2,1)} custom-call(bf16[32,64,256]{2,1,0:T(8,128)(2,1)S(1)} %get-tuple-element.17.pooled_ref, bf16[1,64,256]{2,1,0:T(8,128)(2,1)S(1)} %collective-permute-done.5.top_ref, bf16[1,64,256]{2,1,0:T(8,128)(2,1)S(1)} %collective-permute-done.6.bottom_ref, f32[34,1,256]{2,1,0:T(1,128)S(1)} %reshape.189.left_ref, ...), custom_call_target="tpu_custom_call" | custom-call | tf_op jit(solution)/shard_map/pallas_call | solution.py:305
  (52 shorter events, 0.9 us)
Async XLA Ops:
  6.6 25.0 %all-to-all-start = ((bf16[64,64,128]{2,1,0:T(8,128)(2,1)}), bf16[64,64,128]{2,1,0:T(8,128)(2,1)S(1)}, u32[]{:S(2)}, u32[]{:S(2)}) async-start(bf16[64,64,128]{2,1,0:T(8,128)(2,1)} %bitcast.3), calls=%async_computation | async-start | bytes 2097152 | tf_op jit(solution)/shard_map/all_to_all | solution.py:366
  17.1 30.8 %copy-start.7 = (bf16[8,128,128]{2,1,0:T(8,128)(2,1)S(1)}, bf16[8,128,128]{2,1,0:T(8,128)(2,1)}, u32[]{:S(2)}) copy-start(bf16[8,128,128]{2,1,0:T(8,128)(2,1)} %weights_ref.1) | copy-start | bytes 786436
  18.1 8.7 %collective-permute-start.2 = (bf16[1,128,256]{2,1,0:T(8,128)(2,1)S(1)}, bf16[1,128,256]{2,1,0:T(8,128)(2,1)S(1)}, u32[]{:S(2)}, u32[]{:S(2)}) collective-permute-start(bf16[1,128,256]{2,1,0:T(8,128)(2,1)S(1)} %get-tuple-element.21), channel_id=1, source_target_pairs={{16,0},{32,16},{48,32},{64,48},{80,64},{96,80},{112,96},{17,1},{33... | collective-permute-start | bytes 196616 | tf_op jit(solution)/shard_map/ppermute | solution.py:335
  21.2 8.6 %collective-permute-start.1 = (bf16[1,128,256]{2,1,0:T(8,128)(2,1)S(1)}, bf16[1,128,256]{2,1,0:T(8,128)(2,1)S(1)}, u32[]{:S(2)}, u32[]{:S(2)}) collective-permute-start(bf16[1,128,256]{2,1,0:T(8,128)(2,1)S(1)} %get-tuple-element.22), channel_id=1, source_target_pairs={{0,16},{16,32},{32,48},{48,64},{64,80},{80,96},{96,112},{1,17},{17... | collective-permute-start | bytes 196616 | tf_op jit(solution)/shard_map/ppermute | solution.py:334
  29.9 0.6 copy-start.9
  31.6 13.5 %collective-permute-start = (bf16[64,64,128]{2,1,0:T(8,128)(2,1)S(1)}, bf16[64,64,128]{2,1,0:T(8,128)(2,1)S(1)}, u32[]{:S(2)}, u32[]{:S(2)}) collective-permute-start(bf16[64,64,128]{2,1,0:T(8,128)(2,1)S(1)} %all-to-all-done), channel_id=1, source_target_pairs={{0,16},{16,0},{1,17},{17,1},{2,18},{18,2},{3,19},{19,3},{4,20},{20... | collective-permute-start | bytes 3145736 | tf_op jit(solution)/shard_map/ppermute | solution.py:367
  33.6 6.1 %collective-permute-start.3 = (bf16[66,256]{1,0:T(8,128)(2,1)S(1)}, bf16[66,256]{1,0:T(8,128)(2,1)S(1)}, u32[]{:S(2)}, u32[]{:S(2)}) collective-permute-start(bf16[66,256]{1,0:T(8,128)(2,1)S(1)} %pad_maximum_fusion), channel_id=1, source_target_pairs={{0,1},{1,2},{2,3},{3,4},{4,5},{5,6},{6,7},{7,8},{8,9},{9,10},{10,1... | collective-permute-start | bytes 101384 | tf_op jit(solution)/shard_map/ppermute | solution.py:340
  37.7 6.8 %collective-permute-start.4 = (bf16[66,256]{1,0:T(8,128)(2,1)S(1)}, bf16[66,256]{1,0:T(8,128)(2,1)S(1)}, u32[]{:S(2)}, u32[]{:S(2)}) collective-permute-start(bf16[66,256]{1,0:T(8,128)(2,1)S(1)} %pad_maximum_fusion.1), channel_id=1, source_target_pairs={{1,0},{2,1},{3,2},{4,3},{5,4},{6,5},{7,6},{8,7},{9,8},{10,9},{11,1... | collective-permute-start | bytes 101384 | tf_op jit(solution)/shard_map/ppermute | solution.py:341
  59.3 1.3 copy-start.3
  60.6 8.8 %copy-start.6 = (bf16[3,3,256,256]{3,2,1,0:T(8,128)(2,1)S(1)}, bf16[3,3,256,256]{3,2,1,0:T(8,128)(2,1)}, u32[]{:S(2)}) copy-start(bf16[3,3,256,256]{3,2,1,0:T(8,128)(2,1)} %param.19) | copy-start | bytes 3538948
  60.6 30.4 %all-to-all-start.1 = ((bf16[16,512,128]{2,1,0:T(8,128)(2,1)}), bf16[16,512,128]{2,1,0:T(8,128)(2,1)S(1)}, u32[]{:S(2)}, u32[]{:S(2)}) async-start(bf16[16,512,128]{2,1,0:T(8,128)(2,1)} %bitcast.83), calls=%async_computation.1 | async-start | bytes 4194304 | tf_op jit(solution)/shard_map/all_to_all | solution.py:372
  69.5 2.2 %copy-start.1 = (bf16[64,128,256]{2,1,0:T(8,128)(2,1)S(1)}, bf16[64,128,256]{2,1,0:T(8,128)(2,1)}, u32[]{:S(2)}) copy-start(bf16[64,128,256]{2,1,0:T(8,128)(2,1)} %cells_ref.3) | copy-start | bytes 12582916
  71.6 0.8 copy-start.10
  91.1 3.4 %copy-start = (f32[64,128,256]{2,1,0:T(8,128)S(1)}, f32[64,128,256]{2,1,0:T(8,128)}, u32[]{:S(2)}) copy-start(f32[64,128,256]{2,1,0:T(8,128)} %shard_map.111.conv_ref) | copy-start | bytes 25165828
  94.4 2.2 %copy-start.2 = (bf16[64,128,256]{2,1,0:T(8,128)(2,1)S(1)}, bf16[64,128,256]{2,1,0:T(8,128)(2,1)}, u32[]{:S(2)}) copy-start(bf16[64,128,256]{2,1,0:T(8,128)(2,1)} %cells_ref.3) | copy-start | bytes 12582916
  96.6 35.3 %copy-start.8 = (bf16[512,256]{1,0:T(8,128)(2,1)S(1)}, bf16[512,256]{1,0:T(8,128)(2,1)}, u32[]{:S(2)}) copy-start(bf16[512,256]{1,0:T(8,128)(2,1)} %up_ref.1) | copy-start | bytes 786436
  109.8 2.0 %copy-start.4 = (bf16[64,128,256]{2,1,0:T(8,128)(2,1)}, bf16[64,128,256]{2,1,0:T(8,128)(2,1)S(1)}, u32[]{:S(2)}) copy-start(bf16[64,128,256]{2,1,0:T(8,128)(2,1)S(1)} %get-tuple-element.18.first_ref) | copy-start | bytes 12582916
  111.7 20.2 %copy-start.5 = (bf16[3,3,256,512]{3,2,1,0:T(8,128)(2,1)S(1)}, bf16[3,3,256,512]{3,2,1,0:T(8,128)(2,1)}, u32[]{:S(2)}) copy-start(bf16[3,3,256,512]{3,2,1,0:T(8,128)(2,1)} %param.20) | copy-start | bytes 7077892
  112.3 7.4 %collective-permute-start.6 = (bf16[1,64,256]{2,1,0:T(8,128)(2,1)S(1)}, bf16[1,64,256]{2,1,0:T(8,128)(2,1)S(1)}, u32[]{:S(2)}, u32[]{:S(2)}) collective-permute-start(bf16[1,64,256]{2,1,0:T(8,128)(2,1)S(1)} %get-tuple-element.25), channel_id=1, source_target_pairs={{16,0},{32,16},{48,32},{64,48},{80,64},{96,80},{112,96},{17,1},{33... | collective-permute-start | bytes 98312 | tf_op jit(solution)/shard_map/ppermute | solution.py:335
  117.7 3.1 %collective-permute-start.5 = (bf16[1,64,256]{2,1,0:T(8,128)(2,1)S(1)}, bf16[1,64,256]{2,1,0:T(8,128)(2,1)S(1)}, u32[]{:S(2)}, u32[]{:S(2)}) collective-permute-start(bf16[1,64,256]{2,1,0:T(8,128)(2,1)S(1)} %get-tuple-element.26), channel_id=1, source_target_pairs={{0,16},{16,32},{32,48},{48,64},{64,80},{80,96},{96,112},{1,17},{17... | collective-permute-start | bytes 98312 | tf_op jit(solution)/shard_map/ppermute | solution.py:334
  120.9 6.3 %collective-permute-start.7 = (bf16[34,256]{1,0:T(8,128)(2,1)S(1)}, bf16[34,256]{1,0:T(8,128)(2,1)S(1)}, u32[]{:S(2)}, u32[]{:S(2)}) collective-permute-start(bf16[34,256]{1,0:T(8,128)(2,1)S(1)} %pad_maximum_fusion.2), channel_id=1, source_target_pairs={{0,1},{1,2},{2,3},{3,4},{4,5},{5,6},{6,7},{7,8},{8,9},{9,10},{10,1... | collective-permute-start | bytes 52232 | tf_op jit(solution)/shard_map/ppermute | solution.py:340
  125.3 6.6 %collective-permute-start.8 = (bf16[34,256]{1,0:T(8,128)(2,1)S(1)}, bf16[34,256]{1,0:T(8,128)(2,1)S(1)}, u32[]{:S(2)}, u32[]{:S(2)}) collective-permute-start(bf16[34,256]{1,0:T(8,128)(2,1)S(1)} %pad_maximum_fusion.3), channel_id=1, source_target_pairs={{1,0},{2,1},{3,2},{4,3},{5,4},{6,5},{7,6},{8,7},{9,8},{10,9},{11,1... | collective-permute-start | bytes 52232 | tf_op jit(solution)/shard_map/ppermute | solution.py:341

commit v2 on v1

--- a/solution.py
+++ b/solution.py
@@ -125,7 +125,7 @@
             pl.BlockSpec(memory_space=pltpu.VMEM),
         ],
         out_specs=pl.BlockSpec(memory_space=pltpu.VMEM),
-        out_shape=jax.ShapeDtypeStruct((PX * SUBTILES * SLOT, CELLS), BF16),
+        out_shape=pltpu.HBM((PX * SUBTILES * SLOT, CELLS), BF16),
         scratch_shapes=[pltpu.VMEM((ZERO_TILE + 1, SLOT, CELLS), F32)],
         compiler_params=pltpu.CompilerParams(vmem_limit_bytes=42 * MIB),
     )(index, own, other, weights)
@@ -204,7 +204,12 @@
     def _():
         fill_all(taps_ref, cells_ref, top_ref, bottom_ref, left_ref, right_ref)
 
-    out_ref[...] = taps_dot(taps_ref, weights_ref, step * STRIP, STRIP).reshape(STRIP, COLUMNS, FINE)
+    total = taps_dot(taps_ref, weights_ref, step * STRIP, STRIP)
+    out_ref[...] = total.reshape(STRIP, COLUMNS, FINE).astype(BF16)
+
+
+def in_hbm(array):
+    return pltpu.with_memory_space_constraint(array, pltpu.HBM)
 
 
 def whole(*shape):
@@ -224,10 +229,14 @@
             whole(3, 3 * FINE, FINE),
         ],
         out_specs=pl.BlockSpec((STRIP, COLUMNS, FINE), lambda i: (i, 0, 0)),
-        out_shape=jax.ShapeDtypeStruct((ROWS, COLUMNS, FINE), F32),
+        out_shape=pltpu.HBM((ROWS, COLUMNS, FINE), BF16),
         scratch_shapes=[pltpu.VMEM((ROWS + 2, COLUMNS, 3 * FINE), BF16)],
         compiler_params=pltpu.CompilerParams(vmem_limit_bytes=48 * MIB),
-    )(cells, *halo, weights)
+    )(in_hbm(cells), *halo, weights)
+
+
+STRIPS = 2
+ROW_TILES = COLUMNS // SUBTILE_COLUMNS
 
 
 def first_kernel(blended_ref, lift_ref, conv_ref, cells_ref, first_ref, pooled_ref):
@@ -236,40 +245,48 @@
     row = cell // SUBTILE_COLUMNS
     column = cell % SUBTILE_COLUMNS
     pool = jnp.where((row // 2) * 8 + column // 2 == target, 0.25, 0.0).astype(BF16)
-    for pair in range(COLUMNS // SUBTILE_COLUMNS // 2):
-        both = blended_ref[:, pair * 2 * SLOT : (pair + 1) * 2 * SLOT, :].astype(F32)
-        for half in range(2):
-            tile = 2 * pair + half
+    for strip in range(STRIPS):
+        parts = []
+        for pair in range(ROW_TILES // 2):
+            start = (strip * ROW_TILES + 2 * pair) * SLOT
+            both = blended_ref[:, start : start + 2 * SLOT, :].astype(F32)
+            for half in range(2):
+                part = both[:, half * SLOT : (half + 1) * SLOT, :]
+                parts.append(part.reshape(PX * SLOT, CELLS).astype(BF16))
+        lifted = lax.dot_general(
+            jnp.concatenate(parts, axis=1), lift_ref[...], (((0,), (0,)), ((), ())), preferred_element_type=F32
+        )
+        rows = slice(strip * STRIP, (strip + 1) * STRIP)
+        half_rows = slice(strip * STRIP // 2, (strip + 1) * STRIP // 2)
+        for tile in range(ROW_TILES):
             columns = slice(tile * SUBTILE_COLUMNS, (tile + 1) * SUBTILE_COLUMNS)
-            part = both[:, half * SLOT : (half + 1) * SLOT, :].reshape(PX * SLOT, CELLS).astype(BF16)
-            guidance = lax.dot_general(
-                part, lift_ref[...], (((0,), (0,)), ((), ())), preferred_element_type=F32
-            ).astype(BF16)
-            summed = conv_ref[:, columns, :].reshape(CELLS, FINE) + guidance.astype(F32)
-            kept = cells_ref[:, columns, :].reshape(CELLS, FINE).astype(F32)
+            guidance = lifted[tile * CELLS : (tile + 1) * CELLS].astype(BF16).astype(F32)
+            summed = conv_ref[rows, columns, :].astype(F32).reshape(CELLS, FINE) + guidance
+            kept = cells_ref[rows, columns, :].reshape(CELLS, FINE).astype(F32)
             first = (kept + silu(summed)).astype(BF16)
-            first_ref[:, columns, :] = first.reshape(SUBTILE_ROWS, SUBTILE_COLUMNS, FINE)
-            pooled_ref[:, tile * 8 : (tile + 1) * 8, :] = dot(pool, first).reshape(4, 8, FINE).astype(BF16)
+            first_ref[rows, columns, :] = first.reshape(SUBTILE_ROWS, SUBTILE_COLUMNS, FINE)
+            pooled = dot(pool, first).reshape(STRIP // 2, 8, FINE).astype(BF16)
+            pooled_ref[half_rows, tile * 8 : (tile + 1) * 8, :] = pooled
 
 
 def first_level(blended, lift, conv, cells):
-    strip = pl.BlockSpec((STRIP, COLUMNS, FINE), lambda i: (i, 0, 0))
+    strip = pl.BlockSpec((STRIPS * STRIP, COLUMNS, FINE), lambda i: (i, 0, 0))
     return pl.pallas_call(
         first_kernel,
-        grid=(ROWS // STRIP,),
+        grid=(ROWS // (STRIPS * STRIP),),
         in_specs=[
-            pl.BlockSpec((PX, 8 * SLOT, CELLS), lambda i: (0, i, 0)),
+            pl.BlockSpec((PX, STRIPS * ROW_TILES * SLOT, CELLS), lambda i: (0, i, 0)),
             whole(PX * SLOT, FINE),
             strip,
             strip,
         ],
-        out_specs=[strip, pl.BlockSpec((STRIP // 2, COLUMNS // 2, FINE), lambda i: (i, 0, 0))],
+        out_specs=[strip, pl.BlockSpec((STRIPS * STRIP // 2, COLUMNS // 2, FINE), lambda i: (i, 0, 0))],
         out_shape=[
-            jax.ShapeDtypeStruct((ROWS, COLUMNS, FINE), BF16),
+            pltpu.HBM((ROWS, COLUMNS, FINE), BF16),
             jax.ShapeDtypeStruct((ROWS // 2, COLUMNS // 2, FINE), BF16),
         ],
         compiler_params=pltpu.CompilerParams(vmem_limit_bytes=32 * MIB),
-    )(blended, lift, conv, cells)
+    )(blended, lift, in_hbm(conv), in_hbm(cells))
 
 
 SECOND = 8
@@ -322,24 +339,25 @@
             pltpu.VMEM((FINE // 128, SECOND * COLUMNS, 128), F32),
         ],
         compiler_params=pltpu.CompilerParams(vmem_limit_bytes=48 * MIB),
-    )(pooled, *halo, weights, up, first)
+    )(pooled, *halo, weights, up, in_hbm(first))
 
 
 ROWS_AXES = ("z", "core")
 
 
-def halo_of(cells):
+def halo_rows(cells):
     down = [(i, i + 1) for i in range(PY - 1)]
     up = [(i + 1, i) for i in range(PY - 1)]
-    top = lax.ppermute(cells[-1:], ROWS_AXES, down)
-    bottom = lax.ppermute(cells[:1], ROWS_AXES, up)
-
+    return lax.ppermute(cells[-1:], ROWS_AXES, down), lax.ppermute(cells[:1], ROWS_AXES, up)
+
+
+def halo_columns(cells, top, bottom):
     def column(at):
         return jnp.concatenate([top[:, at], cells[:, at], bottom[:, at]], axis=0)
 
     left = lax.ppermute(column(-1), "px", [(i, i + 1) for i in range(PX - 1)])
     right = lax.ppermute(column(0), "px", [(i + 1, i) for i in range(PX - 1)])
-    return top, bottom, left[:, None].astype(F32), right[:, None].astype(F32)
+    return left[:, None].astype(F32), right[:, None].astype(F32)
 
 
 def local(
@@ -355,7 +373,7 @@
     conv_b,
     up_weight,
 ):
-    edges = halo_of(features)
+    above, below = halo_rows(features)
     ids = send_ids[0].reshape(Z, CORES, PX, 2).transpose(0, 1, 3, 2).reshape(Z, CORES, 2 * PX)
     sent = jnp.concatenate([ids, send_counts[0].reshape(Z, CORES, PX)], axis=2).reshape(Z, 1, CORES * 3 * PX)
     sent = jnp.pad(sent, ((0, 0), (0, 0), (0, CELLS - CORES * 3 * PX)))
@@ -366,17 +384,20 @@
     own = lax.all_to_all(outgoing, ("z", "px"), split_axis=0, concat_axis=0, tiled=True)
     other = lax.ppermute(own, "core", [(0, 1), (1, 0)])
     index = entry_index(own, other)
-    index, edges = lax.optimization_barrier((index, edges))
+    index, above, below = lax.optimization_barrier((index, above, below))
     half = (NEAR * OWNED * SLOT, CELLS)
     parts = blend(index, own.reshape(half), other.reshape(half), interpolation_weights)
     blended = lax.all_to_all(
         parts.reshape(PX, SUBTILES * SLOT, CELLS), "px", split_axis=0, concat_axis=0, tiled=True
     )
+    edges = (above, below, *halo_columns(features, above, below))
     conv = conv_fine(features, edges, conv_a.reshape(3, 3 * FINE, FINE))
     lift = jnp.pad(lift_weight, ((0, PX * PART - CHANNELS), (0, 0))).reshape(PX, PART, FINE)
     lift = jnp.pad(lift, ((0, 0), (0, SLOT - PART), (0, 0))).reshape(PX * SLOT, FINE)
     first, pooled = first_level(blended, lift, conv, features)
-    return second_level(pooled, halo_of(pooled), conv_b.reshape(3, 3 * FINE, WIDE), up_weight, first)
+    above, below = halo_rows(pooled)
+    edges = (above, below, *halo_columns(pooled, above, below))
+    return second_level(pooled, edges, conv_b.reshape(3, 3 * FINE, WIDE), up_weight, first)
 
 
 def solution(mesh):

time: 144 us -> 144 us (level)
  blocking collectives: 0 us -> 24.8 us
  local copies, waits for them, and re-layouts: 20.9 us -> 6.15 us
  starting transfers between devices: 44.9 us -> 31.2 us
  waiting for transfers between devices: 20.4 us -> 26.9 us
  Pallas kernels: 50.3 us -> 47.2 us
    all_to_all x0 -> x1, blocking collectives: none -> 24.8 us  [local(): lax.all_to_all(outgoing, ('z', 'px'), split_axis=0, concat_axis=0, tiled=...]
    unnamed x28 -> x16, local copies, waits for them, and re-layouts: 14 us -> 1.55 us
    ppermute x8, waiting for transfers between devices: 15 us -> 26.8 us  [the longest x2 18 us: halo_columns(): left = lax.ppermute(column(-1), 'px', [(i, i + 1) for i in range(PX - 1)])]
    all_to_all x1 -> x0, starting transfers between devices: 10.6 us -> none  [local(): lax.all_to_all(outgoing, ('z', 'px'), split_axis=0, concat_axis=0, tiled=...]
    pallas_call x1, Pallas kernels: 13.1 us -> 8.1 us  [first_level(): pl.pallas_call(first_kernel, grid=(ROWS // (STRIPS * STRIP),), in_specs=[...]
    all_to_all x1, waiting for transfers between devices: 4.29 us -> 0.01 us  [local(): lax.all_to_all(parts.reshape(PX, SUBTILES * SLOT, CELLS), 'px', split_axi...]
    ppermute x8, starting transfers between devices: 25.9 us -> 21.8 us  [the longest x2 7.25 us: halo_rows(): lax.ppermute(cells[-1:], ROWS_AXES, down)]
    pallas_call x1, Pallas kernels: 14.3 us -> 16.2 us  [conv_fine(): pl.pallas_call(conv_kernel, grid=(ROWS // STRIP,), in_specs=[whole(ROWS,...]
  transfers between devices with their start and end apart: 11 -> 10, of which waited for: 7 -> 4; matrix products, arithmetic and copies ran while one was open for 4% -> 4% of each run, Pallas kernels for 10% -> 11%
where the time goes in v2:
time: 144 us; the launch traced here: 141 us
  Pallas kernels  47.2 us (33%)
  starting transfers between devices  31.2 us (22%)
  waiting for transfers between devices  26.9 us (19%)
  blocking collectives  24.8 us (17%)
  local copies, waits for them, and re-layouts  6.15 us (4%)
  other arithmetic  4.78 us (3%)
    all_to_all x1, blocking collectives, local(): lax.all_to_all(outgoing, ('z', 'px'), split_axis=0, concat_axis=0, tiled=...  24.8 us
    ppermute x2, waiting for transfers between devices, halo_columns(): left = lax.ppermute(column(-1), 'px', [(i, i + 1) for i in range(PX - 1)])  18 us
    pallas_call x1, Pallas kernels, conv_fine(): pl.pallas_call(conv_kernel, grid=(ROWS // STRIP,), in_specs=[whole(ROWS,...  16.2 us
    pallas_call x1, Pallas kernels, blend(): pl.pallas_call(blend_kernel, in_specs=[pl.BlockSpec(memory_space=pltpu.SM...  12.7 us
    pallas_call x1, Pallas kernels, second_level(): pl.pallas_call(second_kernel, grid=(ROWS // 2 // SECOND,), in_specs=[whol...  9.78 us
    pallas_call x1, Pallas kernels, first_level(): pl.pallas_call(first_kernel, grid=(ROWS // (STRIPS * STRIP),), in_specs=[...  8.1 us
    ppermute x2, waiting for transfers between devices, halo_columns(): right = lax.ppermute(column(0), 'px', [(i + 1, i) for i in range(PX - 1)])  7.86 us
    all_to_all x1, starting transfers between devices, local(): lax.all_to_all(parts.reshape(PX, SUBTILES * SLOT, CELLS), 'px', split_axi...  7.42 us
  transfers between devices with their start and end apart: 10, of which 4 were waited for; matrix products, arithmetic and copies ran while one was open for 4% of the time, Pallas kernels for 11%

profile of v2, /device:TPU:29, one launch (start us, length us, event | category | flops | bytes accessed | tf_op | source)
XLA Modules:
  0.0 141.4 jit_solution(1433554832418788753)
XLA Ops:
  0.0 0.1 pad.31.clone
  0.1 0.5 broadcast.221
  0.6 1.3 reduce.3
  1.9 0.1 reshape_squeeze.15
  2.0 0.8 reshape_squeeze.14
  2.8 0.1 reshape.172
  2.9 0.1 pad_add_fusion.1
  2.9 0.1 reshape.173
  3.0 1.0 copy.46.coarse_ref
  4.0 0.7 pad_add_fusion.2
  4.7 0.1 fusion.14.tables_ref
  4.8 0.4 shard_map.109
  5.2 24.8 %all_to_all.10 = bf16[64,64,128]{2,1,0:T(8,128)(2,1)S(1)} all-to-all(bf16[64,64,128]{2,1,0:T(8,128)(2,1)S(1)} %bitcast.85), channel_id=1, replica_groups=mesh['z'=4,'core'=2,'px'=16] {'z','px'}, dimensions={0} | all-to-all | bytes 2097152 | tf_op jit(solution)/shard_map/all_to_all | solution.py:384
  30.0 2.0 %collective-permute-start = (bf16[64,64,128]{2,1,0:T(8,128)(2,1)S(1)}, bf16[64,64,128]{2,1,0:T(8,128)(2,1)S(1)}, u32[]{:S(2)}, u32[]{:S(2)}) collective-permute-start(bf16[64,64,128]{2,1,0:T(8,128)(2,1)S(1)} %all_to_all.10), channel_id=1, source_target_pairs={{0,16},{16,0},{1,17},{17,1},{2,18},{18,2},{3,19},{19,3},{4,20},{20... | collective-permute-start | bytes 3145736 | tf_op jit(solution)/shard_map/ppermute | solution.py:385
  32.0 0.9 fusion.20
  32.9 2.0 %collective-permute-start.2 = (bf16[1,128,256]{2,1,0:T(8,128)(2,1)S(1)}, bf16[1,128,256]{2,1,0:T(8,128)(2,1)S(1)}, u32[]{:S(2)}, u32[]{:S(2)}) collective-permute-start(bf16[1,128,256]{2,1,0:T(8,128)(2,1)S(1)} %get-tuple-element.17), channel_id=1, source_target_pairs={{16,0},{32,16},{48,32},{64,48},{80,64},{96,80},{112,96},{17,1},{33... | collective-permute-start | bytes 196616 | tf_op jit(solution)/shard_map/ppermute | solution.py:351
  34.8 3.6 %collective-permute-start.1 = (bf16[1,128,256]{2,1,0:T(8,128)(2,1)S(1)}, bf16[1,128,256]{2,1,0:T(8,128)(2,1)S(1)}, u32[]{:S(2)}, u32[]{:S(2)}) collective-permute-start(bf16[1,128,256]{2,1,0:T(8,128)(2,1)S(1)} %get-tuple-element.18), channel_id=1, source_target_pairs={{0,16},{16,32},{32,48},{48,64},{64,80},{80,96},{96,112},{1,17},{17... | collective-permute-start | bytes 196616 | tf_op jit(solution)/shard_map/ppermute | solution.py:351
  38.4 0.3 slice.96
  38.7 0.1 dynamic-slice_convert_fusion
  38.9 0.1 fusion.8
  38.9 0.0 collective-permute-done
  38.9 0.3 slice.98
  39.3 0.2 fusion.4
  39.4 0.1 fusion.3
  39.6 0.1 copy.47
  39.6 0.1 copy.48
  39.7 2.1 %select_reduce_fusion = s32[16,256]{1,0:T(8,128)S(1)} fusion(s32[16,128]{1,0:T(8,128)S(1)} %copy.48, s32[16,128]{1,0:T(8,128)S(1)} %copy.47, s32[16,256]{1,0:T(8,128)S(1)} %fusion.8, pred[16,256]{1,0:T(8,128)(4,1)S(1)} %fusion.11), kind=kLoop, calls=%fused_computation | loop fusion | flops 2093056 | bytes 53248 | tf_op jit(solution)/shard_map/reduce_sum | solution.py:155
  41.8 0.0 collective-permute-done.2.bottom_ref
  41.8 0.0 collective-permute-done.1.top_ref
  41.8 12.7 %shard_map.110 = bf16[8192,128]{1,0:T(8,128)(2,1)} custom-call(s32[4096]{0:T(1024)S(1)} %add_select_fusion.6.index_ref, bf16[4096,128]{1,0:T(8,128)(2,1)S(1)} %bitcast.84, bf16[4096,128]{1,0:T(8,128)(2,1)S(1)} %bitcast.88, bf16[8,128,128]{2,1,0:T(8,128)(2,1)S(1)} %copy-done.2), custom_call_target="tpu_custom_call" | custom-call | tf_op jit(solution)/shard_map/pallas_call | solution.py:119
  54.5 7.4 %all-to-all-start.1 = ((bf16[16,512,128]{2,1,0:T(8,128)(2,1)}), bf16[16,512,128]{2,1,0:T(8,128)(2,1)S(1)}, u32[]{:S(2)}, u32[]{:S(2)}) async-start(bf16[16,512,128]{2,1,0:T(8,128)(2,1)} %bitcast.90), calls=%async_computation.1 | async-start | bytes 4194304 | tf_op jit(solution)/shard_map/all_to_all | solution.py:390
  62.0 1.1 fusion.19
  63.2 2.8 %collective-permute-start.3 = (bf16[66,256]{1,0:T(8,128)(2,1)S(1)}, bf16[66,256]{1,0:T(8,128)(2,1)S(1)}, u32[]{:S(2)}, u32[]{:S(2)}) collective-permute-start(bf16[66,256]{1,0:T(8,128)(2,1)S(1)} %pad_maximum_fusion), channel_id=1, source_target_pairs={{0,1},{1,2},{2,3},{3,4},{4,5},{5,6},{6,7},{7,8},{8,9},{9,10},{10,1... | collective-permute-start | bytes 101384 | tf_op jit(solution)/shard_map/ppermute | solution.py:358
  66.1 2.5 %collective-permute-start.4 = (bf16[66,256]{1,0:T(8,128)(2,1)S(1)}, bf16[66,256]{1,0:T(8,128)(2,1)S(1)}, u32[]{:S(2)}, u32[]{:S(2)}) collective-permute-start(bf16[66,256]{1,0:T(8,128)(2,1)S(1)} %pad_maximum_fusion.1), channel_id=1, source_target_pairs={{1,0},{2,1},{3,2},{4,3},{5,4},{6,5},{7,6},{8,7},{9,8},{10,9},{11,1... | collective-permute-start | bytes 101384 | tf_op jit(solution)/shard_map/ppermute | solution.py:359
  68.6 18.0 %collective-permute-done.3 = bf16[66,256]{1,0:T(8,128)(2,1)S(1)} collective-permute-done((bf16[66,256]{1,0:T(8,128)(2,1)S(1)}, bf16[66,256]{1,0:T(8,128)(2,1)S(1)}, u32[]{:S(2)}, u32[]{:S(2)}) %collective-permute-start.3) | collective-permute-done | bytes 33824 | tf_op jit(solution)/shard_map/ppermute | solution.py:358
  86.6 4.3 %collective-permute-done.4 = bf16[66,256]{1,0:T(8,128)(2,1)S(1)} collective-permute-done((bf16[66,256]{1,0:T(8,128)(2,1)S(1)}, bf16[66,256]{1,0:T(8,128)(2,1)S(1)}, u32[]{:S(2)}, u32[]{:S(2)}) %collective-permute-start.4) | collective-permute-done | bytes 33824 | tf_op jit(solution)/shard_map/ppermute | solution.py:359
  91.0 16.2 %shard_map.111.conv_ref = bf16[64,128,256]{2,1,0:T(8,128)(2,1)} custom-call(bf16[64,128,256]{2,1,0:T(8,128)(2,1)} %cells_ref.3, bf16[1,128,256]{2,1,0:T(8,128)(2,1)S(1)} %collective-permute-done.1.top_ref, bf16[1,128,256]{2,1,0:T(8,128)(2,1)S(1)} %collective-permute-done.2.bottom_ref, f32[66,1,256]{2,1,0:T(1,128)S(1)} %reshape.187.left_ref, ...), custom_call_target="tpu_custom_call" | custom-call | tf_op jit(solution)/shard_map/pallas_call | solution.py:220
  107.2 0.0 all-to-all-done.1.blended_ref
  107.2 8.1 %shard_map.112 = (bf16[64,128,256]{2,1,0:T(8,128)(2,1)}, bf16[32,64,256]{2,1,0:T(8,128)(2,1)S(1)}) custom-call(bf16[16,512,128]{2,1,0:T(8,128)(2,1)S(1)} %all-to-all-done.1.blended_ref, bf16[128,256]{1,0:T(8,128)(2,1)S(1)} %pad_bitcast_fusion.lift_ref, bf16[64,128,256]{2,1,0:T(8,128)(2,1)} %shard_map.111.conv_ref, bf16[64,128,256]{2,1,0:T(8,128)(2,1)} %cells_ref.3), custom_call_target="tpu_custom_call" | custom-call | tf_op jit(solution)/shard_map/pallas_call | solution.py:274
  115.3 0.6 copy.51
  115.9 2.1 %collective-permute-start.6 = (bf16[1,64,256]{2,1,0:T(8,128)(2,1)S(1)}, bf16[1,64,256]{2,1,0:T(8,128)(2,1)S(1)}, u32[]{:S(2)}, u32[]{:S(2)}) collective-permute-start(bf16[1,64,256]{2,1,0:T(8,128)(2,1)S(1)} %get-tuple-element.21), channel_id=1, source_target_pairs={{16,0},{32,16},{48,32},{64,48},{80,64},{96,80},{112,96},{17,1},{33... | collective-permute-start | bytes 98312 | tf_op jit(solution)/shard_map/ppermute | solution.py:351
  118.0 3.6 %collective-permute-start.5 = (bf16[1,64,256]{2,1,0:T(8,128)(2,1)S(1)}, bf16[1,64,256]{2,1,0:T(8,128)(2,1)S(1)}, u32[]{:S(2)}, u32[]{:S(2)}) collective-permute-start(bf16[1,64,256]{2,1,0:T(8,128)(2,1)S(1)} %get-tuple-element.22), channel_id=1, source_target_pairs={{0,16},{16,32},{32,48},{48,64},{64,80},{80,96},{96,112},{1,17},{17... | collective-permute-start | bytes 98312 | tf_op jit(solution)/shard_map/ppermute | solution.py:351
  121.7 0.0 collective-permute-done.6.bottom_ref
  121.7 1.0 collective-permute-done.5.top_ref
  122.7 2.2 %collective-permute-start.7 = (bf16[34,256]{1,0:T(8,128)(2,1)S(1)}, bf16[34,256]{1,0:T(8,128)(2,1)S(1)}, u32[]{:S(2)}, u32[]{:S(2)}) collective-permute-start(bf16[34,256]{1,0:T(8,128)(2,1)S(1)} %pad_maximum_fusion.2), channel_id=1, source_target_pairs={{0,1},{1,2},{2,3},{3,4},{4,5},{5,6},{6,7},{7,8},{8,9},{9,10},{10,1... | collective-permute-start | bytes 52232 | tf_op jit(solution)/shard_map/ppermute | solution.py:358
  124.9 3.1 %collective-permute-start.8 = (bf16[34,256]{1,0:T(8,128)(2,1)S(1)}, bf16[34,256]{1,0:T(8,128)(2,1)S(1)}, u32[]{:S(2)}, u32[]{:S(2)}) collective-permute-start(bf16[34,256]{1,0:T(8,128)(2,1)S(1)} %pad_maximum_fusion.3), channel_id=1, source_target_pairs={{1,0},{2,1},{3,2},{4,3},{5,4},{6,5},{7,6},{8,7},{9,8},{10,9},{11,1... | collective-permute-start | bytes 52232 | tf_op jit(solution)/shard_map/ppermute | solution.py:359
  128.0 3.5 %collective-permute-done.8 = bf16[34,256]{1,0:T(8,128)(2,1)S(1)} collective-permute-done((bf16[34,256]{1,0:T(8,128)(2,1)S(1)}, bf16[34,256]{1,0:T(8,128)(2,1)S(1)}, u32[]{:S(2)}, u32[]{:S(2)}) %collective-permute-start.8) | collective-permute-done | bytes 17440 | tf_op jit(solution)/shard_map/ppermute | solution.py:359
  131.6 9.8 %shard_map.113 = bf16[64,128,256]{2,1,0:T(8,128)(2,1)} custom-call(bf16[32,64,256]{2,1,0:T(8,128)(2,1)S(1)} %get-tuple-element.13.pooled_ref, bf16[1,64,256]{2,1,0:T(8,128)(2,1)S(1)} %collective-permute-done.5.top_ref, bf16[1,64,256]{2,1,0:T(8,128)(2,1)S(1)} %collective-permute-done.6.bottom_ref, f32[34,1,256]{2,1,0:T(1,128)S(1)} %reshape.189.left_ref, ...), custom_call_target="tpu_custom_call" | custom-call | tf_op jit(solution)/shard_map/pallas_call | solution.py:322
  (39 shorter events, 0.4 us)
Async XLA Ops:
  30.0 11.8 %copy-start.2 = (bf16[8,128,128]{2,1,0:T(8,128)(2,1)S(1)}, bf16[8,128,128]{2,1,0:T(8,128)(2,1)}, u32[]{:S(2)}) copy-start(bf16[8,128,128]{2,1,0:T(8,128)(2,1)} %weights_ref.1) | copy-start | bytes 786436
  30.0 9.0 %collective-permute-start = (bf16[64,64,128]{2,1,0:T(8,128)(2,1)S(1)}, bf16[64,64,128]{2,1,0:T(8,128)(2,1)S(1)}, u32[]{:S(2)}, u32[]{:S(2)}) collective-permute-start(bf16[64,64,128]{2,1,0:T(8,128)(2,1)S(1)} %all_to_all.10), channel_id=1, source_target_pairs={{0,16},{16,0},{1,17},{17,1},{2,18},{18,2},{3,19},{19,3},{4,20},{20... | collective-permute-start | bytes 3145736 | tf_op jit(solution)/shard_map/ppermute | solution.py:385
  32.9 9.0 %collective-permute-start.2 = (bf16[1,128,256]{2,1,0:T(8,128)(2,1)S(1)}, bf16[1,128,256]{2,1,0:T(8,128)(2,1)S(1)}, u32[]{:S(2)}, u32[]{:S(2)}) collective-permute-start(bf16[1,128,256]{2,1,0:T(8,128)(2,1)S(1)} %get-tuple-element.17), channel_id=1, source_target_pairs={{16,0},{32,16},{48,32},{64,48},{80,64},{96,80},{112,96},{17,1},{33... | collective-permute-start | bytes 196616 | tf_op jit(solution)/shard_map/ppermute | solution.py:351
  34.8 7.0 %collective-permute-start.1 = (bf16[1,128,256]{2,1,0:T(8,128)(2,1)S(1)}, bf16[1,128,256]{2,1,0:T(8,128)(2,1)S(1)}, u32[]{:S(2)}, u32[]{:S(2)}) collective-permute-start(bf16[1,128,256]{2,1,0:T(8,128)(2,1)S(1)} %get-tuple-element.18), channel_id=1, source_target_pairs={{0,16},{16,32},{32,48},{48,64},{64,80},{80,96},{96,112},{1,17},{17... | collective-permute-start | bytes 196616 | tf_op jit(solution)/shard_map/ppermute | solution.py:351
  54.5 7.4 %copy-start.4 = (bf16[100,256]{1,0:T(8,128)(2,1)S(1)}, bf16[100,256]{1,0:T(8,128)(2,1)}, u32[]{:S(2)}) copy-start(bf16[100,256]{1,0:T(8,128)(2,1)} %param.18) | copy-start | bytes 153604
  54.5 36.5 %copy-start.1 = (bf16[3,3,256,256]{3,2,1,0:T(8,128)(2,1)S(1)}, bf16[3,3,256,256]{3,2,1,0:T(8,128)(2,1)}, u32[]{:S(2)}) copy-start(bf16[3,3,256,256]{3,2,1,0:T(8,128)(2,1)} %param.19) | copy-start | bytes 3538948
  54.5 52.7 %all-to-all-start.1 = ((bf16[16,512,128]{2,1,0:T(8,128)(2,1)}), bf16[16,512,128]{2,1,0:T(8,128)(2,1)S(1)}, u32[]{:S(2)}, u32[]{:S(2)}) async-start(bf16[16,512,128]{2,1,0:T(8,128)(2,1)} %bitcast.90), calls=%async_computation.1 | async-start | bytes 4194304 | tf_op jit(solution)/shard_map/all_to_all | solution.py:390
  63.2 23.4 %collective-permute-start.3 = (bf16[66,256]{1,0:T(8,128)(2,1)S(1)}, bf16[66,256]{1,0:T(8,128)(2,1)S(1)}, u32[]{:S(2)}, u32[]{:S(2)}) collective-permute-start(bf16[66,256]{1,0:T(8,128)(2,1)S(1)} %pad_maximum_fusion), channel_id=1, source_target_pairs={{0,1},{1,2},{2,3},{3,4},{4,5},{5,6},{6,7},{7,8},{8,9},{9,10},{10,1... | collective-permute-start | bytes 101384 | tf_op jit(solution)/shard_map/ppermute | solution.py:358
  66.1 24.9 %collective-permute-start.4 = (bf16[66,256]{1,0:T(8,128)(2,1)S(1)}, bf16[66,256]{1,0:T(8,128)(2,1)S(1)}, u32[]{:S(2)}, u32[]{:S(2)}) collective-permute-start(bf16[66,256]{1,0:T(8,128)(2,1)S(1)} %pad_maximum_fusion.1), channel_id=1, source_target_pairs={{1,0},{2,1},{3,2},{4,3},{5,4},{6,5},{7,6},{8,7},{9,8},{10,9},{11,1... | collective-permute-start | bytes 101384 | tf_op jit(solution)/shard_map/ppermute | solution.py:359
  107.2 24.4 %copy-start.3 = (bf16[512,256]{1,0:T(8,128)(2,1)S(1)}, bf16[512,256]{1,0:T(8,128)(2,1)}, u32[]{:S(2)}) copy-start(bf16[512,256]{1,0:T(8,128)(2,1)} %up_ref.1) | copy-start | bytes 786436
  115.3 16.3 %copy-start = (bf16[3,3,256,512]{3,2,1,0:T(8,128)(2,1)S(1)}, bf16[3,3,256,512]{3,2,1,0:T(8,128)(2,1)}, u32[]{:S(2)}) copy-start(bf16[3,3,256,512]{3,2,1,0:T(8,128)(2,1)} %param.20) | copy-start | bytes 7077892
  115.9 5.7 %collective-permute-start.6 = (bf16[1,64,256]{2,1,0:T(8,128)(2,1)S(1)}, bf16[1,64,256]{2,1,0:T(8,128)(2,1)S(1)}, u32[]{:S(2)}, u32[]{:S(2)}) collective-permute-start(bf16[1,64,256]{2,1,0:T(8,128)(2,1)S(1)} %get-tuple-element.21), channel_id=1, source_target_pairs={{16,0},{32,16},{48,32},{64,48},{80,64},{96,80},{112,96},{17,1},{33... | collective-permute-start | bytes 98312 | tf_op jit(solution)/shard_map/ppermute | solution.py:351
  118.0 4.7 %collective-permute-start.5 = (bf16[1,64,256]{2,1,0:T(8,128)(2,1)S(1)}, bf16[1,64,256]{2,1,0:T(8,128)(2,1)S(1)}, u32[]{:S(2)}, u32[]{:S(2)}) collective-permute-start(bf16[1,64,256]{2,1,0:T(8,128)(2,1)S(1)} %get-tuple-element.22), channel_id=1, source_target_pairs={{0,16},{16,32},{32,48},{48,64},{64,80},{80,96},{96,112},{1,17},{17... | collective-permute-start | bytes 98312 | tf_op jit(solution)/shard_map/ppermute | solution.py:351
  122.7 5.3 %collective-permute-start.7 = (bf16[34,256]{1,0:T(8,128)(2,1)S(1)}, bf16[34,256]{1,0:T(8,128)(2,1)S(1)}, u32[]{:S(2)}, u32[]{:S(2)}) collective-permute-start(bf16[34,256]{1,0:T(8,128)(2,1)S(1)} %pad_maximum_fusion.2), channel_id=1, source_target_pairs={{0,1},{1,2},{2,3},{3,4},{4,5},{5,6},{6,7},{7,8},{8,9},{9,10},{10,1... | collective-permute-start | bytes 52232 | tf_op jit(solution)/shard_map/ppermute | solution.py:358
  124.9 6.6 %collective-permute-start.8 = (bf16[34,256]{1,0:T(8,128)(2,1)S(1)}, bf16[34,256]{1,0:T(8,128)(2,1)S(1)}, u32[]{:S(2)}, u32[]{:S(2)}) collective-permute-start(bf16[34,256]{1,0:T(8,128)(2,1)S(1)} %pad_maximum_fusion.3), channel_id=1, source_target_pairs={{1,0},{2,1},{3,2},{4,3},{5,4},{6,5},{7,6},{8,7},{9,8},{10,9},{11,1... | collective-permute-start | bytes 52232 | tf_op jit(solution)/shard_map/ppermute | solution.py:359

commit v3 on v2

v3 whole, which is shorter than its diff:
```python
import functools

import jax
import jax.numpy as jnp
from jax import lax
from jax.experimental import pallas as pl
from jax.experimental.pallas import tpu as pltpu
from jax.sharding import Mesh
from jax.sharding import PartitionSpec as P

F32 = jnp.float32
BF16 = jnp.bfloat16
MIB = 1024 * 1024

SUBTILE_ENTRIES = 4
SUBTILE_ROWS = 8
SUBTILE_COLUMNS = 16
Z = 4
CORES = 2
PY = Z * CORES
PX = 16
NEAR = PY // CORES * PX
DEVICES = PY * PX
OWNED = 8
CELLS = 128
CHANNELS = 100
PART = 7
SLOT = 8
PATTERNS = 8
SUBTILES = 64
ENTRIES = SUBTILES * SUBTILE_ENTRIES
TILE_COLUMNS = 8
PART_ROWS = (SUBTILES + 2) * SLOT
ROWS = 64
COLUMNS = 128
FINE = 256
WIDE = 512
TILES = DEVICES * OWNED
ZERO_TILE = PATTERNS * TILES


def silu(v):
    return 0.5 * v * (1.0 + jnp.tanh(0.5 * v))


def in_hbm(array):
    return pltpu.with_memory_space_constraint(array, pltpu.HBM)


def in_vmem(array):
    return pltpu.with_memory_space_constraint(array, pltpu.VMEM)


def whole(*shape):
    return pl.BlockSpec(shape, lambda i: (0,) * len(shape))


def dot(a, b):
    return jnp.dot(a, b, preferred_element_type=F32)


def part_rows():
    row = lax.broadcasted_iota(jnp.int32, (PX * SLOT, CHANNELS), 0)
    channel = lax.broadcasted_iota(jnp.int32, (PX * SLOT, CHANNELS), 1)
    place = row % SLOT
    chosen = (channel == (row // SLOT) * PART + place) & (place < PART)
    return jnp.where(chosen, 1.0, 0.0).astype(BF16)


def pack_kernel(coarse_ref, ids_ref, counts_ref, slot_ref, pattern_ref, out_ref, wide_ref, parts_ref):
    @pl.when(pl.program_id(0) == 0)
    def _():
        wide_ref[...] = coarse_ref[...].astype(F32).reshape(CHANNELS * OWNED, CELLS)
        pick = part_rows()
        tables = [
            slot_ref[:, :CELLS],
            slot_ref[:, CELLS:],
            pattern_ref[:, :CELLS],
            pattern_ref[:, CELLS:],
            ids_ref[0:1],
            ids_ref[1:2],
            counts_ref[...],
            jnp.zeros((1, CELLS), jnp.int32),
        ]
        last = lax.broadcasted_iota(jnp.int32, (PX, SLOT, CELLS), 1) == PART
        for block in range(OWNED):
            cells = wide_ref[pl.ds(block, CHANNELS, stride=OWNED), :].astype(BF16)
            table = jnp.broadcast_to(tables[block].astype(F32)[None], (PX, SLOT, CELLS))
            part = dot(pick, cells).reshape(PX, SLOT, CELLS)
            parts_ref[:, block] = jnp.where(last, table, part)

    out_ref[0] = parts_ref[...].reshape(PX, OWNED * SLOT, CELLS).astype(BF16)


def pack(coarse, ids, counts, slot, pattern):
    return pl.pallas_call(
        pack_kernel,
        grid=(Z,),
        in_specs=[
            whole(CHANNELS, OWNED, CELLS),
            whole(2, DEVICES),
            whole(1, DEVICES),
            whole(1, ENTRIES),
            whole(1, ENTRIES),
        ],
        out_specs=pl.BlockSpec((1, PX, OWNED * SLOT, CELLS), lambda i: (i, 0, 0, 0)),
        out_shape=pltpu.HBM((Z, PX, OWNED * SLOT, CELLS), BF16),
        scratch_shapes=[pltpu.VMEM((CHANNELS * OWNED, CELLS), F32), pltpu.VMEM((PX, OWNED, SLOT, CELLS), F32)],
        compiler_params=pltpu.CompilerParams(vmem_limit_bytes=24 * MIB),
    )(*(in_hbm(array) for array in (coarse, ids, counts, slot, pattern)))


def find_entries(here_ref, own_ref, other_ref, rows_ref, table_ref):
    z, core = here_ref[0], here_ref[1]
    width = 2 * SLOT

    def table(ref, senders, block):
        count = NEAR if senders is None else PX
        where = slice(None) if senders is None else senders
        both = ref[where, block * SLOT : block * SLOT + width, :].astype(F32)
        rows_ref[: count * width] = both.reshape(count * width, CELLS)
        return [rows_ref[pl.ds(SLOT * k + PART, count, stride=width), :] for k in range(2)]

    def sent(block):
        pairs = zip(table(own_ref, None, block), table(other_ref, None, block))
        return [jnp.concatenate(pair, axis=0) for pair in pairs]

    def of_patches(values):
        table_ref[...] = values.T
        return table_ref[pl.ds(pl.multiple_of((CORES * z + core) * PX, PX), PX), :].astype(jnp.int32)

    ids = [of_patches(part) for part in sent(4)]
    counts = of_patches(sent(6)[0])
    sender = lax.broadcasted_iota(jnp.int32, (PX, DEVICES), 1)
    where = [jnp.where(k < counts, sender * OWNED + ids[k], -1) for k in range(2)]
    mine = pl.ds(pl.multiple_of(z * PX, PX), PX)
    slots = table(own_ref, mine, 0)
    patterns = table(own_ref, mine, 2)
    found = []
    for half in range(2):
        slot = slots[half].astype(jnp.int32)
        pattern = patterns[half].astype(jnp.int32)
        owner = slot // 2
        near = owner // (CORES * PX) * PX + owner % PX
        place = near + jnp.where(owner // PX % CORES == core, 0, NEAR)
        either = [jnp.take_along_axis(part, place, axis=1) for part in where]
        block = jnp.where(slot % 2 == 0, either[0], either[1])
        found.append(jnp.where(block >= 0, pattern * TILES + block, ZERO_TILE))
    return found


def blend_kernel(
    here_ref, own_ref, other_ref, weights_ref, out_ref, table_ref, rows_ref, sent_ref, beside_ref, found_ref, index_ref, sem
):
    chunk = 1024
    found = find_entries(here_ref, own_ref, other_ref, rows_ref, sent_ref)
    for half in range(2):
        found_ref[half] = found[half]
    copy = pltpu.make_async_copy(found_ref, index_ref, sem)
    copy.start()

    def multiply(blocks_ref, first, step):
        senders = pl.ds(step * (chunk // (OWNED * SLOT)), chunk // (OWNED * SLOT))
        part = blocks_ref[senders].reshape(chunk, CELLS)
        for pair in range(PATTERNS // 2):
            both = jnp.concatenate([weights_ref[2 * pair], weights_ref[2 * pair + 1]], axis=1)
            product = dot(part, both)
            for half in range(2):
                tiles = pl.ds((2 * pair + half) * TILES + first + step * (chunk // SLOT), chunk // SLOT)
                lanes = slice(half * CELLS, (half + 1) * CELLS)
                table_ref[tiles] = product[:, lanes].reshape(chunk // SLOT, SLOT, CELLS)

    for first, blocks_ref in ((0, own_ref), (TILES // 2, other_ref)):

        def one(step, carry):
            multiply(blocks_ref, first, step)
            return carry

        lax.fori_loop(0, TILES // 2 * SLOT // chunk, one, 0)
    table_ref[ZERO_TILE] = jnp.zeros((SLOT, CELLS), F32)

    copy.wait()

    def total(half, patch, entry):
        tile = [table_ref[index_ref[half, patch, entry + i]] for i in range(SUBTILE_ENTRIES)]
        return (tile[0] + tile[1]) + (tile[2] + tile[3])

    group = SUBTILES // 2

    def gather(patch, carry):
        for half in range(2):
            sums = [total(half, patch, k * SUBTILE_ENTRIES) for k in range(group)]
            for k in range(group):
                tile_row, tile_column = divmod(half * group + k, TILE_COLUMNS)
                if tile_column in (0, TILE_COLUMNS - 1):
                    side = 0 if tile_column else 1
                    at = pl.ds(pl.multiple_of(patch * SLOT, SLOT), SLOT)
                    beside_ref[side, at, tile_row * CELLS : (tile_row + 1) * CELLS] = sums[k]
            for k in range(0, group, 2):
                start = (half * group + k) * SLOT
                out_ref[patch, start : start + 2 * SLOT, :] = jnp.concatenate(sums[k : k + 2], axis=0).astype(BF16)
        return carry

    lax.fori_loop(0, PX, gather, 0)

    tall = TILE_COLUMNS * CELLS
    source = lax.broadcasted_iota(jnp.int32, (tall, CELLS), 0)
    lane = lax.broadcasted_iota(jnp.int32, (tall, CELLS), 1)
    row = lane % ROWS
    cell = (row // SUBTILE_ROWS) * CELLS + (row % SUBTILE_ROWS) * SUBTILE_COLUMNS + lane // ROWS
    moved = []
    for side, column in ((0, SUBTILE_COLUMNS - 2), (1, 0)):
        chosen = jnp.where(source == cell + column, 1.0, 0.0).astype(BF16)
        moved.append(dot(beside_ref[side].astype(BF16), chosen).reshape(PX, SLOT, CELLS))
    nothing = jnp.zeros((1, SLOT, CELLS), F32)
    left = jnp.concatenate([nothing, moved[0][: PX - 1]], axis=0)
    right = jnp.concatenate([moved[1][1:], nothing], axis=0)
    out_ref[:, SUBTILES * SLOT :, :] = jnp.concatenate([left, right], axis=1).astype(BF16)


def blend(here, own, other, weights):
    vmem = pl.BlockSpec(memory_space=pltpu.VMEM)
    return pl.pallas_call(
        blend_kernel,
        in_specs=[pl.BlockSpec(memory_space=pltpu.SMEM), vmem, vmem, vmem],
        out_specs=vmem,
        out_shape=pltpu.HBM((PX, PART_ROWS, CELLS), BF16),
        scratch_shapes=[
            pltpu.VMEM((ZERO_TILE + 1, SLOT, CELLS), F32),
            pltpu.VMEM((NEAR * 2 * SLOT, CELLS), F32),
            pltpu.VMEM((DEVICES, CELLS), F32),
            pltpu.VMEM((2, PX * SLOT, TILE_COLUMNS * CELLS), F32),
            pltpu.VMEM((2, PX, CELLS), jnp.int32),
            pltpu.SMEM((2, PX, CELLS), jnp.int32),
            pltpu.SemaphoreType.DMA,
        ],
        compiler_params=pltpu.CompilerParams(vmem_limit_bytes=44 * MIB),
    )(here, own, other, in_hbm(weights))


def shifted(rows, left, right):
    wide = rows.astype(F32)
    column = lax.broadcasted_iota(jnp.int32, wide.shape, 0)
    last = wide.shape[0] - 1
    before = jnp.where(column == 0, jnp.broadcast_to(left, wide.shape), pltpu.roll(wide, 1, 0))
    after = jnp.where(column == last, jnp.broadcast_to(right, wide.shape), pltpu.roll(wide, last, 0))
    return before.astype(BF16), rows, after.astype(BF16)


def put(taps_ref, row, parts):
    depth = parts[0].shape[-1]
    for k in range(3):
        taps_ref[row, :, k * depth : (k + 1) * depth] = parts[k]


def fill(taps_ref, row, cells, left_ref, right_ref):
    put(taps_ref, row, shifted(cells, left_ref[row], right_ref[row]))


def fill_all(taps_ref, cells_ref, top_ref, bottom_ref, left_ref, right_ref):
    count = cells_ref.shape[0]
    fill(taps_ref, 0, top_ref[0], left_ref, right_ref)

    def one(row, carry):
        fill(taps_ref, row + 1, cells_ref[row], left_ref, right_ref)
        return carry

    lax.fori_loop(0, count, one, 0)
    fill(taps_ref, count + 1, bottom_ref[0], left_ref, right_ref)


def taps_dot(taps_ref, weights_ref, first_row, count):
    columns, depth = taps_ref.shape[1], taps_ref.shape[2]
    total = None
    for row_off in range(3):
        rows = taps_ref[pl.ds(first_row + row_off, count)].reshape(count * columns, depth)
        product = dot(rows, weights_ref[row_off])
        total = product if total is None else total + product
    return total


STRIP = 8


EDGE = 16
REACH = 3


def edges_kernel(left_ref, right_ref, left_out, right_out, wide_ref):
    for cells_ref, out_ref, column in ((left_ref, left_out, 0), (right_ref, right_out, EDGE - REACH)):
        for lane in range(FINE // 128):
            lanes = slice(lane * 128, (lane + 1) * 128)
            wide_ref[...] = cells_ref[:, :, lanes].astype(F32).reshape(ROWS * EDGE, 128)
            for k in range(REACH):
                out_ref[k, :, lanes] = wide_ref[pl.ds(column + k, ROWS, stride=EDGE), :].astype(BF16)


def edge_columns(cells):
    cells = in_hbm(cells)
    columns = jax.ShapeDtypeStruct((REACH, ROWS, FINE), BF16)
    return pl.pallas_call(
        edges_kernel,
        grid=(1,),
        in_specs=[
            pl.BlockSpec((ROWS, EDGE, FINE), lambda i: (0, 0, 0)),
            pl.BlockSpec((ROWS, EDGE, FINE), lambda i: (0, COLUMNS // EDGE - 1, 0)),
        ],
        out_specs=[whole(REACH, ROWS, FINE)] * 2,
        out_shape=[columns, columns],
        scratch_shapes=[pltpu.VMEM((ROWS * EDGE, 128), F32)],
        compiler_params=pltpu.CompilerParams(vmem_limit_bytes=8 * MIB),
    )(cells, cells)


def strip_kernel(cells_ref, top_ref, weights_ref, out_ref, taps_ref):
    empty = jnp.zeros((1, FINE), F32)
    put(taps_ref, 0, shifted(top_ref[0], empty, empty))
    for row in range(STRIP + 1):
        put(taps_ref, row + 1, shifted(cells_ref[row], empty, empty))
    total = taps_dot(taps_ref, weights_ref, 0, STRIP)
    out_ref[...] = total.reshape(STRIP, COLUMNS, FINE).astype(BF16)


def conv_strip(cells, top, weights):
    return pl.pallas_call(
        strip_kernel,
        grid=(1,),
        in_specs=[whole(2 * STRIP, COLUMNS, FINE), whole(1, COLUMNS, FINE), whole(3, 3 * FINE, FINE)],
        out_specs=whole(STRIP, COLUMNS, FINE),
        out_shape=pltpu.HBM((STRIP, COLUMNS, FINE), BF16),
        scratch_shapes=[pltpu.VMEM((STRIP + 2, COLUMNS, 3 * FINE), BF16)],
        compiler_params=pltpu.CompilerParams(vmem_limit_bytes=16 * MIB),
    )(in_hbm(cells), top, in_hbm(weights))


def conv_kernel(cells_ref, bottom_ref, weights_ref, strip_ref, out_ref, taps_ref):
    step = pl.program_id(0)

    @pl.when(step == 0)
    def _():
        empty = jnp.zeros((1, FINE), F32)

        def one(row, carry):
            put(taps_ref, row + 1, shifted(cells_ref[row], empty, empty))
            return carry

        lax.fori_loop(STRIP - 1, ROWS, one, 0)
        put(taps_ref, ROWS + 1, shifted(bottom_ref[0], empty, empty))
        out_ref[...] = strip_ref[...]

    @pl.when(step > 0)
    def _():
        total = taps_dot(taps_ref, weights_ref, step * STRIP, STRIP)
        out_ref[...] = total.reshape(STRIP, COLUMNS, FINE).astype(BF16)


def conv_inside(cells, bottom, weights, strip):
    return pl.pallas_call(
        conv_kernel,
        grid=(ROWS // STRIP,),
        in_specs=[
            whole(ROWS, COLUMNS, FINE),
            whole(1, COLUMNS, FINE),
            whole(3, 3 * FINE, FINE),
            whole(STRIP, COLUMNS, FINE),
        ],
        out_specs=pl.BlockSpec((STRIP, COLUMNS, FINE), lambda i: (i, 0, 0)),
        out_shape=pltpu.HBM((ROWS, COLUMNS, FINE), BF16),
        scratch_shapes=[pltpu.VMEM((ROWS + 2, COLUMNS, 3 * FINE), BF16)],
        compiler_params=pltpu.CompilerParams(vmem_limit_bytes=40 * MIB),
    )(in_hbm(cells), bottom, in_hbm(weights), strip)


def sides_kernel(before_ref, after_ref, first_ref, last_ref, weights_ref, sides_ref, beside_ref):
    def taps(ref, k):
        ends = [ref[k, ROWS + end : ROWS + end + 1, :].astype(F32) for end in range(2)]
        return jnp.concatenate(shifted(ref[k, :ROWS, :], *ends), axis=1)

    left = [taps(before_ref, k) for k in range(REACH)] + [taps(first_ref, 0)]
    right = [taps(last_ref, REACH - 1)] + [taps(after_ref, k) for k in range(REACH)]
    total = jnp.zeros((4 * ROWS, FINE), F32)
    for col_off in range(3):
        start = col_off * FINE
        part = jnp.concatenate([weights_ref[row_off, start : start + FINE, :] for row_off in range(3)], axis=0)
        if col_off == 0:
            sides_ref[0] = dot(left[2], part).reshape(ROWS, 1, FINE)
        if col_off == 2:
            sides_ref[1] = dot(right[1], part).reshape(ROWS, 1, FINE)
        rows = [left[col_off], left[col_off + 1], right[col_off], right[col_off + 1]]
        total = total + dot(jnp.concatenate(rows, axis=0), part)
    beside_ref[...] = total.reshape(2, 2 * ROWS, FINE)


def conv_sides(before, after, first, last, weights):
    column = whole(REACH, ROWS + 2, FINE)
    return pl.pallas_call(
        sides_kernel,
        grid=(1,),
        in_specs=[column] * 4 + [whole(3, 3 * FINE, FINE)],
        out_specs=[whole(2, ROWS, 1, FINE), whole(2, 2 * ROWS, FINE)],
        out_shape=[
            jax.ShapeDtypeStruct((2, ROWS, 1, FINE), F32),
            jax.ShapeDtypeStruct((2, 2 * ROWS, FINE), F32),
        ],
        compiler_params=pltpu.CompilerParams(vmem_limit_bytes=16 * MIB),
    )(before, after, first, last, in_hbm(weights))


STRIPS = 2
ROW_TILES = COLUMNS // SUBTILE_COLUMNS


def pool_of(group):
    return jnp.where(group == lax.broadcasted_iota(jnp.int32, group.shape, 0), 0.25, 0.0).astype(BF16)


def lifted_of(parts, lift):
    rows = [part.reshape(PX * SLOT, CELLS).astype(BF16) for part in parts]
    return lax.dot_general(
        jnp.concatenate(rows, axis=1), lift, (((0,), (0,)), ((), ())), preferred_element_type=F32
    ).astype(BF16)


def first_of(kept, conv, guidance):
    return (kept.astype(F32) + silu(conv + guidance.astype(F32))).astype(BF16)


def first_kernel(
    here_ref,
    blended_ref,
    blended_beside_ref,
    lift_ref,
    conv_ref,
    cells_ref,
    sides_ref,
    conv_beside_ref,
    before_ref,
    after_ref,
    first_ref,
    pooled_ref,
    pooled_beside_ref,
):
    lift = dot(part_rows(), lift_ref[...]).astype(BF16)
    cell = lax.broadcasted_iota(jnp.int32, (32, CELLS), 1)

    @pl.when(pl.program_id(0) == 0)
    def _():
        pool = pool_of(cell % ROWS // 2)
        both = blended_beside_ref[...].astype(F32)
        lifted = lifted_of([both[:, side * SLOT : (side + 1) * SLOT, :] for side in range(2)], lift)
        kept = [
            jnp.concatenate([before_ref[k, :ROWS, :] for k in (1, 2)], axis=0),
            jnp.concatenate([after_ref[k, :ROWS, :] for k in (0, 1)], axis=0),
        ]
        inside = [here_ref[2] > 0, here_ref[2] < PX - 1]
        for side in range(2):
            guidance = lifted[side * CELLS : (side + 1) * CELLS]
            first = first_of(kept[side], conv_beside_ref[side], guidance)
            pooled_beside_ref[side] = jnp.where(inside[side], dot(pool, first), 0.0).astype(BF16)

    row = cell // SUBTILE_COLUMNS
    column = cell % SUBTILE_COLUMNS
    pool = pool_of((row // 2) * 8 + column // 2)
    at = lax.broadcasted_iota(jnp.int32, (STRIP, SUBTILE_COLUMNS, FINE), 1)
    for strip in range(STRIPS):
        parts = []
        for pair in range(ROW_TILES // 2):
            start = (strip * ROW_TILES + 2 * pair) * SLOT
            both = blended_ref[:, start : start + 2 * SLOT, :].astype(F32)
            parts += [both[:, half * SLOT : (half + 1) * SLOT, :] for half in range(2)]
        lifted = lifted_of(parts, lift)
        rows = slice(strip * STRIP, (strip + 1) * STRIP)
        half_rows = slice(strip * STRIP // 2, (strip + 1) * STRIP // 2)
        for tile in range(ROW_TILES):
            columns = slice(tile * SUBTILE_COLUMNS, (tile + 1) * SUBTILE_COLUMNS)
            conv = conv_ref[rows, columns, :].astype(F32)
            if tile == 0:
                conv = conv + jnp.where(at == 0, sides_ref[0, rows], 0.0)
            if tile == ROW_TILES - 1:
                conv = conv + jnp.where(at == SUBTILE_COLUMNS - 1, sides_ref[1, rows], 0.0)
            kept = cells_ref[rows, columns, :].reshape(CELLS, FINE)
            first = first_of(kept, conv.reshape(CELLS, FINE), lifted[tile * CELLS : (tile + 1) * CELLS])
            first_ref[rows, columns, :] = first.reshape(SUBTILE_ROWS, SUBTILE_COLUMNS, FINE)
            pooled = dot(pool, first).reshape(STRIP // 2, 8, FINE).astype(BF16)
            pooled_ref[half_rows, tile * 8 : (tile + 1) * 8, :] = pooled


def first_level(here, blended, lift, conv, cells, sides, conv_beside, before, after):
    count = STRIPS * STRIP
    strip = pl.BlockSpec((count, COLUMNS, FINE), lambda i: (i, 0, 0))
    beside = pl.BlockSpec((PX, 2 * SLOT, CELLS), lambda i: (0, SUBTILES // 2, 0))
    return pl.pallas_call(
        first_kernel,
        grid=(ROWS // count,),
        in_specs=[
            pl.BlockSpec(memory_space=pltpu.SMEM),
            pl.BlockSpec((PX, STRIPS * ROW_TILES * SLOT, CELLS), lambda i: (0, i, 0)),
            beside,
            whole(CHANNELS, FINE),
            strip,
            strip,
            pl.BlockSpec((2, count, 1, FINE), lambda i: (0, i, 0, 0)),
            whole(2, 2 * ROWS, FINE),
            whole(REACH, ROWS + 2, FINE),
            whole(REACH, ROWS + 2, FINE),
        ],
        out_specs=[
            strip,
            pl.BlockSpec((count // 2, COLUMNS // 2, FINE), lambda i: (i, 0, 0)),
            whole(2, ROWS // 2, FINE),
        ],
        out_shape=[
            pltpu.VMEM((ROWS, COLUMNS, FINE), BF16),
            jax.ShapeDtypeStruct((ROWS // 2, COLUMNS // 2, FINE), BF16),
            jax.ShapeDtypeStruct((2, ROWS // 2, FINE), BF16),
        ],
        compiler_params=pltpu.CompilerParams(vmem_limit_bytes=32 * MIB),
    )(here, blended, blended, in_hbm(lift), in_hbm(conv), in_hbm(cells), sides, conv_beside, before, after)


SECOND = 8


def second_kernel(
    pooled_ref, top_ref, bottom_ref, left_ref, right_ref, weights_ref, up_ref, first_ref, out_ref, taps_ref, spread_ref
):
    step = pl.program_id(0)

    @pl.when(step == 0)
    def _():
        fill_all(taps_ref, pooled_ref, top_ref, bottom_ref, left_ref, right_ref)

    second = silu(taps_dot(taps_ref, weights_ref, step * SECOND, SECOND)).astype(BF16)
    projected = dot(second, up_ref[...])
    half = COLUMNS // 2
    for lane in range(FINE // 128):
        part = projected[:, lane * 128 : (lane + 1) * 128]
        for side in range(2):
            spread_ref[lane, pl.ds(side, SECOND * half, stride=2), :] = part
    for lane in range(FINE // 128):
        lanes = slice(lane * 128, (lane + 1) * 128)
        for row in range(SECOND):
            added = spread_ref[lane, row * COLUMNS : (row + 1) * COLUMNS, :]
            for side in range(2):
                first = first_ref[2 * row + side, :, lanes].astype(F32)
                out_ref[2 * row + side, :, lanes] = (first + added).astype(BF16)


def second_level(pooled, halo, weights, up, first):
    strip = pl.BlockSpec((2 * SECOND, COLUMNS, FINE), lambda i: (i, 0, 0))
    return pl.pallas_call(
        second_kernel,
        grid=(ROWS // 2 // SECOND,),
        in_specs=[
            whole(ROWS // 2, COLUMNS // 2, FINE),
            whole(1, COLUMNS // 2, FINE),
            whole(1, COLUMNS // 2, FINE),
            whole(ROWS // 2 + 2, 1, FINE),
            whole(ROWS // 2 + 2, 1, FINE),
            whole(3, 3 * FINE, WIDE),
            whole(WIDE, FINE),
            strip,
        ],
        out_specs=strip,
        out_shape=jax.ShapeDtypeStruct((ROWS, COLUMNS, FINE), BF16),
        scratch_shapes=[
            pltpu.VMEM((ROWS // 2 + 2, COLUMNS // 2, 3 * FINE), BF16),
            pltpu.VMEM((FINE // 128, SECOND * COLUMNS, 128), F32),
        ],
        compiler_params=pltpu.CompilerParams(vmem_limit_bytes=48 * MIB),
    )(pooled, *halo, weights, up, in_vmem(first))


ROWS_AXES = ("z", "core")


def from_rows(last, first):
    down = [(i, i + 1) for i in range(PY - 1)]
    up = [(i + 1, i) for i in range(PY - 1)]
    return lax.ppermute(last, ROWS_AXES, down), lax.ppermute(first, ROWS_AXES, up)


def from_columns(last, first):
    return (
        lax.ppermute(last, "px", [(i, i + 1) for i in range(PX - 1)]),
        lax.ppermute(first, "px", [(i + 1, i) for i in range(PX - 1)]),
    )


def local(
    features,
    coarse,
    send_ids,
    send_counts,
    entry_slot,
    entry_weight_pattern,
    interpolation_weights,
    lift_weight,
    conv_a,
    conv_b,
    up_weight,
):
    here = jnp.stack([lax.axis_index(axis) for axis in ("z", "core", "px")]).astype(jnp.int32)
    outgoing = pack(coarse.transpose(1, 0, 2), send_ids[0].T, send_counts, entry_slot, entry_weight_pattern)
    outgoing, cells = lax.optimization_barrier((outgoing, features))
    own = lax.all_to_all(
        outgoing.reshape(NEAR, OWNED * SLOT, CELLS), ("z", "px"), split_axis=0, concat_axis=0, tiled=True
    )
    above, below = from_rows(cells[-1:], cells[:1])
    weights = conv_a.reshape(3, 3 * FINE, FINE)
    strip = conv_strip(cells, above, weights)
    first_columns, last_columns = edge_columns(cells)
    own, strip, above, below = lax.optimization_barrier((own, strip, above, below))
    other = lax.ppermute(own, "core", [(0, 1), (1, 0)])
    parts = blend(here, own, other, interpolation_weights)
    parts, strip, above, below = lax.optimization_barrier((parts, strip, above, below))
    blended = lax.all_to_all(parts, "px", split_axis=0, concat_axis=0, tiled=True)

    def with_ends(columns, start):
        ends = [row[:, start : start + REACH].transpose(1, 0, 2) for row in (above, below)]
        return jnp.concatenate([columns, *ends], axis=1)

    first_columns = with_ends(first_columns, 0)
    last_columns = with_ends(last_columns, COLUMNS - REACH)
    before, after = from_columns(last_columns, first_columns)
    conv = conv_inside(cells, below, weights, strip)
    sides, conv_beside = conv_sides(before, after, first_columns, last_columns, weights)
    first, pooled, pooled_beside = first_level(
        here, blended, lift_weight, conv, features, sides, conv_beside, before, after
    )

    def wide(row):
        return jnp.concatenate([pooled[row], pooled_beside[:, row]], axis=0)

    half = COLUMNS // 2
    above, below = from_rows(wide(ROWS // 2 - 1), wide(0))
    columns = [
        jnp.concatenate([above[half + side][None], pooled_beside[side], below[half + side][None]], axis=0)
        for side in range(2)
    ]
    edges = (above[None, :half], below[None, :half], *(column[:, None].astype(F32) for column in columns))
    return second_level(pooled, edges, conv_b.reshape(3, 3 * FINE, WIDE), up_weight, first)


def solution(mesh):
    split = Mesh(mesh.devices.reshape(Z, CORES, PX), ("z", "core", "px"))
    every = ("z", "core", "px")
    placed = (
        P(ROWS_AXES, "px", None),
        P(every, None, None),
        P(every, None, None),
        P(every, None),
        P(every, None),
        P(every, None),
        P(),
        P(),
        P(),
        P(),
        P(),
    )
    return jax.shard_map(
        local, mesh=split, in_specs=placed, out_specs=P(ROWS_AXES, "px", None), check_vma=False
    )
```

time: 144 us -> 115 us (0.80); the launches traced: 141 us -> 115 us
  blocking collectives: 24.8 us -> 0 us
  Pallas kernels: 47.2 us -> 56.2 us
  waiting for transfers between devices: 26.9 us -> 21 us
  local copies, waits for them, and re-layouts: 6.15 us -> 1.05 us
  starting transfers between devices: 31.2 us -> 35.8 us
  other arithmetic: 4.78 us -> 0.24 us
    all_to_all x1 -> x0, blocking collectives: 24.8 us -> none  [local(): lax.all_to_all(outgoing, ('z', 'px'), split_axis=0, concat_axis=0, tiled=...]
    all_to_all x1 -> x2, starting transfers between devices: 7.42 us -> 17.4 us  [the longest x1 10.6 us: local(): lax.all_to_all(outgoing.reshape(NEAR, OWNED * SLOT, CELLS), ('z', 'px'),...]
    ppermute x8 -> x6, waiting for transfers between devices: 26.8 us -> 18.4 us  [the longest x2 5.62 us: from_rows(): lax.ppermute(last, ROWS_AXES, down)]
    pallas_call x3 -> x6, Pallas kernels: 24.7 us -> 32.9 us  [the longest x1 15 us: conv_inside(): pl.pallas_call(conv_kernel, grid=(ROWS // STRIP,), in_specs=[whole(ROWS,...]
    ppermute x8 -> x6, starting transfers between devices: 21.8 us -> 18.4 us  [the longest x2 9.29 us: from_rows(): lax.ppermute(last, ROWS_AXES, down)]
    ppermute x1, waiting for transfers between devices: 0.01 us -> 2.57 us  [local(): other = lax.ppermute(own, 'core', [(0, 1), (1, 0)])]
    reduce_sum x1 -> x0, other arithmetic: 2.09 us -> none  [entry_index(): block = jnp.sum(jnp.where(place[:, :, None] == sender_at, found, 0), axis=2)]
    ppermute x1, starting transfers between devices: 1.99 us -> 0.01 us  [local(): other = lax.ppermute(own, 'core', [(0, 1), (1, 0)])]
  transfers between devices with their start and end apart: 10 -> 9, of which waited for: 4 -> 5; matrix products, arithmetic and copies ran while one was open for 4% -> 1% of each run, Pallas kernels for 11% -> 19%
where the time goes in v3:
time: 115 us
  Pallas kernels  56.2 us (49%)
  starting transfers between devices  35.8 us (31%)
  waiting for transfers between devices  21 us (18%)
    pallas_call x1, Pallas kernels, conv_inside(): pl.pallas_call(conv_kernel, grid=(ROWS // STRIP,), in_specs=[whole(ROWS,...  15 us
    pallas_call x1, Pallas kernels, blend(): pl.pallas_call(blend_kernel, in_specs=[pl.BlockSpec(memory_space=pltpu.SM...  13.1 us
    all_to_all x1, starting transfers between devices, local(): lax.all_to_all(outgoing.reshape(NEAR, OWNED * SLOT, CELLS), ('z', 'px'),...  10.6 us
    pallas_call x1, Pallas kernels, second_level(): pl.pallas_call(second_kernel, grid=(ROWS // 2 // SECOND,), in_specs=[whol...  10.2 us
    ppermute x2, starting transfers between devices, from_rows(): lax.ppermute(last, ROWS_AXES, down)  9.29 us
    pallas_call x1, Pallas kernels, first_level(): pl.pallas_call(first_kernel, grid=(ROWS // count,), in_specs=[pl.BlockSpe...  8 us
    all_to_all x1, starting transfers between devices, local(): lax.all_to_all(parts, 'px', split_axis=0, concat_axis=0, tiled=True)  6.84 us
    ppermute x2, waiting for transfers between devices, from_rows(): lax.ppermute(last, ROWS_AXES, down)  5.62 us
  transfers between devices with their start and end apart: 9, of which 5 were waited for; matrix products, arithmetic and copies ran while one was open for 1% of the time, Pallas kernels for 19%

profile of v3, /device:TPU:29, one launch (start us, length us, event | category | flops | bytes accessed | tf_op | source)
XLA Modules:
  0.0 114.6 jit_solution(17681256790483501550)
XLA Ops:
  0.0 2.8 %shard_map.109 = bf16[4,16,64,128]{3,2,1,0:T(8,128)(2,1)} custom-call(bf16[100,8,128]{2,1,0:T(8,128)(2,1)} %bitcast.47, s32[2,128]{1,0:T(2,128)} %bitcast.48, s32[1,128]{1,0:T(1,128)} %counts_ref.1, s32[1,256]{1,0:T(1,128)} %slot_ref.1, s32[1,256]{1,0:T(1,128)} %pattern_ref.1), custom_call_target="tpu_custom_call" | custom-call | tf_op jit(solution)/shard_map/pallas_call | solution.py:96
  2.8 10.6 %all-to-all-start = ((bf16[64,64,128]{2,1,0:T(8,128)(2,1)}), bf16[64,64,128]{2,1,0:T(8,128)(2,1)S(1)}, u32[]{:S(2)}, u32[]{:S(2)}) async-start(bf16[64,64,128]{2,1,0:T(8,128)(2,1)} %bitcast.45), calls=%async_computation | async-start | bytes 2097152 | tf_op jit(solution)/shard_map/all_to_all | solution.py:606
  13.3 0.9 fusion
  14.2 4.3 %collective-permute-start = (bf16[1,128,256]{2,1,0:T(8,128)(2,1)S(1)}, bf16[1,128,256]{2,1,0:T(8,128)(2,1)S(1)}, u32[]{:S(2)}, u32[]{:S(2)}) collective-permute-start(bf16[1,128,256]{2,1,0:T(8,128)(2,1)S(1)} %get-tuple-element.40), channel_id=1, source_target_pairs={{0,16},{16,32},{32,48},{48,64},{64,80},{80,96},{96,112},{1,17},{17... | collective-permute-start | bytes 196616 | tf_op jit(solution)/shard_map/ppermute | solution.py:580
  18.5 1.9 %collective-permute-start.1 = (bf16[1,128,256]{2,1,0:T(8,128)(2,1)S(1)}, bf16[1,128,256]{2,1,0:T(8,128)(2,1)S(1)}, u32[]{:S(2)}, u32[]{:S(2)}) collective-permute-start(bf16[1,128,256]{2,1,0:T(8,128)(2,1)S(1)} %get-tuple-element.39), channel_id=1, source_target_pairs={{16,0},{32,16},{48,32},{64,48},{80,64},{96,80},{112,96},{17,1},{33... | collective-permute-start | bytes 196616 | tf_op jit(solution)/shard_map/ppermute | solution.py:580
  20.4 5.6 %collective-permute-done.top_ref = bf16[1,128,256]{2,1,0:T(8,128)(2,1)S(1)} collective-permute-done((bf16[1,128,256]{2,1,0:T(8,128)(2,1)S(1)}, bf16[1,128,256]{2,1,0:T(8,128)(2,1)S(1)}, u32[]{:S(2)}, u32[]{:S(2)}) %collective-permute-start) | collective-permute-done | bytes 65568 | tf_op jit(solution)/shard_map/ppermute | solution.py:580
  26.1 3.8 %shard_map.110.strip_ref = bf16[8,128,256]{2,1,0:T(8,128)(2,1)} custom-call(bf16[64,128,256]{2,1,0:T(8,128)(2,1)} %cells_ref.3, bf16[1,128,256]{2,1,0:T(8,128)(2,1)S(1)} %collective-permute-done.top_ref, bf16[3,768,256]{2,1,0:T(8,128)(2,1)} %bitcast.42), custom_call_target="tpu_custom_call" | custom-call | tf_op jit(solution)/shard_map/pallas_call | solution.py:325
  29.8 0.0 collective-permute-done.1.bottom_ref
  29.8 0.0 all-to-all-done.own_ref
  29.9 0.0 collective-permute-start.2
  29.9 0.1 pad_add_fusion.here_ref
  29.9 2.6 %collective-permute-done.2.other_ref = bf16[64,64,128]{2,1,0:T(8,128)(2,1)S(1)} collective-permute-done((bf16[64,64,128]{2,1,0:T(8,128)(2,1)S(1)}, bf16[64,64,128]{2,1,0:T(8,128)(2,1)S(1)}, u32[]{:S(2)}, u32[]{:S(2)}) %collective-permute-start.2) | collective-permute-done | bytes 1048608 | tf_op jit(solution)/shard_map/ppermute | solution.py:614
  32.5 13.1 %shard_map.111 = bf16[16,528,128]{2,1,0:T(8,128)(2,1)} custom-call(s32[3]{0:T(128)S(1)} %pad_add_fusion.here_ref, bf16[64,64,128]{2,1,0:T(8,128)(2,1)S(1)} %all-to-all-done.own_ref, bf16[64,64,128]{2,1,0:T(8,128)(2,1)S(1)} %collective-permute-done.2.other_ref, bf16[8,128,128]{2,1,0:T(8,128)(2,1)} %weights_ref.1), custom_call_target="tpu_custom_call" | custom-call | tf_op jit(solution)/shard_map/pallas_call | solution.py:223
  45.6 6.8 %all-to-all-start.1 = ((bf16[16,528,128]{2,1,0:T(8,128)(2,1)}), bf16[16,528,128]{2,1,0:T(8,128)(2,1)S(1)}, u32[]{:S(2)}, u32[]{:S(2)}) async-start(bf16[16,528,128]{2,1,0:T(8,128)(2,1)} %shard_map.111), calls=%async_computation.1 | async-start | bytes 4325376 | tf_op jit(solution)/shard_map/all_to_all | solution.py:617
  52.5 0.0 copy-start
  52.5 1.5 %shard_map.113 = (bf16[3,64,256]{2,1,0:T(8,128)(2,1)S(1)}, bf16[3,64,256]{2,1,0:T(8,128)(2,1)S(1)}) custom-call(bf16[64,128,256]{2,1,0:T(8,128)(2,1)} %cells_ref.3, bf16[64,128,256]{2,1,0:T(8,128)(2,1)} %cells_ref.3), custom_call_target="tpu_custom_call" | custom-call | tf_op jit(solution)/shard_map/pallas_call | solution.py:301
  54.1 2.8 %collective-permute-start.3 = (bf16[3,66,256]{2,1,0:T(8,128)(2,1)S(1)}, bf16[3,66,256]{2,1,0:T(8,128)(2,1)S(1)}, u32[]{:S(2)}, u32[]{:S(2)}) collective-permute-start(bf16[3,66,256]{2,1,0:T(8,128)(2,1)S(1)} %pad_maximum_fusion.last_ref), channel_id=1, source_target_pairs={{0,1},{1,2},{2,3},{3,4},{4,5},{5,6},{6,7},{7,8},{8,9},{9,10},{10,1... | collective-permute-start | bytes 304136 | tf_op jit(solution)/shard_map/ppermute | solution.py:585
  56.9 2.5 %collective-permute-start.4 = (bf16[3,66,256]{2,1,0:T(8,128)(2,1)S(1)}, bf16[3,66,256]{2,1,0:T(8,128)(2,1)S(1)}, u32[]{:S(2)}, u32[]{:S(2)}) collective-permute-start(bf16[3,66,256]{2,1,0:T(8,128)(2,1)S(1)} %pad_maximum_fusion.1.first_ref), channel_id=1, source_target_pairs={{1,0},{2,1},{3,2},{4,3},{5,4},{6,5},{7,6},{8,7},{9,8},{10,9},{11,1... | collective-permute-start | bytes 304136 | tf_op jit(solution)/shard_map/ppermute | solution.py:586
  59.4 0.0 copy-done
  59.4 15.0 %shard_map.112.conv_ref = bf16[64,128,256]{2,1,0:T(8,128)(2,1)} custom-call(bf16[64,128,256]{2,1,0:T(8,128)(2,1)} %cells_ref.3, bf16[1,128,256]{2,1,0:T(8,128)(2,1)S(1)} %collective-permute-done.1.bottom_ref, bf16[3,768,256]{2,1,0:T(8,128)(2,1)} %bitcast.43, bf16[8,128,256]{2,1,0:T(8,128)(2,1)S(1)} %copy-done), custom_call_target="tpu_custom_call" | custom-call | tf_op jit(solution)/shard_map/pallas_call | solution.py:358
  74.4 4.5 %collective-permute-done.3.before_ref = bf16[3,66,256]{2,1,0:T(8,128)(2,1)S(1)} collective-permute-done((bf16[3,66,256]{2,1,0:T(8,128)(2,1)S(1)}, bf16[3,66,256]{2,1,0:T(8,128)(2,1)S(1)}, u32[]{:S(2)}, u32[]{:S(2)}) %collective-permute-start.3) | collective-permute-done | bytes 101408 | tf_op jit(solution)/shard_map/ppermute | solution.py:585
  78.8 5.0 %collective-permute-done.4.after_ref = bf16[3,66,256]{2,1,0:T(8,128)(2,1)S(1)} collective-permute-done((bf16[3,66,256]{2,1,0:T(8,128)(2,1)S(1)}, bf16[3,66,256]{2,1,0:T(8,128)(2,1)S(1)}, u32[]{:S(2)}, u32[]{:S(2)}) %collective-permute-start.4) | collective-permute-done | bytes 101408 | tf_op jit(solution)/shard_map/ppermute | solution.py:586
  83.8 1.9 %shard_map.114 = (f32[2,64,1,256]{3,2,1,0:T(1,128)S(1)}, f32[2,128,256]{2,1,0:T(8,128)S(1)}) custom-call(bf16[3,66,256]{2,1,0:T(8,128)(2,1)S(1)} %collective-permute-done.3.before_ref, bf16[3,66,256]{2,1,0:T(8,128)(2,1)S(1)} %collective-permute-done.4.after_ref, bf16[3,66,256]{2,1,0:T(8,128)(2,1)S(1)} %pad_maximum_fusion.1.first_ref, ...), custom_call_target="tpu_custom_call" | custom-call | tf_op jit(solution)/shard_map/pallas_call | solution.py:396
  85.7 0.0 all-to-all-done.1.blended_ref.blended_beside_ref
  85.7 0.0 copy-start.1
  85.7 8.0 %shard_map.115 = (bf16[64,128,256]{2,1,0:T(8,128)(2,1)S(1)}, bf16[32,64,256]{2,1,0:T(8,128)(2,1)S(1)}, bf16[2,32,256]{2,1,0:T(8,128)(2,1)S(1)}) custom-call(s32[3]{0:T(128)S(1)} %pad_add_fusion.here_ref, bf16[16,528,128]{2,1,0:T(8,128)(2,1)S(1)} %all-to-all-done.1.blended_ref.blended_beside_ref, ...), custom_call_target="tpu_custom_call" | custom-call | tf_op jit(solution)/shard_map/pallas_call | solution.py:492
  93.9 5.0 %collective-permute-start.5 = (bf16[66,256]{1,0:T(8,128)(2,1)S(1)}, bf16[66,256]{1,0:T(8,128)(2,1)S(1)}, u32[]{:S(2)}, u32[]{:S(2)}) collective-permute-start(bf16[66,256]{1,0:T(8,128)(2,1)S(1)} %pad_maximum_fusion.2), channel_id=1, source_target_pairs={{0,16},{16,32},{32,48},{48,64},{64,80},{80,96},{96,112},{1,17},{17... | collective-permute-start | bytes 101384 | tf_op jit(solution)/shard_map/ppermute | solution.py:580
  99.0 1.9 %collective-permute-start.6 = (bf16[66,256]{1,0:T(8,128)(2,1)S(1)}, bf16[66,256]{1,0:T(8,128)(2,1)S(1)}, u32[]{:S(2)}, u32[]{:S(2)}) collective-permute-start(bf16[66,256]{1,0:T(8,128)(2,1)S(1)} %pad_maximum_fusion.3), channel_id=1, source_target_pairs={{16,0},{32,16},{48,32},{64,48},{80,64},{96,80},{112,96},{17,1},{33... | collective-permute-start | bytes 101384 | tf_op jit(solution)/shard_map/ppermute | solution.py:580
  100.9 0.0 collective-permute-done.5
  100.9 3.3 %collective-permute-done.6 = bf16[66,256]{1,0:T(8,128)(2,1)S(1)} collective-permute-done((bf16[66,256]{1,0:T(8,128)(2,1)S(1)}, bf16[66,256]{1,0:T(8,128)(2,1)S(1)}, u32[]{:S(2)}, u32[]{:S(2)}) %collective-permute-start.6) | collective-permute-done | bytes 33824 | tf_op jit(solution)/shard_map/ppermute | solution.py:580
  104.2 0.1 maximum_convert_fusion.1.right_ref
  104.3 0.1 maximum_convert_fusion.left_ref
  104.4 0.0 copy-done.1
  104.4 10.2 %shard_map.116 = bf16[64,128,256]{2,1,0:T(8,128)(2,1)} custom-call(bf16[32,64,256]{2,1,0:T(8,128)(2,1)S(1)} %get-tuple-element.36.pooled_ref, bf16[1,64,256]{2,1,0:T(8,128)(2,1)S(1)} %slice_bitcast_fusion.1.top_ref, bf16[1,64,256]{2,1,0:T(8,128)(2,1)S(1)} %slice_bitcast_fusion.bottom_ref, f32[34,1,256]{2,1,0:T(1,128)S(1)} %maximum_convert_fusion.left_ref, ...), custom_call_target="tpu_custom_call" | custom-call | tf_op jit(solution)/shard_map/pallas_call | solution.py:551
  (19 shorter events, 0.2 us)
Async XLA Ops:
  2.8 27.1 %all-to-all-start = ((bf16[64,64,128]{2,1,0:T(8,128)(2,1)}), bf16[64,64,128]{2,1,0:T(8,128)(2,1)S(1)}, u32[]{:S(2)}, u32[]{:S(2)}) async-start(bf16[64,64,128]{2,1,0:T(8,128)(2,1)} %bitcast.45), calls=%async_computation | async-start | bytes 2097152 | tf_op jit(solution)/shard_map/all_to_all | solution.py:606
  14.2 11.8 %collective-permute-start = (bf16[1,128,256]{2,1,0:T(8,128)(2,1)S(1)}, bf16[1,128,256]{2,1,0:T(8,128)(2,1)S(1)}, u32[]{:S(2)}, u32[]{:S(2)}) collective-permute-start(bf16[1,128,256]{2,1,0:T(8,128)(2,1)S(1)} %get-tuple-element.40), channel_id=1, source_target_pairs={{0,16},{16,32},{32,48},{48,64},{64,80},{80,96},{96,112},{1,17},{17... | collective-permute-start | bytes 196616 | tf_op jit(solution)/shard_map/ppermute | solution.py:580
  18.5 11.3 %collective-permute-start.1 = (bf16[1,128,256]{2,1,0:T(8,128)(2,1)S(1)}, bf16[1,128,256]{2,1,0:T(8,128)(2,1)S(1)}, u32[]{:S(2)}, u32[]{:S(2)}) collective-permute-start(bf16[1,128,256]{2,1,0:T(8,128)(2,1)S(1)} %get-tuple-element.39), channel_id=1, source_target_pairs={{16,0},{32,16},{48,32},{64,48},{80,64},{96,80},{112,96},{17,1},{33... | collective-permute-start | bytes 196616 | tf_op jit(solution)/shard_map/ppermute | solution.py:580
  29.9 2.7 %collective-permute-start.2 = (bf16[64,64,128]{2,1,0:T(8,128)(2,1)S(1)}, bf16[64,64,128]{2,1,0:T(8,128)(2,1)S(1)}, u32[]{:S(2)}, u32[]{:S(2)}) collective-permute-start(bf16[64,64,128]{2,1,0:T(8,128)(2,1)S(1)} %all-to-all-done.own_ref), channel_id=1, source_target_pairs={{0,16},{16,0},{1,17},{17,1},{2,18},{18,2},{3,19},{19,3},{4,20},{20... | collective-permute-start | bytes 3145736 | tf_op jit(solution)/shard_map/ppermute | solution.py:614
  45.6 40.1 %all-to-all-start.1 = ((bf16[16,528,128]{2,1,0:T(8,128)(2,1)}), bf16[16,528,128]{2,1,0:T(8,128)(2,1)S(1)}, u32[]{:S(2)}, u32[]{:S(2)}) async-start(bf16[16,528,128]{2,1,0:T(8,128)(2,1)} %shard_map.111), calls=%async_computation.1 | async-start | bytes 4325376 | tf_op jit(solution)/shard_map/all_to_all | solution.py:617
  52.5 6.9 %copy-start = (bf16[8,128,256]{2,1,0:T(8,128)(2,1)S(1)}, bf16[8,128,256]{2,1,0:T(8,128)(2,1)}, u32[]{:S(2)}) copy-start(bf16[8,128,256]{2,1,0:T(8,128)(2,1)} %shard_map.110.strip_ref) | copy-start | bytes 1572868
  54.1 24.8 %collective-permute-start.3 = (bf16[3,66,256]{2,1,0:T(8,128)(2,1)S(1)}, bf16[3,66,256]{2,1,0:T(8,128)(2,1)S(1)}, u32[]{:S(2)}, u32[]{:S(2)}) collective-permute-start(bf16[3,66,256]{2,1,0:T(8,128)(2,1)S(1)} %pad_maximum_fusion.last_ref), channel_id=1, source_target_pairs={{0,1},{1,2},{2,3},{3,4},{4,5},{5,6},{6,7},{7,8},{8,9},{9,10},{10,1... | collective-permute-start | bytes 304136 | tf_op jit(solution)/shard_map/ppermute | solution.py:585
  56.9 27.0 %collective-permute-start.4 = (bf16[3,66,256]{2,1,0:T(8,128)(2,1)S(1)}, bf16[3,66,256]{2,1,0:T(8,128)(2,1)S(1)}, u32[]{:S(2)}, u32[]{:S(2)}) collective-permute-start(bf16[3,66,256]{2,1,0:T(8,128)(2,1)S(1)} %pad_maximum_fusion.1.first_ref), channel_id=1, source_target_pairs={{1,0},{2,1},{3,2},{4,3},{5,4},{6,5},{7,6},{8,7},{9,8},{10,9},{11,1... | collective-permute-start | bytes 304136 | tf_op jit(solution)/shard_map/ppermute | solution.py:586
  85.7 18.7 %copy-start.1 = (bf16[512,256]{1,0:T(8,128)(2,1)S(1)}, bf16[512,256]{1,0:T(8,128)(2,1)}, u32[]{:S(2)}) copy-start(bf16[512,256]{1,0:T(8,128)(2,1)} %up_ref.1) | copy-start | bytes 786436
  93.9 7.0 %collective-permute-start.5 = (bf16[66,256]{1,0:T(8,128)(2,1)S(1)}, bf16[66,256]{1,0:T(8,128)(2,1)S(1)}, u32[]{:S(2)}, u32[]{:S(2)}) collective-permute-start(bf16[66,256]{1,0:T(8,128)(2,1)S(1)} %pad_maximum_fusion.2), channel_id=1, source_target_pairs={{0,16},{16,32},{32,48},{48,64},{64,80},{80,96},{96,112},{1,17},{17... | collective-permute-start | bytes 101384 | tf_op jit(solution)/shard_map/ppermute | solution.py:580
  99.0 5.3 %collective-permute-start.6 = (bf16[66,256]{1,0:T(8,128)(2,1)S(1)}, bf16[66,256]{1,0:T(8,128)(2,1)S(1)}, u32[]{:S(2)}, u32[]{:S(2)}) collective-permute-start(bf16[66,256]{1,0:T(8,128)(2,1)S(1)} %pad_maximum_fusion.3), channel_id=1, source_target_pairs={{16,0},{32,16},{48,32},{64,48},{80,64},{96,80},{112,96},{17,1},{33... | collective-permute-start | bytes 101384 | tf_op jit(solution)/shard_map/ppermute | solution.py:580

commit v4 on v3

--- a/solution.py
+++ b/solution.py
@@ -284,6 +284,7 @@
 
 EDGE = 16
 REACH = 3
+LONG = COLUMNS + 16
 
 
 def edges_kernel(left_ref, right_ref, left_out, right_out, wide_ref):
@@ -312,28 +313,30 @@
     )(cells, cells)
 
 
-def strip_kernel(cells_ref, top_ref, weights_ref, out_ref, taps_ref):
+INNER = 1
+
+
+def strip_kernel(cells_ref, weights_ref, out_ref, taps_ref):
     empty = jnp.zeros((1, FINE), F32)
-    put(taps_ref, 0, shifted(top_ref[0], empty, empty))
-    for row in range(STRIP + 1):
-        put(taps_ref, row + 1, shifted(cells_ref[row], empty, empty))
+    for row in range(STRIP + 2):
+        put(taps_ref, row, shifted(cells_ref[INNER * STRIP - 1 + row], empty, empty))
     total = taps_dot(taps_ref, weights_ref, 0, STRIP)
     out_ref[...] = total.reshape(STRIP, COLUMNS, FINE).astype(BF16)
 
 
-def conv_strip(cells, top, weights):
+def conv_strip(cells, weights):
     return pl.pallas_call(
         strip_kernel,
         grid=(1,),
-        in_specs=[whole(2 * STRIP, COLUMNS, FINE), whole(1, COLUMNS, FINE), whole(3, 3 * FINE, FINE)],
+        in_specs=[whole((INNER + 2) * STRIP, COLUMNS, FINE), whole(3, 3 * FINE, FINE)],
         out_specs=whole(STRIP, COLUMNS, FINE),
         out_shape=pltpu.HBM((STRIP, COLUMNS, FINE), BF16),
         scratch_shapes=[pltpu.VMEM((STRIP + 2, COLUMNS, 3 * FINE), BF16)],
         compiler_params=pltpu.CompilerParams(vmem_limit_bytes=16 * MIB),
-    )(in_hbm(cells), top, in_hbm(weights))
-
-
-def conv_kernel(cells_ref, bottom_ref, weights_ref, strip_ref, out_ref, taps_ref):
+    )(in_hbm(cells), in_hbm(weights))
+
+
+def conv_kernel(cells_ref, above_ref, below_ref, weights_ref, strip_ref, out_ref, taps_ref):
     step = pl.program_id(0)
 
     @pl.when(step == 0)
@@ -344,23 +347,28 @@
             put(taps_ref, row + 1, shifted(cells_ref[row], empty, empty))
             return carry
 
-        lax.fori_loop(STRIP - 1, ROWS, one, 0)
-        put(taps_ref, ROWS + 1, shifted(bottom_ref[0], empty, empty))
+        lax.fori_loop(0, ROWS, one, 0)
+        put(taps_ref, 0, shifted(above_ref[:COLUMNS], empty, empty))
+        put(taps_ref, ROWS + 1, shifted(below_ref[:COLUMNS], empty, empty))
+
+    @pl.when(step == INNER)
+    def _():
         out_ref[...] = strip_ref[...]
 
-    @pl.when(step > 0)
+    @pl.when(step != INNER)
     def _():
         total = taps_dot(taps_ref, weights_ref, step * STRIP, STRIP)
         out_ref[...] = total.reshape(STRIP, COLUMNS, FINE).astype(BF16)
 
 
-def conv_inside(cells, bottom, weights, strip):
+def conv_inside(cells, above, below, weights, strip):
     return pl.pallas_call(
         conv_kernel,
         grid=(ROWS // STRIP,),
         in_specs=[
             whole(ROWS, COLUMNS, FINE),
-            whole(1, COLUMNS, FINE),
+            whole(LONG, FINE),
+            whole(LONG, FINE),
             whole(3, 3 * FINE, FINE),
             whole(STRIP, COLUMNS, FINE),
         ],
@@ -368,16 +376,19 @@
         out_shape=pltpu.HBM((ROWS, COLUMNS, FINE), BF16),
         scratch_shapes=[pltpu.VMEM((ROWS + 2, COLUMNS, 3 * FINE), BF16)],
         compiler_params=pltpu.CompilerParams(vmem_limit_bytes=40 * MIB),
-    )(in_hbm(cells), bottom, in_hbm(weights), strip)
-
-
-def sides_kernel(before_ref, after_ref, first_ref, last_ref, weights_ref, sides_ref, beside_ref):
-    def taps(ref, k):
-        ends = [ref[k, ROWS + end : ROWS + end + 1, :].astype(F32) for end in range(2)]
-        return jnp.concatenate(shifted(ref[k, :ROWS, :], *ends), axis=1)
-
-    left = [taps(before_ref, k) for k in range(REACH)] + [taps(first_ref, 0)]
-    right = [taps(last_ref, REACH - 1)] + [taps(after_ref, k) for k in range(REACH)]
+    )(in_hbm(cells), above, below, in_hbm(weights), strip)
+
+
+def sides_kernel(
+    before_ref, after_ref, first_ref, last_ref, above_ref, below_ref, weights_ref, sides_ref, beside_ref
+):
+    def taps(ref, k, at):
+        ends = [row_ref[at : at + 1, :].astype(F32) for row_ref in (above_ref, below_ref)]
+        return jnp.concatenate(shifted(ref[k], *ends), axis=1)
+
+    left = [taps(before_ref, k, COLUMNS + k) for k in range(REACH)] + [taps(first_ref, 0, 0)]
+    right = [taps(last_ref, REACH - 1, COLUMNS - 1)]
+    right += [taps(after_ref, k, COLUMNS + REACH + k) for k in range(REACH)]
     total = jnp.zeros((4 * ROWS, FINE), F32)
     for col_off in range(3):
         start = col_off * FINE
@@ -391,19 +402,18 @@
     beside_ref[...] = total.reshape(2, 2 * ROWS, FINE)
 
 
-def conv_sides(before, after, first, last, weights):
-    column = whole(REACH, ROWS + 2, FINE)
+def conv_sides(before, after, first, last, above, below, weights):
     return pl.pallas_call(
         sides_kernel,
         grid=(1,),
-        in_specs=[column] * 4 + [whole(3, 3 * FINE, FINE)],
+        in_specs=[whole(REACH, ROWS, FINE)] * 4 + [whole(LONG, FINE)] * 2 + [whole(3, 3 * FINE, FINE)],
         out_specs=[whole(2, ROWS, 1, FINE), whole(2, 2 * ROWS, FINE)],
         out_shape=[
             jax.ShapeDtypeStruct((2, ROWS, 1, FINE), F32),
             jax.ShapeDtypeStruct((2, 2 * ROWS, FINE), F32),
         ],
         compiler_params=pltpu.CompilerParams(vmem_limit_bytes=16 * MIB),
-    )(before, after, first, last, in_hbm(weights))
+    )(before, after, first, last, above, below, in_hbm(weights))
 
 
 STRIPS = 2
@@ -449,8 +459,8 @@
         both = blended_beside_ref[...].astype(F32)
         lifted = lifted_of([both[:, side * SLOT : (side + 1) * SLOT, :] for side in range(2)], lift)
         kept = [
-            jnp.concatenate([before_ref[k, :ROWS, :] for k in (1, 2)], axis=0),
-            jnp.concatenate([after_ref[k, :ROWS, :] for k in (0, 1)], axis=0),
+            jnp.concatenate([before_ref[k] for k in (1, 2)], axis=0),
+            jnp.concatenate([after_ref[k] for k in (0, 1)], axis=0),
         ]
         inside = [here_ref[2] > 0, here_ref[2] < PX - 1]
         for side in range(2):
@@ -501,8 +511,8 @@
             strip,
             pl.BlockSpec((2, count, 1, FINE), lambda i: (0, i, 0, 0)),
             whole(2, 2 * ROWS, FINE),
-            whole(REACH, ROWS + 2, FINE),
-            whole(REACH, ROWS + 2, FINE),
+            whole(REACH, ROWS, FINE),
+            whole(REACH, ROWS, FINE),
         ],
         out_specs=[
             strip,
@@ -606,25 +616,24 @@
     own = lax.all_to_all(
         outgoing.reshape(NEAR, OWNED * SLOT, CELLS), ("z", "px"), split_axis=0, concat_axis=0, tiled=True
     )
-    above, below = from_rows(cells[-1:], cells[:1])
     weights = conv_a.reshape(3, 3 * FINE, FINE)
-    strip = conv_strip(cells, above, weights)
     first_columns, last_columns = edge_columns(cells)
-    own, strip, above, below = lax.optimization_barrier((own, strip, above, below))
+    first_columns, last_columns, cells = lax.optimization_barrier((first_columns, last_columns, cells))
+    before, after = from_columns(last_columns, first_columns)
+    strip = conv_strip(cells, weights)
+    own, strip, before, after = lax.optimization_barrier((own, strip, before, after))
     other = lax.ppermute(own, "core", [(0, 1), (1, 0)])
     parts = blend(here, own, other, interpolation_weights)
-    parts, strip, above, below = lax.optimization_barrier((parts, strip, above, below))
+    parts, strip, before, after = lax.optimization_barrier((parts, strip, before, after))
     blended = lax.all_to_all(parts, "px", split_axis=0, concat_axis=0, tiled=True)
 
-    def with_ends(columns, start):
-        ends = [row[:, start : start + REACH].transpose(1, 0, 2) for row in (above, below)]
-        return jnp.concatenate([columns, *ends], axis=1)
-
-    first_columns = with_ends(first_columns, 0)
-    last_columns = with_ends(last_columns, COLUMNS - REACH)
-    before, after = from_columns(last_columns, first_columns)
-    conv = conv_inside(cells, below, weights, strip)
-    sides, conv_beside = conv_sides(before, after, first_columns, last_columns, weights)
+    def long(row):
+        rest = jnp.zeros((LONG - COLUMNS - 2 * REACH, FINE), BF16)
+        return jnp.concatenate([cells[row], before[:, row], after[:, row], rest], axis=0)
+
+    above, below = from_rows(long(ROWS - 1), long(0))
+    conv = conv_inside(cells, above, below, weights, strip)
+    sides, conv_beside = conv_sides(before, after, first_columns, last_columns, above, below, weights)
     first, pooled, pooled_beside = first_level(
         here, blended, lift_weight, conv, features, sides, conv_beside, before, after
     )

time: 115 us -> 113 us (0.983)
  the two profiles are of different devices: /device:TPU:29 before, /device:TPU:1 now
where the time goes in v4:
time: 113 us; the launch traced here: 112 us
  Pallas kernels  57.3 us (51%)
  starting transfers between devices  34.6 us (31%)
  waiting for transfers between devices  18.4 us (16%)
    pallas_call x1, Pallas kernels, conv_inside(): pl.pallas_call(conv_kernel, grid=(ROWS // STRIP,), in_specs=[whole(ROWS,...  16 us
    pallas_call x1, Pallas kernels, blend(): pl.pallas_call(blend_kernel, in_specs=[pl.BlockSpec(memory_space=pltpu.SM...  13.1 us
    all_to_all x1, starting transfers between devices, local(): lax.all_to_all(outgoing.reshape(NEAR, OWNED * SLOT, CELLS), ('z', 'px'),...  12 us
    pallas_call x1, Pallas kernels, second_level(): pl.pallas_call(second_kernel, grid=(ROWS // 2 // SECOND,), in_specs=[whol...  10.2 us
    pallas_call x1, Pallas kernels, first_level(): pl.pallas_call(first_kernel, grid=(ROWS // count,), in_specs=[pl.BlockSpe...  7.97 us
    ppermute x2, starting transfers between devices, from_rows(): lax.ppermute(last, ROWS_AXES, down)  7.57 us
    ppermute x2, starting transfers between devices, from_rows(): lax.ppermute(first, ROWS_AXES, up)  4.31 us
    pallas_call x1, Pallas kernels, conv_strip(): pl.pallas_call(strip_kernel, grid=(1,), in_specs=[whole((INNER + 2) * STR...  3.94 us
  transfers between devices with their start and end apart: 9, of which 8 were waited for; matrix products, arithmetic and copies ran while one was open for 1% of the time, Pallas kernels for 21%

profile of v4, /device:TPU:1, one launch (start us, length us, event | category | flops | bytes accessed | tf_op | source)
XLA Modules:
  0.0 112.0 jit_solution(8686291457358626057)
XLA Ops:
  0.0 2.8 %shard_map.109 = bf16[4,16,64,128]{3,2,1,0:T(8,128)(2,1)} custom-call(bf16[100,8,128]{2,1,0:T(8,128)(2,1)} %bitcast.55, s32[2,128]{1,0:T(2,128)} %bitcast.60, s32[1,128]{1,0:T(1,128)} %counts_ref.1, s32[1,256]{1,0:T(1,128)} %slot_ref.1, s32[1,256]{1,0:T(1,128)} %pattern_ref.1), custom_call_target="tpu_custom_call" | custom-call | tf_op jit(solution)/shard_map/pallas_call | solution.py:96
  2.8 12.0 %all-to-all-start = ((bf16[64,64,128]{2,1,0:T(8,128)(2,1)}), bf16[64,64,128]{2,1,0:T(8,128)(2,1)S(1)}, u32[]{:S(2)}, u32[]{:S(2)}) async-start(bf16[64,64,128]{2,1,0:T(8,128)(2,1)} %bitcast.53), calls=%async_computation | async-start | bytes 2097152 | tf_op jit(solution)/shard_map/all_to_all | solution.py:616
  14.7 1.4 %shard_map.110 = (bf16[3,64,256]{2,1,0:T(8,128)(2,1)S(1)}, bf16[3,64,256]{2,1,0:T(8,128)(2,1)S(1)}) custom-call(bf16[64,128,256]{2,1,0:T(8,128)(2,1)} %cells_ref.3, bf16[64,128,256]{2,1,0:T(8,128)(2,1)} %cells_ref.3), custom_call_target="tpu_custom_call" | custom-call | tf_op jit(solution)/shard_map/pallas_call | solution.py:302
  16.2 2.9 %collective-permute-start = (bf16[3,64,256]{2,1,0:T(8,128)(2,1)S(1)}, bf16[3,64,256]{2,1,0:T(8,128)(2,1)S(1)}, u32[]{:S(2)}, u32[]{:S(2)}) collective-permute-start(bf16[3,64,256]{2,1,0:T(8,128)(2,1)S(1)} %get-tuple-element.30.last_ref), channel_id=1, source_target_pairs={{0,1},{1,2},{2,3},{3,4},{4,5},{5,6},{6,7},{7,8},{8,9},{9,10},{10,1... | collective-permute-start | bytes 294920 | tf_op jit(solution)/shard_map/ppermute | solution.py:595
  19.1 1.3 %collective-permute-start.1 = (bf16[3,64,256]{2,1,0:T(8,128)(2,1)S(1)}, bf16[3,64,256]{2,1,0:T(8,128)(2,1)S(1)}, u32[]{:S(2)}, u32[]{:S(2)}) collective-permute-start(bf16[3,64,256]{2,1,0:T(8,128)(2,1)S(1)} %get-tuple-element.31.first_ref), channel_id=1, source_target_pairs={{1,0},{2,1},{3,2},{4,3},{5,4},{6,5},{7,6},{8,7},{9,8},{10,9},{11,1... | collective-permute-start | bytes 294920 | tf_op jit(solution)/shard_map/ppermute | solution.py:596
  20.4 3.9 %shard_map.111.strip_ref = bf16[8,128,256]{2,1,0:T(8,128)(2,1)} custom-call(bf16[64,128,256]{2,1,0:T(8,128)(2,1)} %cells_ref.3, bf16[3,768,256]{2,1,0:T(8,128)(2,1)} %bitcast.50), custom_call_target="tpu_custom_call" | custom-call | tf_op jit(solution)/shard_map/pallas_call | solution.py:328
  24.4 2.0 %collective-permute-done.before_ref = bf16[3,64,256]{2,1,0:T(8,128)(2,1)S(1)} collective-permute-done((bf16[3,64,256]{2,1,0:T(8,128)(2,1)S(1)}, bf16[3,64,256]{2,1,0:T(8,128)(2,1)S(1)}, u32[]{:S(2)}, u32[]{:S(2)}) %collective-permute-start) | collective-permute-done | bytes 98336 | tf_op jit(solution)/shard_map/ppermute | solution.py:595
  26.4 2.9 %collective-permute-done.1.after_ref = bf16[3,64,256]{2,1,0:T(8,128)(2,1)S(1)} collective-permute-done((bf16[3,64,256]{2,1,0:T(8,128)(2,1)S(1)}, bf16[3,64,256]{2,1,0:T(8,128)(2,1)S(1)}, u32[]{:S(2)}, u32[]{:S(2)}) %collective-permute-start.1) | collective-permute-done | bytes 98336 | tf_op jit(solution)/shard_map/ppermute | solution.py:596
  29.3 2.6 %all-to-all-done.own_ref = bf16[64,64,128]{2,1,0:T(8,128)(2,1)S(1)} async-done(((bf16[64,64,128]{2,1,0:T(8,128)(2,1)}), bf16[64,64,128]{2,1,0:T(8,128)(2,1)S(1)}, u32[]{:S(2)}, u32[]{:S(2)}) %all-to-all-start) | async-done | bytes 1048608 | tf_op jit(solution)/shard_map/all_to_all | solution.py:616
  31.9 2.7 %collective-permute-start.2 = (bf16[64,64,128]{2,1,0:T(8,128)(2,1)S(1)}, bf16[64,64,128]{2,1,0:T(8,128)(2,1)S(1)}, u32[]{:S(2)}, u32[]{:S(2)}) collective-permute-start(bf16[64,64,128]{2,1,0:T(8,128)(2,1)S(1)} %all-to-all-done.own_ref), channel_id=1, source_target_pairs={{0,16},{16,0},{1,17},{17,1},{2,18},{18,2},{3,19},{19,3},{4,20},{20... | collective-permute-start | bytes 3145736 | tf_op jit(solution)/shard_map/ppermute | solution.py:625
  34.6 0.1 pad_add_fusion.here_ref
  34.6 2.2 %collective-permute-done.2.other_ref = bf16[64,64,128]{2,1,0:T(8,128)(2,1)S(1)} collective-permute-done((bf16[64,64,128]{2,1,0:T(8,128)(2,1)S(1)}, bf16[64,64,128]{2,1,0:T(8,128)(2,1)S(1)}, u32[]{:S(2)}, u32[]{:S(2)}) %collective-permute-start.2) | collective-permute-done | bytes 1048608 | tf_op jit(solution)/shard_map/ppermute | solution.py:625
  36.9 13.1 %shard_map.112 = bf16[16,528,128]{2,1,0:T(8,128)(2,1)} custom-call(s32[3]{0:T(128)S(1)} %pad_add_fusion.here_ref, bf16[64,64,128]{2,1,0:T(8,128)(2,1)S(1)} %all-to-all-done.own_ref, bf16[64,64,128]{2,1,0:T(8,128)(2,1)S(1)} %collective-permute-done.2.other_ref, bf16[8,128,128]{2,1,0:T(8,128)(2,1)} %weights_ref.1), custom_call_target="tpu_custom_call" | custom-call | tf_op jit(solution)/shard_map/pallas_call | solution.py:223
  50.0 0.0 copy-start
  50.0 3.9 %all-to-all-start.1 = ((bf16[16,528,128]{2,1,0:T(8,128)(2,1)}), bf16[16,528,128]{2,1,0:T(8,128)(2,1)S(1)}, u32[]{:S(2)}, u32[]{:S(2)}) async-start(bf16[16,528,128]{2,1,0:T(8,128)(2,1)} %shard_map.112), calls=%async_computation.1 | async-start | bytes 4325376 | tf_op jit(solution)/shard_map/all_to_all | solution.py:628
  53.9 0.1 pad.17.clone
  53.9 0.9 slice_bitcast_fusion
  54.9 0.1 maximum_maximum_fusion.1
  55.0 2.4 %collective-permute-start.4 = (bf16[144,256]{1,0:T(8,128)(2,1)S(1)}, bf16[144,256]{1,0:T(8,128)(2,1)S(1)}, u32[]{:S(2)}, u32[]{:S(2)}) collective-permute-start(bf16[144,256]{1,0:T(8,128)(2,1)S(1)} %get-tuple-element.61), channel_id=1, source_target_pairs={{16,0},{32,16},{48,32},{64,48},{80,64},{96,80},{112,96},{17,1},{33... | collective-permute-start | bytes 221192 | tf_op jit(solution)/shard_map/ppermute | solution.py:590
  57.4 3.2 %collective-permute-start.3 = (bf16[144,256]{1,0:T(8,128)(2,1)S(1)}, bf16[144,256]{1,0:T(8,128)(2,1)S(1)}, u32[]{:S(2)}, u32[]{:S(2)}) collective-permute-start(bf16[144,256]{1,0:T(8,128)(2,1)S(1)} %get-tuple-element.62), channel_id=1, source_target_pairs={{0,16},{16,32},{32,48},{48,64},{64,80},{80,96},{96,112},{1,17},{17... | collective-permute-start | bytes 221192 | tf_op jit(solution)/shard_map/ppermute | solution.py:590
  60.6 0.4 collective-permute-done.4.below_ref
  61.0 1.0 collective-permute-done.3.above_ref
  62.0 1.9 %shard_map.114 = (f32[2,64,1,256]{3,2,1,0:T(1,128)S(1)}, f32[2,128,256]{2,1,0:T(8,128)S(1)}) custom-call(bf16[3,64,256]{2,1,0:T(8,128)(2,1)S(1)} %collective-permute-done.before_ref, bf16[3,64,256]{2,1,0:T(8,128)(2,1)S(1)} %collective-permute-done.1.after_ref, bf16[3,64,256]{2,1,0:T(8,128)(2,1)S(1)} %get-tuple-element.31.first_ref, ...), custom_call_target="tpu_custom_call" | custom-call | tf_op jit(solution)/shard_map/pallas_call | solution.py:406
  63.8 0.0 copy-done
  63.9 16.0 %shard_map.113.conv_ref = bf16[64,128,256]{2,1,0:T(8,128)(2,1)} custom-call(bf16[64,128,256]{2,1,0:T(8,128)(2,1)} %cells_ref.3, bf16[144,256]{1,0:T(8,128)(2,1)S(1)} %collective-permute-done.3.above_ref, bf16[144,256]{1,0:T(8,128)(2,1)S(1)} %collective-permute-done.4.below_ref, bf16[3,768,256]{2,1,0:T(8,128)(2,1)} %bitcast.52, bf16[8,128,256]{2,1,0:T(8,128)(2,1)S(1)} %copy-done), custom_call_target="tpu_custom_call" | custom-call | tf_op jit(solution)/shard_map/pallas_call | solution.py:365
  79.9 3.9 %all-to-all-done.1.blended_ref.blended_beside_ref = bf16[16,528,128]{2,1,0:T(8,128)(2,1)S(1)} async-done(((bf16[16,528,128]{2,1,0:T(8,128)(2,1)}), bf16[16,528,128]{2,1,0:T(8,128)(2,1)S(1)}, u32[]{:S(2)}, u32[]{:S(2)}) %all-to-all-start.1) | async-done | bytes 2162720 | tf_op jit(solution)/shard_map/all_to_all | solution.py:628
  83.8 0.0 copy-start.1
  83.8 8.0 %shard_map.115 = (bf16[64,128,256]{2,1,0:T(8,128)(2,1)S(1)}, bf16[32,64,256]{2,1,0:T(8,128)(2,1)S(1)}, bf16[2,32,256]{2,1,0:T(8,128)(2,1)S(1)}) custom-call(s32[3]{0:T(128)S(1)} %pad_add_fusion.here_ref, bf16[16,528,128]{2,1,0:T(8,128)(2,1)S(1)} %all-to-all-done.1.blended_ref.blended_beside_ref, ...), custom_call_target="tpu_custom_call" | custom-call | tf_op jit(solution)/shard_map/pallas_call | solution.py:502
  91.8 4.4 %collective-permute-start.5 = (bf16[66,256]{1,0:T(8,128)(2,1)S(1)}, bf16[66,256]{1,0:T(8,128)(2,1)S(1)}, u32[]{:S(2)}, u32[]{:S(2)}) collective-permute-start(bf16[66,256]{1,0:T(8,128)(2,1)S(1)} %pad_maximum_fusion), channel_id=1, source_target_pairs={{0,16},{16,32},{32,48},{48,64},{64,80},{80,96},{96,112},{1,17},{17... | collective-permute-start | bytes 101384 | tf_op jit(solution)/shard_map/ppermute | solution.py:590
  96.3 1.9 %collective-permute-start.6 = (bf16[66,256]{1,0:T(8,128)(2,1)S(1)}, bf16[66,256]{1,0:T(8,128)(2,1)S(1)}, u32[]{:S(2)}, u32[]{:S(2)}) collective-permute-start(bf16[66,256]{1,0:T(8,128)(2,1)S(1)} %pad_maximum_fusion.1), channel_id=1, source_target_pairs={{16,0},{32,16},{48,32},{64,48},{80,64},{96,80},{112,96},{17,1},{33... | collective-permute-start | bytes 101384 | tf_op jit(solution)/shard_map/ppermute | solution.py:590
  98.3 0.0 collective-permute-done.5
  98.3 3.3 %collective-permute-done.6 = bf16[66,256]{1,0:T(8,128)(2,1)S(1)} collective-permute-done((bf16[66,256]{1,0:T(8,128)(2,1)S(1)}, bf16[66,256]{1,0:T(8,128)(2,1)S(1)}, u32[]{:S(2)}, u32[]{:S(2)}) %collective-permute-start.6) | collective-permute-done | bytes 33824 | tf_op jit(solution)/shard_map/ppermute | solution.py:590
  101.6 0.1 maximum_convert_fusion.1.right_ref
  101.7 0.1 maximum_convert_fusion.left_ref
  101.8 0.0 copy-done.1
  101.8 10.2 %shard_map.116 = bf16[64,128,256]{2,1,0:T(8,128)(2,1)} custom-call(bf16[32,64,256]{2,1,0:T(8,128)(2,1)S(1)} %get-tuple-element.42.pooled_ref, bf16[1,64,256]{2,1,0:T(8,128)(2,1)S(1)} %slice_bitcast_fusion.3.top_ref, bf16[1,64,256]{2,1,0:T(8,128)(2,1)S(1)} %slice_bitcast_fusion.2.bottom_ref, f32[34,1,256]{2,1,0:T(1,128)S(1)} %maximum_convert_fusion.left_ref, ...), custom_call_target="tpu_custom_call" | custom-call | tf_op jit(solution)/shard_map/pallas_call | solution.py:561
  (18 shorter events, 0.2 us)
Async XLA Ops:
  2.8 29.1 %all-to-all-start = ((bf16[64,64,128]{2,1,0:T(8,128)(2,1)}), bf16[64,64,128]{2,1,0:T(8,128)(2,1)S(1)}, u32[]{:S(2)}, u32[]{:S(2)}) async-start(bf16[64,64,128]{2,1,0:T(8,128)(2,1)} %bitcast.53), calls=%async_computation | async-start | bytes 2097152 | tf_op jit(solution)/shard_map/all_to_all | solution.py:616
  16.2 10.2 %collective-permute-start = (bf16[3,64,256]{2,1,0:T(8,128)(2,1)S(1)}, bf16[3,64,256]{2,1,0:T(8,128)(2,1)S(1)}, u32[]{:S(2)}, u32[]{:S(2)}) collective-permute-start(bf16[3,64,256]{2,1,0:T(8,128)(2,1)S(1)} %get-tuple-element.30.last_ref), channel_id=1, source_target_pairs={{0,1},{1,2},{2,3},{3,4},{4,5},{5,6},{6,7},{7,8},{8,9},{9,10},{10,1... | collective-permute-start | bytes 294920 | tf_op jit(solution)/shard_map/ppermute | solution.py:595
  19.1 10.2 %collective-permute-start.1 = (bf16[3,64,256]{2,1,0:T(8,128)(2,1)S(1)}, bf16[3,64,256]{2,1,0:T(8,128)(2,1)S(1)}, u32[]{:S(2)}, u32[]{:S(2)}) collective-permute-start(bf16[3,64,256]{2,1,0:T(8,128)(2,1)S(1)} %get-tuple-element.31.first_ref), channel_id=1, source_target_pairs={{1,0},{2,1},{3,2},{4,3},{5,4},{6,5},{7,6},{8,7},{9,8},{10,9},{11,1... | collective-permute-start | bytes 294920 | tf_op jit(solution)/shard_map/ppermute | solution.py:596
  31.9 4.9 %collective-permute-start.2 = (bf16[64,64,128]{2,1,0:T(8,128)(2,1)S(1)}, bf16[64,64,128]{2,1,0:T(8,128)(2,1)S(1)}, u32[]{:S(2)}, u32[]{:S(2)}) collective-permute-start(bf16[64,64,128]{2,1,0:T(8,128)(2,1)S(1)} %all-to-all-done.own_ref), channel_id=1, source_target_pairs={{0,16},{16,0},{1,17},{17,1},{2,18},{18,2},{3,19},{19,3},{4,20},{20... | collective-permute-start | bytes 3145736 | tf_op jit(solution)/shard_map/ppermute | solution.py:625
  50.0 13.9 %copy-start = (bf16[8,128,256]{2,1,0:T(8,128)(2,1)S(1)}, bf16[8,128,256]{2,1,0:T(8,128)(2,1)}, u32[]{:S(2)}) copy-start(bf16[8,128,256]{2,1,0:T(8,128)(2,1)} %shard_map.111.strip_ref) | copy-start | bytes 1572868
  50.0 33.8 %all-to-all-start.1 = ((bf16[16,528,128]{2,1,0:T(8,128)(2,1)}), bf16[16,528,128]{2,1,0:T(8,128)(2,1)S(1)}, u32[]{:S(2)}, u32[]{:S(2)}) async-start(bf16[16,528,128]{2,1,0:T(8,128)(2,1)} %shard_map.112), calls=%async_computation.1 | async-start | bytes 4325376 | tf_op jit(solution)/shard_map/all_to_all | solution.py:628
  55.0 6.0 %collective-permute-start.4 = (bf16[144,256]{1,0:T(8,128)(2,1)S(1)}, bf16[144,256]{1,0:T(8,128)(2,1)S(1)}, u32[]{:S(2)}, u32[]{:S(2)}) collective-permute-start(bf16[144,256]{1,0:T(8,128)(2,1)S(1)} %get-tuple-element.61), channel_id=1, source_target_pairs={{16,0},{32,16},{48,32},{64,48},{80,64},{96,80},{112,96},{17,1},{33... | collective-permute-start | bytes 221192 | tf_op jit(solution)/shard_map/ppermute | solution.py:590
  57.4 4.6 %collective-permute-start.3 = (bf16[144,256]{1,0:T(8,128)(2,1)S(1)}, bf16[144,256]{1,0:T(8,128)(2,1)S(1)}, u32[]{:S(2)}, u32[]{:S(2)}) collective-permute-start(bf16[144,256]{1,0:T(8,128)(2,1)S(1)} %get-tuple-element.62), channel_id=1, source_target_pairs={{0,16},{16,32},{32,48},{48,64},{64,80},{80,96},{96,112},{1,17},{17... | collective-permute-start | bytes 221192 | tf_op jit(solution)/shard_map/ppermute | solution.py:590
  83.8 18.0 %copy-start.1 = (bf16[512,256]{1,0:T(8,128)(2,1)S(1)}, bf16[512,256]{1,0:T(8,128)(2,1)}, u32[]{:S(2)}) copy-start(bf16[512,256]{1,0:T(8,128)(2,1)} %up_ref.1) | copy-start | bytes 786436
  91.8 6.4 %collective-permute-start.5 = (bf16[66,256]{1,0:T(8,128)(2,1)S(1)}, bf16[66,256]{1,0:T(8,128)(2,1)S(1)}, u32[]{:S(2)}, u32[]{:S(2)}) collective-permute-start(bf16[66,256]{1,0:T(8,128)(2,1)S(1)} %pad_maximum_fusion), channel_id=1, source_target_pairs={{0,16},{16,32},{32,48},{48,64},{64,80},{80,96},{96,112},{1,17},{17... | collective-permute-start | bytes 101384 | tf_op jit(solution)/shard_map/ppermute | solution.py:590
  96.3 5.3 %collective-permute-start.6 = (bf16[66,256]{1,0:T(8,128)(2,1)S(1)}, bf16[66,256]{1,0:T(8,128)(2,1)S(1)}, u32[]{:S(2)}, u32[]{:S(2)}) collective-permute-start(bf16[66,256]{1,0:T(8,128)(2,1)S(1)} %pad_maximum_fusion.1), channel_id=1, source_target_pairs={{16,0},{32,16},{48,32},{64,48},{80,64},{96,80},{112,96},{17,1},{33... | collective-permute-start | bytes 101384 | tf_op jit(solution)/shard_map/ppermute | solution.py:590
